TPU v7x, 32 devices: a whole 2x2x4 slice. The times are simulated.
32 devices in a mesh: cells: 8 (over z, x), chan: 4 (over y, core).
Axes of the slice: x: 2, y: 2, z: 4, core: 2. Of those that a mesh axis runs over, the one named last changes fastest.
Arguments:
- charges: bfloat16 [128, 8192], P('chan', 'cells'), may hold values from -6 to 6
- basis: float32 [25, 8192], P(None, 'cells'), may hold values from -1.5 to 1.5
- atom_leaf: int32 [8192], P('cells'), may hold values from 0 to 1023, as said below
- leaf_lists: int32 [64, 1024], P(None, 'cells'), may hold values from -1 to 1023, as said below
- coarse_lists: int32 [64, 128], P(None, 'cells'), may hold values from -1 to 127, as said below
- up_ops: bfloat16 [8, 25, 25], replicated, may hold values from -0.4375 to 0.4375
- down_ops: bfloat16 [8, 25, 25], replicated, may hold values from -1.25 to 1.25
- leaf_ops: bfloat16 [25, 25, 64], replicated, may hold values from -0.15625 to 0.15625
- coarse_ops: bfloat16 [25, 25, 64], replicated, may hold values from -0.15625 to 0.15625
- mix: bfloat16 [128, 128], replicated, may hold values from -0.5 to 0.5
- cotangent: bfloat16 [128, 8192], P('chan', 'cells'), may hold values from -0.016479492 to 0.016479492
Outputs:
- refined: bfloat16 [128, 8192], P('chan', 'cells')
- grad_leaf_ops: float32 [25, 25, 64], replicated
- grad_coarse_ops: float32 [25, 25, 64], replicated
Inputs may be any that keep to these rules, and one draw needn't show every extreme that they name: `atom_leaf`: an atom's leaf is one of the 128 consecutive leaves whose block along cells holds that atom. `leaf_lists`: entry [s, t] is -1 for an empty slot, else a leaf within 64 leaves of the block of 128 leaves that holds t. `coarse_lists`: entry [s, p] is -1 for an empty slot, else a parent cell within 8 cells of the block of 16 parent cells that holds p.
All inputs are finite; a program needn't handle non-finite values.
Results may differ from a plain program's by a relative error of at most 0.014.
Values may be sent and summed in bfloat16 or wider, within the bound.
No kernel may reach another device: no remote copies, remote signals or barrier semaphores. Data moves between devices by JAX's collectives and lax.ppermute only.
A program may use at most 128 MiB of HBM per device.

v0:
```python
import jax
import jax.numpy as jnp
from jax import lax
from jax.sharding import PartitionSpec as P

SLOT_BLOCK = 16


def extended(block, sides, width):
    for axis, dim in sides:
        count = lax.axis_size(axis)
        forward = [(i, i + 1) for i in range(count - 1)]
        backward = [(target, source) for source, target in forward]
        low = lax.ppermute(
            lax.slice_in_dim(block, block.shape[dim] - width, None, axis=dim), axis, forward
        )
        high = lax.ppermute(lax.slice_in_dim(block, 0, width, axis=dim), axis, backward)
        block = jnp.concatenate([low, block, high], axis=dim)
    return block


def spread(weights, values, local_leaf, leaf_dev):
    kcount, atoms = weights.shape
    chan_part = values.shape[0]
    width = min(1024, atoms)

    def spread_accumulate(counter, running):
        member = (local_leaf[:, None] == jnp.arange(leaf_dev, dtype=jnp.int32)[None, :]).astype(
            jnp.bfloat16
        )
        scaled = (weights[:, None, :] * values[None].astype(jnp.float32)).astype(jnp.bfloat16)
        return running + jnp.dot(
            scaled.reshape(kcount * chan_part, width), member, preferred_element_type=jnp.float32
        )

    start_value = jnp.zeros((kcount * chan_part, leaf_dev), jnp.float32)
    result = lax.fori_loop(0, atoms // width, spread_accumulate, start_value)
    return result.reshape(kcount, chan_part, leaf_dev)


def collect(weights, fields, local_leaf):
    kcount, chan_part, leaf_dev = fields.shape
    atoms = weights.shape[1]
    width = min(1024, atoms)
    flat_fields = fields.reshape(kcount * chan_part, leaf_dev)

    def collect_accumulate(counter, running):
        member = (jnp.arange(leaf_dev, dtype=jnp.int32)[:, None] == local_leaf[None, :]).astype(
            jnp.bfloat16
        )
        per_atom = jnp.dot(flat_fields, member, preferred_element_type=jnp.float32).reshape(
            kcount, chan_part, width
        )
        summed = jnp.sum(weights[:, None, :] * per_atom, axis=0)
        return summed

    start_value = jnp.zeros((chan_part, atoms), jnp.float32)
    return lax.fori_loop(0, atoms // width, collect_accumulate, start_value)


def pick(source, group_list, first_cell):
    valid = group_list >= 0
    position = jnp.where(valid, group_list - first_cell, 0)
    picked = jnp.take(source, position, axis=2)
    return picked * valid.astype(jnp.bfloat16)[None, None]


def translate(source, lists, first_cell, ops):
    kcount, chan_part, _ = source.shape
    slot_count, targets = lists.shape
    groups = slot_count // SLOT_BLOCK
    list_groups = lists.reshape(groups, SLOT_BLOCK, targets)
    op_groups = jnp.transpose(ops.reshape(kcount, kcount, groups, SLOT_BLOCK), (2, 3, 0, 1))

    def translate_advance(running, pieces):
        group_list, group_ops = pieces
        picked = pick(source, group_list, first_cell)
        return (
            running
            + jnp.einsum("okj,jcot->kct", group_ops, picked, preferred_element_type=jnp.float32),
            None,
        )

    start_value = jnp.zeros((kcount, chan_part, targets), jnp.float32)
    result, _ = lax.scan(translate_advance, start_value, (list_groups, op_groups))
    return result


def slot_gradients(source, lists, first_cell, fields):
    kcount = source.shape[0]
    slot_count, targets = lists.shape
    groups = slot_count // SLOT_BLOCK
    list_groups = lists.reshape(groups, SLOT_BLOCK, targets)

    def slot_advance(carried, group_list):
        picked = pick(source, group_list, first_cell)
        return (
            carried,
            jnp.einsum("kct,jcot->kjo", fields, picked, preferred_element_type=jnp.float32),
        )

    _, stacked = lax.scan(slot_advance, jnp.zeros((), jnp.float32), list_groups)
    return jnp.transpose(stacked, (1, 2, 0, 3)).reshape(kcount, kcount, slot_count)


def local(
    charges,
    basis,
    atom_leaf,
    leaf_lists,
    coarse_lists,
    up_ops,
    down_ops,
    leaf_ops,
    coarse_ops,
    mix,
    cotangent,
):
    chan_part = charges.shape[0]
    kcount = basis.shape[0]
    leaf_dev = leaf_lists.shape[1]
    coarse_dev = coarse_lists.shape[1]
    cells_pos = lax.axis_index("cells")
    chan_pos = lax.axis_index("chan")
    local_leaf = atom_leaf - cells_pos * leaf_dev
    moments = spread(basis, charges, local_leaf, leaf_dev).astype(jnp.bfloat16)
    grouped = moments.reshape(kcount, chan_part, coarse_dev, 8)
    coarse = jnp.einsum(
        "okj,jcpo->kcp", up_ops, grouped, preferred_element_type=jnp.float32
    ).astype(jnp.bfloat16)
    leaf_source = extended(moments, (("cells", 2),), leaf_dev // 2)
    leaf_first = cells_pos * leaf_dev - leaf_dev // 2
    coarse_source = extended(coarse, (("cells", 2),), coarse_dev // 2)
    coarse_first = cells_pos * coarse_dev - coarse_dev // 2
    near_field = translate(leaf_source, leaf_lists, leaf_first, leaf_ops)
    far_field = translate(coarse_source, coarse_lists, coarse_first, coarse_ops).astype(
        jnp.bfloat16
    )
    child = jnp.einsum("okj,jcp->kcpo", down_ops, far_field, preferred_element_type=jnp.float32)
    expansion = (near_field + child.reshape(kcount, chan_part, leaf_dev)).astype(jnp.bfloat16)
    potential = collect(basis, expansion, local_leaf).astype(jnp.bfloat16)
    rows_mine = lax.dynamic_slice_in_dim(mix, chan_pos * chan_part, chan_part, 0)
    cols_mine = lax.dynamic_slice_in_dim(mix, chan_pos * chan_part, chan_part, 1)
    mixed = lax.dot_general(
        cols_mine,
        lax.all_gather(potential, "chan", axis=0, tiled=True),
        (((0,), (0,)), ((), ())),
        preferred_element_type=jnp.float32,
    )
    back_sum = jnp.dot(
        rows_mine,
        lax.all_gather(cotangent, "chan", axis=0, tiled=True),
        preferred_element_type=jnp.float32,
    )
    refined = (charges.astype(jnp.float32) + mixed).astype(jnp.bfloat16)
    back_potential = back_sum.astype(jnp.bfloat16)
    back_expansion = spread(basis, back_potential, local_leaf, leaf_dev).astype(jnp.bfloat16)
    back_grouped = back_expansion.reshape(kcount, chan_part, coarse_dev, 8)
    back_far = jnp.einsum(
        "okj,kcpo->jcp", down_ops, back_grouped, preferred_element_type=jnp.float32
    ).astype(jnp.bfloat16)
    grad_leaf = slot_gradients(leaf_source, leaf_lists, leaf_first, back_expansion)
    grad_coarse = slot_gradients(coarse_source, coarse_lists, coarse_first, back_far)
    grad_leaf, grad_coarse = lax.psum((grad_leaf, grad_coarse), ("cells", "chan"))
    return (refined, grad_leaf, grad_coarse)


def solution(mesh):
    placed = (
        P("chan", "cells"),
        P(None, "cells"),
        P("cells"),
        P(None, "cells"),
        P(None, "cells"),
        P(),
        P(),
        P(),
        P(),
        P(),
        P("chan", "cells"),
    )
    return jax.shard_map(
        local, mesh=mesh, in_specs=placed, out_specs=(P("chan", "cells"), P(), P()), check_vma=False
    )
```

profile of v0, /device:TPU:0, one launch (start us, length us, event | category | flops | bytes accessed | tf_op | source)
XLA Modules:
  0.0 580.8 jit_solution(18252151324319015125)
XLA Ops:
  12.5 6.1 %collective-permute-start = (bf16[25,32,64]{2,1,0:T(8,128)(2,1)}, bf16[25,32,64]{2,1,0:T(8,128)(2,1)}, u32[]{:S(2)}, u32[]{:S(2)}) collective-permute-start(bf16[25,32,64]{2,1,0:T(8,128)(2,1)} %get-tuple-element.330), channel_id=1, source_target_pairs={{0,4},{4,8},{8,12},{12,16},{16,20},{20,24},{24,28},{1,5},{5,9},{9,... | collective-permute-start | bytes 307208 | tf_op jit(solution)/shard_map/ppermute | solution.py:14
  22.1 4.8 collective-permute-start.2
  26.9 6.1 %all_gather.7 = bf16[128,1024]{1,0:T(8,128)(2,1)S(1)} all-gather(bf16[32,1024]{1,0:T(8,128)(2,1)S(1)} %copy-done.9), channel_id=1, replica_groups=mesh['cells'=8,'chan'=4] {'chan'}, dimensions={0}, use_global_device_ids=true | all-gather | bytes 327680 | tf_op jit(solution)/shard_map/all_gather | solution.py:152
  40.7 13.1 %while.57 = (s32[]{:T(128)}, f32[25,32,16]{1,0,2:T(8,128)S(1)}, bf16[4,16,25,25]{3,2,1,0:T(8,128)(2,1)S(1)}, s32[4,16,16]{2,1,0:T(8,128)S(1)}, s32[]{:T(128)}, /...) while((s32[]{:T(128)}, f32[25,32,16]{1,0,2:T(8,128)S(1)}, ...), condition=%wide.region_3.6_spmd.clone, body=%wide.region_2.5_spmd.clone.sunk | while | flops 10678787 | bytes 4553847 | solution.py:85
  53.9 17.5 %while.15 = (s32[]{:T(128)}, f32[4,25,25,16]{1,2,3,0:T(8,128)}, s32[4,16,16]{2,1,0:T(8,128)S(1)}, s32[]{:T(128)}, bf16[25,32,32]{1,0,2:T(8,128)(2,1)S(1)}, /*index=5*/bf16[25,32,16]{1,0,2:T(8,128)(2,1)}, s32[]{:T(128)}) while((s32[]{:T(128)}, f32[4,25,25,16]{1,2,3,0:T(8,128)}, s32[4,16,16]{2,1,0:T(8,128)S(1)}, s32[]{:T(128)}, ...), condition=%wide.region_9.12_spmd, body=%wide.region_8.11_spmd.sunk | while | flops 10653186 | bytes 3270785 | solution.py:102
  80.4 193.7 %while.56 = (s32[]{:T(128)}, f32[25,32,128]{2,0,1:T(8,128)}, bf16[4,16,25,25]{3,2,1,0:T(8,128)(2,1)}, s32[4,16,128]{2,1,0:T(8,128)S(1)}, s32[]{:T(128)}, /*index...) while((s32[]{:T(128)}, f32[25,32,128]{2,0,1:T(8,128)}, bf16[4,16,25,25]{3,2,1,0:T(8,128)(2,1)}, ...), condition=%wide.region_1.3_spmd.clone, body=%wide.region_0.2_spmd.clone.sunk | while | flops 90349568 | bytes 18425984 | solution.py:85
  80.5 19.3 %gather_fusion.2 = bf16[2048,25,32]{2,1,0:T(8,128)(2,1)} fusion(bf16[25,32,256]{1,0,2:T(8,128)(2,1)S(1)} %get-tuple-element.527, s32[2048]{0:T(1024)S(1)} %bitcast_clamp_fusion.5), kind=kCustom, calls=%fused_computation.clone.clone.1 | custom fusion | bytes 6561792 | tf_op jit(solution)/shard_map/while/body/eval_jaxpr/jit(_take)/gather | solution.py:64
  99.8 24.5 %copy.113 = bf16[16,128,25,32]{1,2,0,3:T(8,128)(2,1)} copy(bf16[16,128,25,32]{3,2,1,0:T(8,128)(2,1)} %bitcast.208) | data formatting | bytes 6553600 | tf_op jit(solution)/shard_map/while/body/eval_jaxpr/jit(_take)/gather | solution.py:64
  124.3 4.5 fusion.98
  128.8 19.3 %gather_fusion.2 = bf16[2048,25,32]{2,1,0:T(8,128)(2,1)} fusion(bf16[25,32,256]{1,0,2:T(8,128)(2,1)S(1)} %get-tuple-element.527, s32[2048]{0:T(1024)S(1)} %bitcast_clamp_fusion.5), kind=kCustom, calls=%fused_computation.clone.clone.1 | custom fusion | bytes 6561792 | tf_op jit(solution)/shard_map/while/body/eval_jaxpr/jit(_take)/gather | solution.py:64
  148.1 24.5 %copy.113 = bf16[16,128,25,32]{1,2,0,3:T(8,128)(2,1)} copy(bf16[16,128,25,32]{3,2,1,0:T(8,128)(2,1)} %bitcast.208) | data formatting | bytes 6553600 | tf_op jit(solution)/shard_map/while/body/eval_jaxpr/jit(_take)/gather | solution.py:64
  172.6 4.6 fusion.98
  177.2 19.3 %gather_fusion.2 = bf16[2048,25,32]{2,1,0:T(8,128)(2,1)} fusion(bf16[25,32,256]{1,0,2:T(8,128)(2,1)S(1)} %get-tuple-element.527, s32[2048]{0:T(1024)S(1)} %bitcast_clamp_fusion.5), kind=kCustom, calls=%fused_computation.clone.clone.1 | custom fusion | bytes 6561792 | tf_op jit(solution)/shard_map/while/body/eval_jaxpr/jit(_take)/gather | solution.py:64
  196.5 24.5 %copy.113 = bf16[16,128,25,32]{1,2,0,3:T(8,128)(2,1)} copy(bf16[16,128,25,32]{3,2,1,0:T(8,128)(2,1)} %bitcast.208) | data formatting | bytes 6553600 | tf_op jit(solution)/shard_map/while/body/eval_jaxpr/jit(_take)/gather | solution.py:64
  221.1 4.6 fusion.98
  225.7 19.3 %gather_fusion.2 = bf16[2048,25,32]{2,1,0:T(8,128)(2,1)} fusion(bf16[25,32,256]{1,0,2:T(8,128)(2,1)S(1)} %get-tuple-element.527, s32[2048]{0:T(1024)S(1)} %bitcast_clamp_fusion.5), kind=kCustom, calls=%fused_computation.clone.clone.1 | custom fusion | bytes 6561792 | tf_op jit(solution)/shard_map/while/body/eval_jaxpr/jit(_take)/gather | solution.py:64
  245.0 24.5 %copy.113 = bf16[16,128,25,32]{1,2,0,3:T(8,128)(2,1)} copy(bf16[16,128,25,32]{3,2,1,0:T(8,128)(2,1)} %bitcast.208) | data formatting | bytes 6553600 | tf_op jit(solution)/shard_map/while/body/eval_jaxpr/jit(_take)/gather | solution.py:64
  269.5 4.6 fusion.98
  275.9 5.9 %all_gather.6 = bf16[128,1024]{1,0:T(8,128)(2,1)S(1)} all-gather(bf16[32,1024]{1,0:T(8,128)(2,1)S(1)} %multiply_reduce_fusion), channel_id=1, replica_groups=mesh['cells'=8,'chan'=4] {'chan'}, dimensions={0}, use_global_device_ids=true | all-gather | bytes 327680 | tf_op jit(solution)/shard_map/all_gather | solution.py:146
  281.8 151.2 %while.14 = (s32[]{:T(128)}, f32[4,25,25,16]{1,3,2,0:T(8,128)}, s32[4,16,128]{2,1,0:T(8,128)S(1)}, s32[]{:T(128)}, bf16[25,32,256]{1,0,2:T(8,128)(2,1)S(1)}, /*index=5*/bf16[25,32,128]{2,0,1:T(8,128)(2,1)S(1)}, s32[]{:T(128)}) while((s32[]{:T(128)}, f32[4,25,25,16]{1,3,2,0:T(8,128)}, s32[4,16,128]{2,1,0:T(8,128)S(1)}, s32[]{:T(128)}, ...), condition=%wide.region_6.9_spmd, body=%wide.region_5.8_spmd.sunk | while | flops 85229568 | bytes 16853100 | solution.py:102
  281.8 19.3 %gather_fusion = bf16[2048,25,32]{2,1,0:T(8,128)(2,1)} fusion(bf16[25,32,256]{1,0,2:T(8,128)(2,1)S(1)} %get-tuple-element.572, s32[2048]{0:T(1024)S(1)} %bitcast_clamp_fusion.4), kind=kCustom, calls=%fused_computation.2.clone.clone.1 | custom fusion | bytes 6561792 | tf_op jit(solution)/shard_map/while/body/eval_jaxpr/jit(_take)/gather | solution.py:64
  301.1 14.9 %copy.110 = bf16[16,128,25,32]{1,0,3,2:T(8,128)(2,1)} copy(bf16[16,128,25,32]{3,2,1,0:T(8,128)(2,1)} %bitcast.209) | data formatting | bytes 6553600 | tf_op jit(solution)/shard_map/while/body/eval_jaxpr/jit(_take)/gather | solution.py:64
  315.9 3.6 fusion.93
  319.6 19.3 %gather_fusion = bf16[2048,25,32]{2,1,0:T(8,128)(2,1)} fusion(bf16[25,32,256]{1,0,2:T(8,128)(2,1)S(1)} %get-tuple-element.572, s32[2048]{0:T(1024)S(1)} %bitcast_clamp_fusion.4), kind=kCustom, calls=%fused_computation.2.clone.clone.1 | custom fusion | bytes 6561792 | tf_op jit(solution)/shard_map/while/body/eval_jaxpr/jit(_take)/gather | solution.py:64
  338.9 14.9 %copy.110 = bf16[16,128,25,32]{1,0,3,2:T(8,128)(2,1)} copy(bf16[16,128,25,32]{3,2,1,0:T(8,128)(2,1)} %bitcast.209) | data formatting | bytes 6553600 | tf_op jit(solution)/shard_map/while/body/eval_jaxpr/jit(_take)/gather | solution.py:64
  353.8 3.6 fusion.93
  357.4 19.3 %gather_fusion = bf16[2048,25,32]{2,1,0:T(8,128)(2,1)} fusion(bf16[25,32,256]{1,0,2:T(8,128)(2,1)S(1)} %get-tuple-element.572, s32[2048]{0:T(1024)S(1)} %bitcast_clamp_fusion.4), kind=kCustom, calls=%fused_computation.2.clone.clone.1 | custom fusion | bytes 6561792 | tf_op jit(solution)/shard_map/while/body/eval_jaxpr/jit(_take)/gather | solution.py:64
  376.7 14.9 %copy.110 = bf16[16,128,25,32]{1,0,3,2:T(8,128)(2,1)} copy(bf16[16,128,25,32]{3,2,1,0:T(8,128)(2,1)} %bitcast.209) | data formatting | bytes 6553600 | tf_op jit(solution)/shard_map/while/body/eval_jaxpr/jit(_take)/gather | solution.py:64
  395.2 19.3 %gather_fusion = bf16[2048,25,32]{2,1,0:T(8,128)(2,1)} fusion(bf16[25,32,256]{1,0,2:T(8,128)(2,1)S(1)} %get-tuple-element.572, s32[2048]{0:T(1024)S(1)} %bitcast_clamp_fusion.4), kind=kCustom, calls=%fused_computation.2.clone.clone.1 | custom fusion | bytes 6561792 | tf_op jit(solution)/shard_map/while/body/eval_jaxpr/jit(_take)/gather | solution.py:64
  414.5 14.9 %copy.110 = bf16[16,128,25,32]{1,0,3,2:T(8,128)(2,1)} copy(bf16[16,128,25,32]{3,2,1,0:T(8,128)(2,1)} %bitcast.209) | data formatting | bytes 6553600 | tf_op jit(solution)/shard_map/while/body/eval_jaxpr/jit(_take)/gather | solution.py:64
  429.3 3.6 fusion.93
  436.8 132.7 %all-reduce.3.cloned.1.call-done = (f32[25,25,64]{1,2,0:T(8,128)}, f32[25,25,64]{1,2,0:T(8,128)}) async-done(((f32[25,25,64]{1,2,0:T(8,128)}, f32[25,25,64]{1,2,0:T(8,128)}), (f32[25,25,64]{1,2,0:T(8,128)}, f32[25,25,64]{1,2,0:T(8,128)})) %all-reduce.3.cloned.1.call-update) | async-done | bytes 320016 | tf_op jit(solution)/shard_map/psum | solution.py:164
  (162 shorter events, 69.3 us)
Async XLA Ops:
  7.2 25.8 %copy-start = (bf16[128,128]{1,0:T(8,128)(2,1)S(1)}, bf16[128,128]{1,0:T(8,128)(2,1)}, u32[]{:S(2)}) copy-start(bf16[128,128]{1,0:T(8,128)(2,1)} %param.32) | copy-start | bytes 98308
  7.2 562.3 %all-reduce.3.cloned.1.call-start = ((), (), s32[]{:S(2)}) async-start(), calls=%async_computation | async-start | bytes 3276800 | tf_op jit(solution)/shard_map/psum | solution.py:164
  8.1 12.3 %copy-start.7 = (bf16[8,25,25]{2,0,1:T(8,128)(2,1)S(1)}, bf16[8,25,25]{2,0,1:T(8,128)(2,1)}, u32[]{:S(2)}) copy-start(bf16[8,25,25]{2,0,1:T(8,128)(2,1)} %param.28) | copy-start | bytes 30004
  10.4 16.5 %copy-start.9 = (bf16[32,1024]{1,0:T(8,128)(2,1)S(1)}, bf16[32,1024]{1,0:T(8,128)(2,1)}, u32[]{:S(2)}) copy-start(bf16[32,1024]{1,0:T(8,128)(2,1)} %param.33) | copy-start | bytes 196612
  10.4 22.7 %copy-start.11 = (f32[25,1024]{1,0:T(8,128)S(1)}, f32[25,1024]{1,0:T(8,128)}, u32[]{:S(2)}) copy-start(f32[25,1024]{1,0:T(8,128)} %param.24) | copy-start | bytes 307204
  11.2 64.9 %collective-permute-start.1 = (bf16[25,32,64]{2,1,0:T(8,128)(2,1)}, bf16[25,32,64]{2,1,0:T(8,128)(2,1)}, u32[]{:S(2)}, u32[]{:S(2)}) collective-permute-start(bf16[25,32,64]{2,1,0:T(8,128)(2,1)} %get-tuple-element.331), channel_id=1, source_target_pairs={{4,0},{8,4},{12,8},{16,12},{20,16},{24,20},{28,24},{5,1},{9,5},{13... | collective-permute-start | bytes 307208 | tf_op jit(solution)/shard_map/ppermute | solution.py:17
  12.5 63.6 %collective-permute-start = (bf16[25,32,64]{2,1,0:T(8,128)(2,1)}, bf16[25,32,64]{2,1,0:T(8,128)(2,1)}, u32[]{:S(2)}, u32[]{:S(2)}) collective-permute-start(bf16[25,32,64]{2,1,0:T(8,128)(2,1)} %get-tuple-element.330), channel_id=1, source_target_pairs={{0,4},{4,8},{8,12},{12,16},{16,20},{20,24},{24,28},{1,5},{5,9},{9,... | collective-permute-start | bytes 307208 | tf_op jit(solution)/shard_map/ppermute | solution.py:14
  20.8 14.8 %copy-start.8 = (bf16[8,25,25]{2,0,1:T(8,128)(2,1)S(1)}, bf16[8,25,25]{2,0,1:T(8,128)(2,1)}, u32[]{:S(2)}) copy-start(bf16[8,25,25]{2,0,1:T(8,128)(2,1)} %param.29) | copy-start | bytes 30004
  20.8 19.5 %collective-permute-start.3 = (bf16[25,32,8]{0,1,2:T(8,128)(2,1)S(1)}, bf16[25,32,8]{0,1,2:T(8,128)(2,1)S(1)}, u32[]{:S(2)}, u32[]{:S(2)}) collective-permute-start(bf16[25,32,8]{0,1,2:T(8,128)(2,1)S(1)} %get-tuple-element.333), channel_id=1, source_target_pairs={{4,0},{8,4},{12,8},{16,12},{20,16},{24,20},{28,24},{5,1},{9,5},{13... | collective-permute-start | bytes 38408 | tf_op jit(solution)/shard_map/ppermute | solution.py:17
  22.1 18.2 %collective-permute-start.2 = (bf16[25,32,8]{0,1,2:T(8,128)(2,1)S(1)}, bf16[25,32,8]{0,1,2:T(8,128)(2,1)S(1)}, u32[]{:S(2)}, u32[]{:S(2)}) collective-permute-start(bf16[25,32,8]{0,1,2:T(8,128)(2,1)S(1)} %get-tuple-element.332), channel_id=1, source_target_pairs={{0,4},{4,8},{8,12},{12,16},{16,20},{20,24},{24,28},{1,5},{5,9},{9,... | collective-permute-start | bytes 38408 | tf_op jit(solution)/shard_map/ppermute | solution.py:14
  33.2 3.6 copy-start.4
  33.9 4.6 copy-start.5
  33.9 5.5 copy-start.10
  55.7 0.9 copy-start.6
  60.0 0.9 copy-start.6
  64.4 0.9 copy-start.6
  68.8 0.9 copy-start.6
  76.1 4.3 copy-start.1
  80.4 194.9 %copy-start.12 = (f32[25,1024]{1,0:T(8,128)S(1)}, f32[25,1024]{1,0:T(8,128)}, u32[]{:S(2)}) copy-start(f32[25,1024]{1,0:T(8,128)} %param.24) | copy-start | bytes 307204
  274.1 7.7 %copy-start.2 = (bf16[25,32,128]{2,0,1:T(8,128)(2,1)S(1)}, bf16[25,32,128]{2,0,1:T(8,128)(2,1)}, u32[]{:S(2)}) copy-start(bf16[25,32,128]{2,0,1:T(8,128)(2,1)} %copy.53) | copy-start | bytes 614404
  432.9 2.9 copy-start.3
Sparse Core Ops, SparseCore 0:
  436.0 133.4 all-reduce.2
where the time goes:
time: 583 us; the launch traced here: 581 us
  local copies, waits for them, and re-layouts  352 us (60%)
  waiting for transfers between devices  133 us (23%)
  matrix products  49.3 us (8%)
  between operations  14.3 us (2%)
  starting transfers between devices  13.5 us (2%)
  blocking collectives  11.9 us (2%)
  other arithmetic  6.58 us (1%)
    gather x32, local copies, waits for them, and re-layouts, pick(): picked = jnp.take(source, position, axis=2)  325 us
    psum x1, waiting for transfers between devices, local(): lax.psum((grad_leaf, grad_coarse), ('cells', 'chan'))  133 us
    dot_general x8, matrix products, translate_advance(): jnp.einsum('okj,jcot->kct', group_ops, picked, preferred_element_type=jnp...  22.9 us
    dot_general x8, matrix products, slot_advance(): jnp.einsum('kct,jcot->kjo', fields, picked, preferred_element_type=jnp.fl...  21.2 us
  transfers between devices with their start and end apart: 5, of which 1 were waited for; matrix products, arithmetic and copies ran while one was open for 7% of the time, Pallas kernels for 0%

commit v1 on v0

v1 whole, which is shorter than its diff:
```python
import jax
import jax.numpy as jnp
from jax import lax
from jax.experimental import pallas as pl
from jax.experimental.pallas import tpu as pltpu
from jax.sharding import PartitionSpec as P

KP = 32
GROUP = 8
OCT = 8
VMEM_BYTES = 48 * 1024 * 1024
f32 = jnp.float32
bf16 = jnp.bfloat16


def nt(a, b):
    return lax.dot_general(a, b, (((1,), (1,)), ((), ())), preferred_element_type=f32)


def nn(a, b):
    return jnp.dot(a, b, preferred_element_type=f32)


def member(leaf_row, leaf_dev):
    shape = (leaf_dev, leaf_row.shape[1])
    return jnp.where(lax.broadcasted_iota(jnp.int32, shape, 0) == leaf_row, 1.0, 0.0).astype(bf16)


def padded_basis(basis_ref, base):
    base[...] = jnp.zeros_like(base)
    base[0 : basis_ref.shape[0], :] = basis_ref[...]


def spread(base, values, scaled):
    wide = values.astype(f32)
    for c in range(values.shape[0]):
        scaled[c * KP : (c + 1) * KP, :] = (base[...] * wide[c : c + 1, :]).astype(bf16)


def pooling(rows, cols):
    return jnp.where(
        lax.broadcasted_iota(jnp.int32, (rows, cols), 0) // OCT
        == lax.broadcasted_iota(jnp.int32, (rows, cols), 1),
        1.0,
        0.0,
    ).astype(bf16)


def by_octant(stacked):
    octant = lax.broadcasted_iota(jnp.int32, (KP, stacked.shape[1]), 1) % OCT
    result = stacked[0:KP, :]
    for o in range(1, OCT):
        result = jnp.where(octant == o, stacked[o * KP : (o + 1) * KP, :], result)
    return result


def upward(ops, wide_ref, store):
    lanes = OCT * 128
    pool = pooling(lanes, 128)
    for part in range(wide_ref.shape[1] // lanes):
        stacked = nn(ops, wide_ref[:, part * lanes : (part + 1) * lanes])
        store(part, nn(by_octant(stacked).astype(bf16), pool).astype(bf16))


def moments_kernel(charges, basis, leaf, m_out, hi_out, lo_out, base, scaled):
    leaf_dev = m_out.shape[1]
    half = leaf_dev // 2
    padded_basis(basis, base)
    local = leaf[...] - lax.axis_index("cells") * leaf_dev
    spread(base, charges[...], scaled)
    m = nt(scaled[...], member(local, leaf_dev))
    m_out[...] = m.astype(bf16)
    rows = m.shape[0] // 2
    first, second = m[:rows], m[rows:]
    low_lane = lax.broadcasted_iota(jnp.int32, (rows, leaf_dev), 1) < half
    hi_out[...] = jnp.where(low_lane, pltpu.roll(first, half, 1), second).astype(bf16)
    lo_out[...] = jnp.where(low_lane, first, pltpu.roll(second, half, 1)).astype(bf16)


def back_kernel(
    own, core, cross, mix, basis, leaf, m, up, down_t, be_out, bf_out, cc_out, base, scaled, gathered, wide
):
    leaf_dev = m.shape[1]
    part = own.shape[0]
    me = lax.axis_index("chan")
    padded_basis(basis, base)
    gathered[pl.ds(me * part, part), :] = own[...]
    gathered[pl.ds((me ^ 1) * part, part), :] = core[...]
    gathered[pl.ds((me ^ 2) * part, part), :] = cross[0:part, :]
    gathered[pl.ds((me ^ 3) * part, part), :] = cross[part : 2 * part, :]
    potential = nn(mix[pl.ds(me * part, part), :], gathered[...]).astype(bf16)
    local = leaf[...] - lax.axis_index("cells") * leaf_dev
    spread(base, potential, scaled)
    be = nt(scaled[...], member(local, leaf_dev)).astype(bf16)
    for c in range(part):
        be_out[:, c * leaf_dev : (c + 1) * leaf_dev] = be[c * KP : (c + 1) * KP, :]
        wide[:, c * leaf_dev : (c + 1) * leaf_dev] = m[c * KP : (c + 1) * KP, :]

    def store_far(at, value):
        bf_out[:, at * 128 : (at + 1) * 128] = value

    def store_coarse(at, value):
        cc_out[at * KP : (at + 1) * KP, :] = value

    upward(down_t[...], be_out, store_far)
    upward(up[...], wide, store_coarse)


def slot_of(group, at):
    return (at % 4) * 16 + 2 * group + at // 4


def grads_kernel(
    m, low, high, cc, ll, cl, be, bf, up, p_out, pc_out, g_out, src, srcc, idx, idxc, wide, blocks, turned
):
    step = pl.program_id(0)
    cell = lax.axis_index("cells")
    leaf_dev = m.shape[1]
    half = leaf_dev // 2
    window = 2 * leaf_dev
    channels = m.shape[0] // KP
    slots, coarse_dev = cl.shape

    @pl.when(step == 0)
    def prepare():
        src[:, 0:leaf_dev] = m[...]
        rows = low.shape[0]
        a, b = low[...].astype(f32), high[...].astype(f32)
        low_lane = lax.broadcasted_iota(jnp.int32, (rows, leaf_dev), 1) < half
        src[0:rows, leaf_dev:] = jnp.where(low_lane, a, pltpu.roll(b, half, 1)).astype(bf16)
        src[rows:, leaf_dev:] = jnp.where(low_lane, pltpu.roll(a, half, 1), b).astype(bf16)
        for c in range(channels):
            wide[:, c * leaf_dev : (c + 1) * leaf_dev] = src[c * KP : (c + 1) * KP, leaf_dev:]
        srcc[:, 0:128] = cc[...]

        def store_halo(at, value):
            srcc[at * KP : (at + 1) * KP, 128:] = value

        upward(up[...], wide, store_halo)
        rel = ll[...] - cell * leaf_dev
        place = jnp.where(rel < 0, rel + leaf_dev + half, jnp.where(rel < leaf_dev, rel, rel + half))
        idx[...] = jnp.where(ll[...] < 0, -1, place)
        crel = cl[...] - cell * coarse_dev
        side = coarse_dev // 2
        cplace = jnp.where(crel < 0, crel + 128 + side, jnp.where(crel < coarse_dev, crel, crel + 128 - side))
        cplace = jnp.where(cl[...] < 0, -1, cplace).astype(f32).astype(bf16)
        copies = jnp.where(
            lax.broadcasted_iota(jnp.int32, (coarse_dev, 128), 0)
            == lax.broadcasted_iota(jnp.int32, (coarse_dev, 128), 1) % coarse_dev,
            1.0,
            0.0,
        ).astype(bf16)
        spot = nn(cplace, copies).astype(jnp.int32)
        base = lax.broadcasted_iota(jnp.int32, (slots, 128), 1) // coarse_dev * coarse_dev
        idxc[...] = jnp.where(spot < 0, -1, spot + base)

    place_of = lax.broadcasted_iota(jnp.int32, (window, 128), 0)

    def chosen(ref, at):
        row = ref[pl.ds(slot_of(step, at), 1), :]
        return jnp.where(place_of == row, 1.0, 0.0).astype(bf16)

    for pair in range(GROUP // 2):
        at = 2 * pair
        both = jnp.concatenate([chosen(idx, at), chosen(idx, at + 1)], axis=1)
        picked = nn(src[...], both).astype(bf16)
        for i in range(2):
            for c in range(channels):
                p_out[(at + i) * KP : (at + i + 1) * KP, c * 128 : (c + 1) * 128] = picked[
                    c * KP : (c + 1) * KP, i * 128 : (i + 1) * 128
                ]
        both = jnp.concatenate([chosen(idxc, at), chosen(idxc, at + 1)], axis=1)
        picked = nn(srcc[...], both).astype(bf16)
        for i in range(2):
            for c in range(srcc.shape[0] // KP):
                pc_out[(at + i) * KP : (at + i + 1) * KP, c * 128 : (c + 1) * 128] = picked[
                    c * KP : (c + 1) * KP, i * 128 : (i + 1) * 128
                ]
    leaf_part = nt(be[...], p_out[...])
    coarse_part = nt(bf[...], pc_out[...])
    for i in range(2):
        blocks[2 * step + i] = leaf_part[:, i * 128 : (i + 1) * 128]
        blocks[slots // 4 + 2 * step + i] = coarse_part[:, i * 128 : (i + 1) * 128]

    @pl.when(step == slots // GROUP - 1)
    def finish():
        for b in range(slots // 2):
            turned[:, b, :] = blocks[b]
        g_out[...] = turned[...].astype(bf16)


def potential_kernel(p, pc, lops, cops, down, basis, leaf, out, near, far, base, field, total):
    step = pl.program_id(0)
    leaf_dev = p.shape[1] // out.shape[0]

    @pl.when(step == 0)
    def start():
        near[...] = nn(lops[...], p[...])
        far[...] = nn(cops[...], pc[...])

    @pl.when(step > 0)
    def advance():
        near[...] += nn(lops[...], p[...])
        far[...] += nn(cops[...], pc[...])

    @pl.when(step == pl.num_programs(0) - 1)
    def finish():
        padded_basis(basis, base)
        local = leaf[...] - lax.axis_index("cells") * leaf_dev
        inside = member(local, leaf_dev)
        lanes = OCT * 128
        copies = jnp.where(
            lax.broadcasted_iota(jnp.int32, (128, lanes), 1) // OCT
            == lax.broadcasted_iota(jnp.int32, (128, lanes), 0),
            1.0,
            0.0,
        ).astype(bf16)
        for part in range(far.shape[1] // 128):
            parent = nn(far[:, part * 128 : (part + 1) * 128].astype(bf16), copies).astype(bf16)
            child = by_octant(nn(down[...], parent))
            expansion = (near[:, part * lanes : (part + 1) * lanes] + child).astype(bf16)
            for c in range(OCT):
                field[c * KP : (c + 1) * KP, :] = expansion[:, c * leaf_dev : (c + 1) * leaf_dev]
            per_atom = nn(field[...], inside)
            for c in range(OCT):
                at = part * OCT + c
                total[at : at + 1, :] = jnp.sum(
                    base[...] * per_atom[c * KP : (c + 1) * KP, :], axis=0, keepdims=True
                )
        out[...] = total[...].astype(bf16)


def reduce_kernel(parts, out):
    total = parts[0].astype(f32)
    for d in range(1, parts.shape[0]):
        total = total + parts[d].astype(f32)
    turned = total.T
    pieces = []
    for level in range(2):
        for place in range(4):
            pieces.append(turned[place * KP : (place + 1) * KP, level * 16 : (level + 1) * 16])
    laid = jnp.concatenate(pieces, axis=1).astype(bf16)
    for d in range(out.shape[0]):
        out[d] = laid


def unpack_kernel(whole, leaf_out, coarse_out):
    kcount, jcount, slots = leaf_out.shape
    for k in range(kcount):
        row = whole[k].astype(f32)
        leaf_out[k] = row[0:jcount, 0:slots]
        coarse_out[k] = pltpu.roll(row, slots, 1)[0:jcount, 0:slots]


def mixing_kernel(own, core, cross, mix, charges, out, gathered, mixed):
    part = own.shape[0]
    me = lax.axis_index("chan")
    gathered[pl.ds(me * part, part), :] = own[...]
    gathered[pl.ds((me ^ 1) * part, part), :] = core[...]
    gathered[pl.ds((me ^ 2) * part, part), :] = cross[0:part, :]
    gathered[pl.ds((me ^ 3) * part, part), :] = cross[part : 2 * part, :]
    mixed[...] = lax.dot_general(
        mix[...], gathered[...], (((0,), (0,)), ((), ())), preferred_element_type=f32
    )
    out[...] = (charges[...].astype(f32) + mixed[pl.ds(me * part, part), :]).astype(bf16)


def call(kernel, outs, scratch, flops=10**8, moved=10**6, **kw):
    return pl.pallas_call(
        kernel,
        out_shape=outs,
        scratch_shapes=scratch,
        compiler_params=pltpu.CompilerParams(vmem_limit_bytes=VMEM_BYTES),
        cost_estimate=pl.CostEstimate(flops=flops, bytes_accessed=moved, transcendentals=0),
        **kw,
    )


def from_chan(block):
    count = lax.axis_size("chan")
    core = lax.ppermute(block, "chan", [(i, i ^ 1) for i in range(count)])
    cross = lax.ppermute(
        jnp.concatenate([block, core], axis=0), "chan", [(i, i ^ 2) for i in range(count)]
    )
    return core, cross


def slot_ops(ops):
    kcount, _, slots = ops.shape
    laid = jnp.transpose(ops.reshape(kcount, kcount, 4, slots // 4), (0, 3, 2, 1))
    laid = jnp.pad(laid, ((0, KP - kcount), (0, 0), (0, 0), (0, KP - kcount)))
    return laid.reshape(KP, slots * KP)


def octant_ops(ops):
    kcount = ops.shape[1]
    return jnp.pad(ops, ((0, 0), (0, KP - kcount), (0, KP - kcount))).reshape(OCT * KP, KP)


def local(
    charges, basis, atom_leaf, leaf_lists, coarse_lists, up_ops, down_ops, leaf_ops, coarse_ops, mix, cotangent
):
    part, atoms = charges.shape
    kcount = basis.shape[0]
    slots, leaf_dev = leaf_lists.shape
    rows = part * KP
    steps = slots // GROUP
    cells = lax.axis_size("cells")
    devices = cells * lax.axis_size("chan")
    leaf = atom_leaf.reshape(1, atoms)
    shape = jax.ShapeDtypeStruct

    cot_core, cot_cross = from_chan(cotangent)
    m, hi, lo = call(
        moments_kernel,
        (
            shape((rows, leaf_dev), bf16),
            shape((rows // 2, leaf_dev), bf16),
            shape((rows // 2, leaf_dev), bf16),
        ),
        [pltpu.VMEM((KP, atoms), f32), pltpu.VMEM((rows, atoms), bf16)],
    )(charges, basis, leaf)
    forward = [(i, i + 1) for i in range(cells - 1)]
    low = lax.ppermute(hi, "cells", forward)
    high = lax.ppermute(lo, "cells", [(b, a) for a, b in forward])

    up = octant_ops(up_ops)
    down_t = octant_ops(jnp.swapaxes(down_ops, 1, 2))
    down = octant_ops(down_ops)
    be, bf, cc = call(
        back_kernel,
        (
            shape((KP, part * leaf_dev), bf16),
            shape((KP, part * leaf_dev // OCT), bf16),
            shape((128, 128), bf16),
        ),
        [
            pltpu.VMEM((KP, atoms), f32),
            pltpu.VMEM((rows, atoms), bf16),
            pltpu.VMEM((mix.shape[0], atoms), bf16),
            pltpu.VMEM((KP, part * leaf_dev), bf16),
        ],
    )(cotangent, cot_core, cot_cross, mix, basis, leaf, m, up, down_t)

    full = lambda a: pl.BlockSpec(a.shape, lambda g: (0,) * a.ndim)
    wide = part * leaf_dev
    operands = (m, low, high, cc, leaf_lists, coarse_lists, be, bf, up)
    p, pc, grads = call(
        grads_kernel,
        (
            shape((slots * KP, wide), bf16),
            shape((slots * KP, wide // OCT), bf16),
            shape((KP, slots // 2, 128), bf16),
        ),
        [
            pltpu.VMEM((rows, 2 * leaf_dev), bf16),
            pltpu.VMEM((128, 256), bf16),
            pltpu.VMEM((slots, 128), jnp.int32),
            pltpu.VMEM((slots, 128), jnp.int32),
            pltpu.VMEM((KP, wide), bf16),
            pltpu.VMEM((slots // 2, KP, 128), f32),
            pltpu.VMEM((KP, slots // 2, 128), f32),
        ],
        grid=(steps,),
        in_specs=[full(a) for a in operands],
        out_specs=[
            pl.BlockSpec((GROUP * KP, wide), lambda g: (g, 0)),
            pl.BlockSpec((GROUP * KP, wide // OCT), lambda g: (g, 0)),
            pl.BlockSpec((KP, slots // 2, 128), lambda g: (0, 0, 0)),
        ],
    )(*operands)

    axes = ("cells", "chan")
    if devices == KP:
        parts = lax.all_to_all(grads, axes, 0, 0)
        spread_out = call(reduce_kernel, shape((devices, KP, 128), bf16), [])(parts)
        whole = lax.all_to_all(spread_out, axes, 0, 0)
    else:
        laid = grads.reshape(KP, 2, slots // 4, 4, KP)
        laid = jnp.transpose(laid, (0, 4, 1, 3, 2)).reshape(devices, -1, 128)
        parts = lax.all_to_all(laid, axes, 0, 0)
        mine = jnp.sum(parts.astype(f32), axis=0).astype(bf16)
        whole = lax.all_gather(mine, axes).reshape(KP, KP, 128)
    grad_shape = shape((kcount, kcount, slots), f32)
    grad_leaf, grad_coarse = call(unpack_kernel, (grad_shape, grad_shape), [])(whole)

    lops, cops = slot_ops(leaf_ops), slot_ops(coarse_ops)
    small = (down, basis, leaf)
    potential = call(
        potential_kernel,
        shape((part, atoms), bf16),
        [
            pltpu.VMEM((KP, wide), f32),
            pltpu.VMEM((KP, wide // OCT), f32),
            pltpu.VMEM((KP, atoms), f32),
            pltpu.VMEM((OCT * KP, leaf_dev), bf16),
            pltpu.VMEM((part, atoms), f32),
        ],
        grid=(steps,),
        in_specs=[
            pl.BlockSpec((GROUP * KP, wide), lambda g: (g, 0)),
            pl.BlockSpec((GROUP * KP, wide // OCT), lambda g: (g, 0)),
            pl.BlockSpec((KP, GROUP * KP), lambda g: (0, g)),
            pl.BlockSpec((KP, GROUP * KP), lambda g: (0, g)),
        ]
        + [full(a) for a in small],
        out_specs=pl.BlockSpec((part, atoms), lambda g: (0, 0)),
    )(p, pc, lops, cops, *small)
    pot_core, pot_cross = from_chan(potential)
    refined = call(
        mixing_kernel,
        shape((part, atoms), bf16),
        [pltpu.VMEM((mix.shape[0], atoms), bf16), pltpu.VMEM((mix.shape[0], atoms), f32)],
    )(potential, pot_core, pot_cross, mix, charges)
    return refined, grad_leaf, grad_coarse


def solution(mesh):
    placed = (
        P("chan", "cells"),
        P(None, "cells"),
        P("cells"),
        P(None, "cells"),
        P(None, "cells"),
        P(),
        P(),
        P(),
        P(),
        P(),
        P("chan", "cells"),
    )
    return jax.shard_map(
        local, mesh=mesh, in_specs=placed, out_specs=(P("chan", "cells"), P(), P()), check_vma=False
    )
```

time: 583 us -> 93.9 us (0.16)
  local copies, waits for them, and re-layouts: 352 us -> 15.8 us
  waiting for transfers between devices: 133 us -> 6.45 us
  matrix products: 49.3 us -> 0 us
  Pallas kernels: 0 us -> 40.1 us
  between operations: 14.3 us -> 0.83 us
    gather x32 -> x0, local copies, waits for them, and re-layouts: 325 us -> none  [pick(): picked = jnp.take(source, position, axis=2)]
    psum x1 -> x0, waiting for transfers between devices: 133 us -> none  [local(): lax.psum((grad_leaf, grad_coarse), ('cells', 'chan'))]
    dot_general x24 -> x0, matrix products: 49.3 us -> none  [the longest x8 22.9 us: translate_advance(): jnp.einsum('okj,jcot->kct', group_ops, picked, preferred_element_type=jnp...]
    pallas_call x0 -> x7, Pallas kernels: none -> 40.1 us  [the longest x1 20.8 us: local(): call(grads_kernel, (shape((slots * KP, wide), bf16), shape((slots * KP, w...]
    all_to_all x0 -> x1, blocking collectives: none -> 16.4 us  [local(): parts = lax.all_to_all(grads, axes, 0, 0)]
    all_gather x2 -> x0, blocking collectives: 11.9 us -> none  [the longest x1 6.06 us: local(): lax.all_gather(cotangent, 'chan', axis=0, tiled=True)]
    ppermute x4 -> x6, waiting for transfers between devices: 0.01 us -> 6.44 us  [the longest x2 4.09 us: from_chan(): lax.ppermute(jnp.concatenate([block, core], axis=0), 'chan', [(i, i ^ 2)...]
    transpose x2 -> x0, local copies, waits for them, and re-layouts: 5.85 us -> none  [slot_gradients(): jnp.transpose(stacked, (1, 2, 0, 3)).reshape(kcount, kcount, slot_count)]
  transfers between devices with their start and end apart: 5 -> 7, of which waited for: 1 -> 3; matrix products, arithmetic and copies ran while one was open for 7% -> 8% of each run, Pallas kernels for 0% -> 19%
where the time goes in v1:
time: 93.9 us; the launch traced here: 92.9 us
  Pallas kernels  40.1 us (43%)
  blocking collectives  16.4 us (17%)
  local copies, waits for them, and re-layouts  15.8 us (17%)
  starting transfers between devices  12.5 us (13%)
  waiting for transfers between devices  6.45 us (7%)
    pallas_call x1, Pallas kernels, local(): call(grads_kernel, (shape((slots * KP, wide), bf16), shape((slots * KP, w...  20.8 us
    all_to_all x1, blocking collectives, local(): parts = lax.all_to_all(grads, axes, 0, 0)  16.4 us
    unnamed x32, local copies, waits for them, and re-layouts  14.1 us
    pallas_call x1, Pallas kernels, local(): call(potential_kernel, shape((part, atoms), bf16), [pltpu.VMEM((KP, wide)...  11.9 us
    ppermute x2, starting transfers between devices, from_chan(): lax.ppermute(jnp.concatenate([block, core], axis=0), 'chan', [(i, i ^ 2)...  4.47 us
    ppermute x2, waiting for transfers between devices, from_chan(): lax.ppermute(jnp.concatenate([block, core], axis=0), 'chan', [(i, i ^ 2)...  4.09 us
    pallas_call x1, Pallas kernels, local(): call(back_kernel, (shape((KP, part * leaf_dev), bf16), shape((KP, part *...  3.83 us
    ppermute x1, starting transfers between devices, local(): low = lax.ppermute(hi, 'cells', forward)  3.4 us
  transfers between devices with their start and end apart: 7, of which 3 were waited for; matrix products, arithmetic and copies ran while one was open for 8% of the time, Pallas kernels for 19%

profile of v1, /device:TPU:0, one launch (start us, length us, event | category | flops | bytes accessed | tf_op | source)
XLA Modules:
  0.0 92.9 jit_solution(5533527749775934770)
XLA Ops:
  1.2 1.1 %collective-permute-done.2.core = bf16[32,1024]{1,0:T(8,128)(2,1)S(1)} collective-permute-done((bf16[32,1024]{1,0:T(8,128)(2,1)}, bf16[32,1024]{1,0:T(8,128)(2,1)S(1)}, u32[]{:S(2)}, u32[]{:S(2)}) %collective-permute-start.2) | collective-permute-done | bytes 65568 | tf_op jit(solution)/shard_map/ppermute | solution.py:281
  2.3 0.8 pad_maximum_fusion
  3.1 2.9 %collective-permute-start.3 = (bf16[64,1024]{1,0:T(8,128)(2,1)S(1)}, bf16[64,1024]{1,0:T(8,128)(2,1)S(1)}, u32[]{:S(2)}, u32[]{:S(2)}) collective-permute-start(bf16[64,1024]{1,0:T(8,128)(2,1)S(1)} %pad_maximum_fusion), channel_id=1, source_target_pairs={{0,2},{1,3},{2,0},{3,1},{4,6},{5,7},{6,4},{7,5},{8,10},{9,11},{10,... | collective-permute-start | bytes 393224 | tf_op jit(solution)/shard_map/ppermute | solution.py:282
  6.1 0.9 copy-done
  7.0 0.8 copy-done.6
  7.8 0.7 copy-done.9
  8.5 0.8 shard_map.130
  9.3 3.4 %collective-permute-start = (bf16[512,128]{1,0:T(8,128)(2,1)S(1)}, bf16[512,128]{1,0:T(8,128)(2,1)S(1)}, u32[]{:S(2)}, u32[]{:S(2)}) collective-permute-start(bf16[512,128]{1,0:T(8,128)(2,1)S(1)} %get-tuple-element.15), channel_id=1, source_target_pairs={{0,4},{4,8},{8,12},{12,16},{16,20},{20,24},{24,28},{1,5},{5,9},{9,... | collective-permute-start | bytes 393224 | tf_op jit(solution)/shard_map/ppermute | solution.py:324
  12.7 1.3 %collective-permute-start.1 = (bf16[512,128]{1,0:T(8,128)(2,1)S(1)}, bf16[512,128]{1,0:T(8,128)(2,1)S(1)}, u32[]{:S(2)}, u32[]{:S(2)}) collective-permute-start(bf16[512,128]{1,0:T(8,128)(2,1)S(1)} %get-tuple-element.16), channel_id=1, source_target_pairs={{4,0},{8,4},{12,8},{16,12},{20,16},{24,20},{28,24},{5,1},{9,5},{13... | collective-permute-start | bytes 393224 | tf_op jit(solution)/shard_map/ppermute | solution.py:325
  14.0 0.8 copy.28
  14.8 1.0 %copy.29 = bf16[8,25,25]{2,1,0:T(8,128)(2,1)S(1)} copy(bf16[8,25,25]{1,0,2:T(8,128)(2,1)} %bitcast.20) | data formatting | bytes 20000
  15.8 0.8 copy.22.cl
  16.6 0.9 copy-done.1
  17.5 0.8 copy-done.3
  18.4 0.8 copy-done.4
  19.1 0.7 copy-done.10
  19.8 3.8 %shard_map.131 = (bf16[32,4096]{1,0:T(8,128)(2,1)S(1)}, bf16[32,512]{1,0:T(8,128)(2,1)S(1)}, bf16[128,128]{1,0:T(8,128)(2,1)S(1)}) custom-call(bf16[32,1024]{1,0:T(8,128)(2,1)S(1)} %copy-done.3, bf16[32,1024]{1,0:T(8,128)(2,1)S(1)} %collective-permute-done.2.core, bf16[64,1024]{1,0:T(8,128)(2,1)S(1)} %collective-permute-done.3.cross, ...), custom_call_target="tpu_custom_call" | custom-call | flops 100000000 | bytes 1000000 | tf_op jit(solution)/shard_map/pallas_call | solution.py:330
  23.7 0.7 copy-done.8
  24.4 20.8 %shard_map.132 = (bf16[2048,4096]{1,0:T(8,128)(2,1)}, bf16[2048,512]{1,0:T(8,128)(2,1)S(1)}, bf16[32,32,128]{2,1,0:T(8,128)(2,1)S(1)}) custom-call(bf16[1024,128]{1,0:T(8,128)(2,1)S(1)} %get-tuple-element.14.m, bf16[512,128]{1,0:T(8,128)(2,1)S(1)} %collective-permute-done.low, bf16[512,128]{1,0:T(8,128)(2,1)S(1)} %collective-permute-done.1.high, ...), custom_call_target="tpu_custom_call" | custom-call | flops 100000000 | bytes 1000000 | tf_op jit(solution)/shard_map/pallas_call | solution.py:348
  45.3 16.4 %all_to_all.10.parts = bf16[32,32,128]{2,1,0:T(8,128)(2,1)S(1)} all-to-all(bf16[32,32,128]{2,1,0:T(8,128)(2,1)S(1)} %get-tuple-element.22), channel_id=1, replica_groups=mesh['cells'=8,'chan'=4] {'cells','chan'}, dimensions={0} | all-to-all | bytes 524288 | tf_op jit(solution)/shard_map/all_to_all | solution.py:375
  61.7 0.9 %shard_map.135 = bf16[32,32,128]{2,1,0:T(8,128)(2,1)} custom-call(bf16[32,32,128]{2,1,0:T(8,128)(2,1)S(1)} %all_to_all.10.parts), custom_call_target="tpu_custom_call" | custom-call | flops 100000000 | bytes 1000000 | tf_op jit(solution)/shard_map/pallas_call | solution.py:376
  62.6 2.8 %all-to-all-start.1 = ((bf16[32,32,128]{2,1,0:T(8,128)(2,1)}), bf16[32,32,128]{2,1,0:T(8,128)(2,1)S(1)}, u32[]{:S(2)}, u32[]{:S(2)}) async-start(bf16[32,32,128]{2,1,0:T(8,128)(2,1)} %shard_map.135), calls=%async_computation.1 | async-start | bytes 524288 | tf_op jit(solution)/shard_map/all_to_all | solution.py:377
  65.4 0.8 copy.32
  66.2 1.2 %copy.23 = bf16[25,25,64]{1,2,0:T(8,128)(2,1)S(1)} copy(bf16[25,25,64]{2,1,0:T(8,128)(2,1)} %param.18) | data formatting | bytes 160000 | tf_op args[7]
  68.5 1.2 %copy.25 = bf16[25,25,64]{1,2,0:T(8,128)(2,1)S(1)} copy(bf16[25,25,64]{2,1,0:T(8,128)(2,1)} %param.19) | data formatting | bytes 160000 | tf_op args[8]
  70.7 0.9 copy-done.2
  72.3 11.9 %shard_map.133.own = bf16[32,1024]{1,0:T(8,128)(2,1)S(1)} custom-call(bf16[2048,4096]{1,0:T(8,128)(2,1)} %get-tuple-element.20.p, bf16[2048,512]{1,0:T(8,128)(2,1)S(1)} %get-tuple-element.21.pc, bf16[32,2048]{1,0:T(8,128)(2,1)S(1)} %reshape.34.lops, bf16[32,2048]{1,0:T(8,128)(2,1)S(1)} %reshape.36.cops, bf16[256,32]{1,0:T(8,128)(2,1)S(1)} %bitcast.13, ...), custom_call_target="tpu_custom_call" | custom-call | flops 100000000 | bytes 1000000 | tf_op jit(solution)/shard_map/pallas_call | solution.py:389
  84.2 1.2 %collective-permute-done.4.core = bf16[32,1024]{1,0:T(8,128)(2,1)S(1)} collective-permute-done((bf16[32,1024]{1,0:T(8,128)(2,1)S(1)}, bf16[32,1024]{1,0:T(8,128)(2,1)S(1)}, u32[]{:S(2)}, u32[]{:S(2)}) %collective-permute-start.4) | collective-permute-done | bytes 65568 | tf_op jit(solution)/shard_map/ppermute | solution.py:281
  85.5 1.5 %collective-permute-start.5 = (bf16[64,1024]{1,0:T(8,128)(2,1)S(1)}, bf16[64,1024]{1,0:T(8,128)(2,1)S(1)}, u32[]{:S(2)}, u32[]{:S(2)}) collective-permute-start(bf16[64,1024]{1,0:T(8,128)(2,1)S(1)} %pad_maximum_fusion.1), channel_id=1, source_target_pairs={{0,2},{1,3},{2,0},{3,1},{4,6},{5,7},{6,4},{7,5},{8,10},{9,11},{10,... | collective-permute-start | bytes 393224 | tf_op jit(solution)/shard_map/ppermute | solution.py:282
  87.0 4.1 %collective-permute-done.5.cross = bf16[64,1024]{1,0:T(8,128)(2,1)S(1)} collective-permute-done((bf16[64,1024]{1,0:T(8,128)(2,1)S(1)}, bf16[64,1024]{1,0:T(8,128)(2,1)S(1)}, u32[]{:S(2)}, u32[]{:S(2)}) %collective-permute-start.5) | collective-permute-done | bytes 131104 | tf_op jit(solution)/shard_map/ppermute | solution.py:282
  91.1 0.9 shard_map.134
  92.0 0.9 shard_map.136
  (31 shorter events, 3.4 us)
Async XLA Ops:
  0.6 90.5 %copy-start.7 = (bf16[32,1024]{1,0:T(8,128)(2,1)S(1)}, bf16[32,1024]{1,0:T(8,128)(2,1)}, u32[]{:S(2)}) copy-start(bf16[32,1024]{1,0:T(8,128)(2,1)} %charges.3) | copy-start | bytes 196612
  0.6 90.5 %copy-start.5 = (bf16[128,128]{1,0:T(8,128)(2,1)S(1)}, bf16[128,128]{1,0:T(8,128)(2,1)}, u32[]{:S(2)}) copy-start(bf16[128,128]{1,0:T(8,128)(2,1)} %mix.3) | copy-start | bytes 98308
  0.7 1.6 %collective-permute-start.2 = (bf16[32,1024]{1,0:T(8,128)(2,1)}, bf16[32,1024]{1,0:T(8,128)(2,1)S(1)}, u32[]{:S(2)}, u32[]{:S(2)}) collective-permute-start(bf16[32,1024]{1,0:T(8,128)(2,1)} %own.1), channel_id=1, source_target_pairs={{0,1},{1,0},{2,3},{3,2},{4,5},{5,4},{6,7},{7,6},{8,9},{9,8},{10,11... | collective-permute-start | bytes 196616 | tf_op jit(solution)/shard_map/ppermute | solution.py:281
  3.1 13.5 %collective-permute-start.3 = (bf16[64,1024]{1,0:T(8,128)(2,1)S(1)}, bf16[64,1024]{1,0:T(8,128)(2,1)S(1)}, u32[]{:S(2)}, u32[]{:S(2)}) collective-permute-start(bf16[64,1024]{1,0:T(8,128)(2,1)S(1)} %pad_maximum_fusion), channel_id=1, source_target_pairs={{0,2},{1,3},{2,0},{3,1},{4,6},{5,7},{6,4},{7,5},{8,10},{9,11},{10,... | collective-permute-start | bytes 393224 | tf_op jit(solution)/shard_map/ppermute | solution.py:282
  6.1 0.9 copy-start
  7.0 0.8 copy-start.6
  7.8 0.7 copy-start.9
  9.3 14.4 %collective-permute-start = (bf16[512,128]{1,0:T(8,128)(2,1)S(1)}, bf16[512,128]{1,0:T(8,128)(2,1)S(1)}, u32[]{:S(2)}, u32[]{:S(2)}) collective-permute-start(bf16[512,128]{1,0:T(8,128)(2,1)S(1)} %get-tuple-element.15), channel_id=1, source_target_pairs={{0,4},{4,8},{8,12},{12,16},{16,20},{20,24},{24,28},{1,5},{5,9},{9,... | collective-permute-start | bytes 393224 | tf_op jit(solution)/shard_map/ppermute | solution.py:324
  12.7 10.9 %collective-permute-start.1 = (bf16[512,128]{1,0:T(8,128)(2,1)S(1)}, bf16[512,128]{1,0:T(8,128)(2,1)S(1)}, u32[]{:S(2)}, u32[]{:S(2)}) collective-permute-start(bf16[512,128]{1,0:T(8,128)(2,1)S(1)} %get-tuple-element.16), channel_id=1, source_target_pairs={{4,0},{8,4},{12,8},{16,12},{20,16},{24,20},{28,24},{5,1},{9,5},{13... | collective-permute-start | bytes 393224 | tf_op jit(solution)/shard_map/ppermute | solution.py:325
  16.6 0.9 copy-start.1
  17.5 0.8 copy-start.3
  18.4 0.8 copy-start.4
  19.1 0.7 copy-start.10
  23.7 0.8 copy-start.8
  62.6 29.4 %all-to-all-start.1 = ((bf16[32,32,128]{2,1,0:T(8,128)(2,1)}), bf16[32,32,128]{2,1,0:T(8,128)(2,1)S(1)}, u32[]{:S(2)}, u32[]{:S(2)}) async-start(bf16[32,32,128]{2,1,0:T(8,128)(2,1)} %shard_map.135), calls=%async_computation.1 | async-start | bytes 524288 | tf_op jit(solution)/shard_map/all_to_all | solution.py:377
  70.7 0.9 copy-start.2
  71.6 0.7 copy-start.11
  84.2 1.3 %collective-permute-start.4 = (bf16[32,1024]{1,0:T(8,128)(2,1)S(1)}, bf16[32,1024]{1,0:T(8,128)(2,1)S(1)}, u32[]{:S(2)}, u32[]{:S(2)}) collective-permute-start(bf16[32,1024]{1,0:T(8,128)(2,1)S(1)} %shard_map.133.own), channel_id=1, source_target_pairs={{0,1},{1,0},{2,3},{3,2},{4,5},{5,4},{6,7},{7,6},{8,9},{9,8},{10,11... | collective-permute-start | bytes 196616 | tf_op jit(solution)/shard_map/ppermute | solution.py:281
  85.5 5.6 %collective-permute-start.5 = (bf16[64,1024]{1,0:T(8,128)(2,1)S(1)}, bf16[64,1024]{1,0:T(8,128)(2,1)S(1)}, u32[]{:S(2)}, u32[]{:S(2)}) collective-permute-start(bf16[64,1024]{1,0:T(8,128)(2,1)S(1)} %pad_maximum_fusion.1), channel_id=1, source_target_pairs={{0,2},{1,3},{2,0},{3,1},{4,6},{5,7},{6,4},{7,5},{8,10},{9,11},{10,... | collective-permute-start | bytes 393224 | tf_op jit(solution)/shard_map/ppermute | solution.py:282

commit v2 on v1

v2 whole, which is shorter than its diff:
```python
import jax
import jax.numpy as jnp
from jax import lax
from jax.experimental import pallas as pl
from jax.experimental.pallas import tpu as pltpu
from jax.sharding import PartitionSpec as P

KP = 32
GROUP = 8
CHUNK = 128
OCT = 8
MORE = 8
VMEM_BYTES = 24 * 1024 * 1024
f32 = jnp.float32
bf16 = jnp.bfloat16


def nt(a, b):
    return lax.dot_general(a, b, (((1,), (1,)), ((), ())), preferred_element_type=f32)


def nn(a, b):
    return jnp.dot(a, b, preferred_element_type=f32)


def member(leaf_row, leaf_dev):
    shape = (leaf_dev, leaf_row.shape[1])
    return jnp.where(lax.broadcasted_iota(jnp.int32, shape, 0) == leaf_row, 1.0, 0.0).astype(bf16)


def spread(base, values, scaled):
    wide = values.astype(f32)
    for c in range(values.shape[0]):
        scaled[c * KP : (c + 1) * KP, :] = (base[...] * wide[c : c + 1, :]).astype(bf16)


def fetch(pairs, sems):
    copies = [pltpu.make_async_copy(src, dst, sems.at[i]) for i, (src, dst) in enumerate(pairs)]
    for copy in copies:
        copy.start()
    return copies


def pooling(rows, cols):
    return jnp.where(
        lax.broadcasted_iota(jnp.int32, (rows, cols), 0) // OCT
        == lax.broadcasted_iota(jnp.int32, (rows, cols), 1),
        1.0,
        0.0,
    ).astype(bf16)


def by_octant(values):
    octant = lax.broadcasted_iota(jnp.int32, (1, values.shape[1]), 1) % OCT
    return jnp.concatenate(
        [values * jnp.where(octant == o, 1.0, 0.0).astype(values.dtype) for o in range(OCT)], axis=0
    )


def upward(ops, wide_ref, sums):
    lanes = OCT * 128
    for part in range(wide_ref.shape[1] // lanes):
        spaced = by_octant(wide_ref[:, part * lanes : (part + 1) * lanes])
        sums[part * KP : (part + 1) * KP, :] = nn(ops, spaced).astype(bf16)
    return nn(sums[...], pooling(lanes, 128)).astype(bf16)


def moments_kernel(charges_hbm, basis_hbm, leaf_hbm, *rest):
    more = rest[:MORE]
    m_out, first_out, second_out, base_out, inside_out, charges = rest[MORE : MORE + 6]
    held = rest[MORE + 6 : 2 * MORE + 6]
    basis, leaf, scaled, sems = rest[2 * MORE + 6 :]
    leaf_dev = m_out.shape[1]
    half = leaf_dev // 2
    cell = lax.axis_index("cells")
    copies = fetch(
        [(charges_hbm, charges), (basis_hbm, basis), (leaf_hbm, leaf), *zip(more, held)], sems
    )
    kcount = basis.shape[0]
    base_out[...] = jnp.zeros_like(base_out)
    for copy in copies[:3]:
        copy.wait()
    base_out[0:kcount, :] = basis[...]
    inside_out[...] = member(leaf[...] - cell * leaf_dev, leaf_dev)
    spread(base_out, charges[...], scaled)
    m = nt(scaled[...], inside_out[...])
    m_out[...] = m.astype(bf16)
    rows = m.shape[0] // 2
    upper, lower = m[:rows], m[rows:]
    low_lane = lax.broadcasted_iota(jnp.int32, (rows, leaf_dev), 1) < half
    hi = jnp.where(low_lane, pltpu.roll(upper, half, 1), lower).astype(bf16)
    lo = jnp.where(low_lane, upper, pltpu.roll(lower, half, 1)).astype(bf16)
    odd = lax.rem(cell, 2)
    first_out[...] = jnp.where(odd == 1, hi, lo)
    second_out[...] = jnp.where(odd == 1, lo, hi)
    for copy in copies[3:]:
        copy.wait()


def slot_ops(ops, padded, turned, out):
    kcount, jcount, slots = ops.shape
    turned[...] = jnp.zeros_like(turned)
    padded[...] = jnp.zeros_like(padded)
    for k in range(kcount):
        padded[k, 0:jcount, 0:slots] = ops[k].astype(f32)
        turned[k, :, :] = padded[k].T[0:slots]
    blocks = slots // 4
    for b in range(blocks):
        out[:, b * 128 : (b + 1) * 128] = jnp.concatenate(
            [turned[:, place * blocks + b, :] for place in range(4)], axis=1
        ).astype(bf16)


def prepare_kernel(
    up,
    down,
    lops,
    cops,
    ll,
    cl,
    m,
    cc_out,
    up_out,
    down_out,
    back_out,
    lops_out,
    cops_out,
    idx,
    idxc,
    wide,
    stack,
    padded,
    turned,
    sums,
):
    leaf_dev = m.shape[1]
    half = leaf_dev // 2
    kcount = up.shape[0]
    coarse_dev, slots = cl.shape
    cell = lax.axis_index("cells")
    for c in range(m.shape[0] // KP):
        wide[:, c * leaf_dev : (c + 1) * leaf_dev] = m[c * KP : (c + 1) * KP, :]
    stack[...] = jnp.zeros_like(stack)
    for k in range(kcount):
        stack[0, :, k, 0:kcount] = up[k].astype(f32)
        stack[1, :, k, 0:kcount] = down[k].astype(f32)

    def side_by_side(pieces):
        return jnp.concatenate(pieces, axis=1).astype(bf16)

    up_out[...] = side_by_side([stack[0, o, :, 0:KP] for o in range(OCT)])
    down_out[...] = side_by_side([stack[1, o, :, 0:KP] for o in range(OCT)])
    back_out[...] = side_by_side([stack[1, o].T[0:KP, :] for o in range(OCT)])
    cc_out[...] = upward(up_out[...], wide, sums)

    slot_ops(lops, padded, turned, lops_out)
    slot_ops(cops, padded, turned, cops_out)
    rel = ll[...] - cell * leaf_dev
    place = jnp.where(rel < 0, rel + leaf_dev + half, jnp.where(rel < leaf_dev, rel, rel + half))
    idx[...] = jnp.where(ll[...] < 0, -1, place)
    crel = cl[...] - cell * coarse_dev
    side = coarse_dev // 2
    cplace = jnp.where(crel < 0, crel + 128 + side, jnp.where(crel < coarse_dev, crel, crel + 128 - side))
    cplace = jnp.where(cl[...] < 0, -1, cplace).astype(f32).astype(bf16)
    copied = jnp.where(
        lax.broadcasted_iota(jnp.int32, (coarse_dev, 128), 0)
        == lax.broadcasted_iota(jnp.int32, (coarse_dev, 128), 1) % coarse_dev,
        1.0,
        0.0,
    ).astype(bf16)
    spot = lax.dot_general(cplace, copied, (((0,), (0,)), ((), ())), preferred_element_type=f32)
    spot = spot.astype(jnp.int32)
    start = lax.broadcasted_iota(jnp.int32, (slots, 128), 1) // coarse_dev * coarse_dev
    idxc[...] = jnp.where(spot < 0, -1, spot + start)


def back_kernel(own, core, cross, other, mix, base, inside, back_ops, be_out, bf_out, scaled, gathered, sums):
    leaf_dev = inside.shape[0]
    part = own.shape[0]
    me = lax.axis_index("chan")
    gathered[pl.ds(me * part, part), :] = own[...]
    gathered[pl.ds((me ^ 1) * part, part), :] = core[...]
    gathered[pl.ds((me ^ 2) * part, part), :] = cross[...]
    gathered[pl.ds((me ^ 3) * part, part), :] = other[...]
    potential = nn(mix[pl.ds(me * part, part), :], gathered[...]).astype(bf16)
    spread(base, potential, scaled)
    be = nt(scaled[...], inside[...]).astype(bf16)
    for c in range(part):
        be_out[:, c * leaf_dev : (c + 1) * leaf_dev] = be[c * KP : (c + 1) * KP, :]
    far = upward(back_ops[...], be_out, sums)
    for at in range(far.shape[0] // KP):
        bf_out[:, at * 128 : (at + 1) * 128] = far[at * KP : (at + 1) * KP, :]


def slot_of(group, at):
    return (at % 4) * 16 + 2 * group + at // 4


def grads_kernel(
    m,
    first,
    second,
    cc,
    be,
    bf,
    up,
    idx,
    idxc,
    lops,
    cops,
    near,
    far,
    g_out,
    src,
    srcc,
    wide,
    even,
    odd,
    even_c,
    odd_c,
    sums,
    blocks,
    turned,
):
    leaf_dev = m.shape[1]
    half = leaf_dev // 2
    window = 2 * leaf_dev
    channels = m.shape[0] // KP
    slots = idx.shape[0]
    steps = slots // GROUP
    rows = GROUP * KP
    is_odd = lax.rem(lax.axis_index("cells"), 2) == 1

    src[:, 0:leaf_dev] = m[...]
    mid = first.shape[0]
    a, b = first[...].astype(f32), second[...].astype(f32)
    low, high = jnp.where(is_odd, b, a), jnp.where(is_odd, a, b)
    low_lane = lax.broadcasted_iota(jnp.int32, (mid, leaf_dev), 1) < half
    src[0:mid, leaf_dev:] = jnp.where(low_lane, low, pltpu.roll(high, half, 1)).astype(bf16)
    src[mid:, leaf_dev:] = jnp.where(low_lane, pltpu.roll(low, half, 1), high).astype(bf16)
    for c in range(channels):
        wide[:, c * leaf_dev : (c + 1) * leaf_dev] = src[c * KP : (c + 1) * KP, leaf_dev:]
    srcc[:, 0:128] = cc[...]
    srcc[:, 128:] = upward(up[...], wide, sums)
    place_of = lax.broadcasted_iota(jnp.int32, (window, 128), 0)

    def chosen(ref, group, at):
        row = ref[pl.ds(slot_of(group, at), 1), :]
        return jnp.where(place_of == row, 1.0, 0.0).astype(bf16)

    def picks(source, ref, group, out, chunk):
        for pair in range(GROUP // 2):
            at = 2 * pair
            both = jnp.concatenate([chosen(ref, group, at), chosen(ref, group, at + 1)], axis=1)
            for begin in range(0, source.shape[0], chunk):
                picked = nn(source[begin : begin + chunk, :], both).astype(bf16)
                for i in range(2):
                    for c in range(chunk // KP):
                        lane = (begin // KP + c) * 128
                        out[(at + i) * KP : (at + i + 1) * KP, lane : lane + 128] = picked[
                            c * KP : (c + 1) * KP, i * 128 : (i + 1) * 128
                        ]

    def products(group, held, held_c):
        leaf_part = nt(be[...], held[...])
        coarse_part = nt(bf[...], held_c[...])
        for i in range(2):
            blocks[2 * group + i] = leaf_part[:, i * 128 : (i + 1) * 128]
            blocks[2 * group + slots // 4 + i] = coarse_part[:, i * 128 : (i + 1) * 128]
        ops = pl.ds(pl.multiple_of(group * rows, rows), rows)
        near[...] += nn(lops[:, ops], held[...])
        far[...] += nn(cops[:, ops], held_c[...])

    def pick_group(group, held, held_c):
        picks(src, idx, group, held, CHUNK)
        picks(srcc, idxc, group, held_c, 128)

    near[...] = jnp.zeros_like(near)
    far[...] = jnp.zeros_like(far)
    pick_group(0, even, even_c)

    def two_groups(i, carry):
        group = 2 * i + 1
        pick_group(group, odd, odd_c)
        products(group - 1, even, even_c)
        pick_group(group + 1, even, even_c)
        products(group, odd, odd_c)
        return carry

    lax.fori_loop(0, steps // 2 - 1, two_groups, 0)
    pick_group(steps - 1, odd, odd_c)
    products(steps - 2, even, even_c)
    products(steps - 1, odd, odd_c)
    for b in range(slots // 2):
        turned[:, b, :] = blocks[b]
    g_out[...] = turned[...].astype(bf16)


def potential_kernel(near, far, down, base, inside, out, field, total):
    leaf_dev = near.shape[1] // out.shape[0]
    lanes = OCT * 128
    copies = jnp.where(
        lax.broadcasted_iota(jnp.int32, (128, lanes), 1) // OCT
        == lax.broadcasted_iota(jnp.int32, (128, lanes), 0),
        1.0,
        0.0,
    ).astype(bf16)
    for at in range(far.shape[1] // 128):
        parent = nn(far[:, at * 128 : (at + 1) * 128].astype(bf16), copies).astype(bf16)
        child = nn(down[...], by_octant(parent))
        columns = slice(at * lanes, (at + 1) * lanes)
        expansion = (near[:, columns] + child).astype(bf16)
        for c in range(OCT):
            field[c * KP : (c + 1) * KP, :] = expansion[:, c * leaf_dev : (c + 1) * leaf_dev]
        for c in range(OCT):
            row = at * OCT + c
            per_atom = nn(field[c * KP : (c + 1) * KP, :], inside[...])
            total[row : row + 1, :] = jnp.sum(base[...] * per_atom, axis=0, keepdims=True)
    out[...] = total[...].astype(bf16)


def reduce_kernel(parts, after, out):
    total = parts[0].astype(f32)
    for d in range(1, parts.shape[0]):
        total = total + parts[d].astype(f32)
    turned = total.T
    pieces = []
    for level in range(2):
        for place in range(4):
            pieces.append(turned[place * KP : (place + 1) * KP, level * 16 : (level + 1) * 16])
    laid = jnp.concatenate(pieces, axis=1).astype(bf16)
    for d in range(out.shape[0]):
        out[d] = laid


def unpack_kernel(whole, leaf_out, coarse_out):
    kcount, jcount, slots = leaf_out.shape
    for k in range(kcount):
        row = whole[k].astype(f32)
        leaf_out[k] = row[0:jcount, 0:slots]
        coarse_out[k] = pltpu.roll(row, slots, 1)[0:jcount, 0:slots]


def mixing_kernel(whole, mix, charges, out, mixed):
    part = out.shape[0]
    me = lax.axis_index("chan")
    mixed[...] = lax.dot_general(
        mix[...], whole[...], (((0,), (0,)), ((), ())), preferred_element_type=f32
    )
    out[...] = (charges[...].astype(f32) + mixed[pl.ds(me * part, part), :]).astype(bf16)


def call(kernel, outs, scratch, flops=10**8, moved=10**6, limit=VMEM_BYTES, **kw):
    return pl.pallas_call(
        kernel,
        out_shape=outs,
        scratch_shapes=scratch,
        compiler_params=pltpu.CompilerParams(vmem_limit_bytes=limit),
        cost_estimate=pl.CostEstimate(flops=flops, bytes_accessed=moved, transcendentals=0),
        **kw,
    )


def from_chan(block):
    count = lax.axis_size("chan")
    return [lax.ppermute(block, "chan", [(i, i ^ d) for i in range(count)]) for d in range(1, count)]


def local(
    charges, basis, atom_leaf, leaf_lists, coarse_lists, up_ops, down_ops, leaf_ops, coarse_ops, mix, cotangent
):
    part, atoms = charges.shape
    kcount = basis.shape[0]
    slots, leaf_dev = leaf_lists.shape
    rows = part * KP
    steps = slots // GROUP
    cells = lax.axis_size("cells")
    devices = cells * lax.axis_size("chan")
    leaf = atom_leaf.reshape(1, atoms)
    shape = jax.ShapeDtypeStruct
    far_off = pl.BlockSpec(memory_space=pltpu.HBM)
    near_by = pl.BlockSpec(memory_space=pltpu.VMEM)
    like = lambda a: pltpu.VMEM(a.shape, a.dtype)
    stay = lambda *arrays: [pltpu.with_memory_space_constraint(a, pltpu.HBM) for a in arrays]
    wide = part * leaf_dev
    count = slots * KP

    cot = from_chan(cotangent)
    held = (
        cotangent,
        mix,
        jnp.swapaxes(up_ops, 0, 1),
        jnp.swapaxes(down_ops, 0, 1),
        leaf_ops,
        coarse_ops,
        leaf_lists,
        coarse_lists.T,
    )
    m, first, second, base, inside, charges_near, *held = call(
        moments_kernel,
        (
            shape((rows, leaf_dev), bf16),
            shape((rows // 2, leaf_dev), bf16),
            shape((rows // 2, leaf_dev), bf16),
            shape((KP, atoms), f32),
            shape((leaf_dev, atoms), bf16),
            shape(charges.shape, bf16),
            *[shape(a.shape, a.dtype) for a in held],
        ),
        [like(basis), like(leaf), pltpu.VMEM((rows, atoms), bf16), pltpu.SemaphoreType.DMA((3 + MORE,))],
        in_specs=[far_off] * (3 + MORE),
    )(*stay(charges, basis, leaf, *held))
    inner = [(i, i + 1) for i in range(1, cells - 1, 2)]
    outer = [(i, i + 1) for i in range(0, cells - 1, 2)]
    first = lax.ppermute(first, "cells", inner + [(b, a) for a, b in inner])
    second = lax.ppermute(second, "cells", outer + [(b, a) for a, b in outer])
    own, mix_near, *prepared = held

    wide_ops = shape((KP, OCT * KP), bf16)
    cc, up, down, back_ops, lops, cops, idx, idxc = call(
        prepare_kernel,
        (
            shape((128, 128), bf16),
            wide_ops,
            wide_ops,
            wide_ops,
            shape((KP, count), bf16),
            shape((KP, count), bf16),
            shape((slots, 128), jnp.int32),
            shape((slots, 128), jnp.int32),
        ),
        [
            pltpu.VMEM((KP, wide), bf16),
            pltpu.VMEM((2, OCT, KP, 128), f32),
            pltpu.VMEM((kcount, KP, 128), f32),
            pltpu.VMEM((KP, slots, KP), f32),
            pltpu.VMEM((128, OCT * 128), bf16),
        ],
    )(*prepared, m)
    be, bf = call(
        back_kernel,
        (shape((KP, wide), bf16), shape((KP, wide // OCT), bf16)),
        [
            pltpu.VMEM((rows, atoms), bf16),
            pltpu.VMEM((mix.shape[0], atoms), bf16),
            pltpu.VMEM((128, OCT * 128), bf16),
        ],
    )(own, *cot, mix_near, base, inside, back_ops)

    near, far, grads = call(
        grads_kernel,
        (shape((KP, wide), f32), shape((KP, wide // OCT), f32), shape((KP, slots // 2, 128), bf16)),
        [
            pltpu.VMEM((rows, 2 * leaf_dev), bf16),
            pltpu.VMEM((128, 256), bf16),
            pltpu.VMEM((KP, wide), bf16),
            pltpu.VMEM((GROUP * KP, wide), bf16),
            pltpu.VMEM((GROUP * KP, wide), bf16),
            pltpu.VMEM((GROUP * KP, wide // OCT), bf16),
            pltpu.VMEM((GROUP * KP, wide // OCT), bf16),
            pltpu.VMEM((128, OCT * 128), bf16),
            pltpu.VMEM((slots // 2, KP, 128), f32),
            pltpu.VMEM((KP, slots // 2, 128), f32),
        ],
    )(m, first, second, cc, be, bf, up, idx, idxc, lops, cops)
    potential = call(
        potential_kernel,
        shape((part, atoms), bf16),
        [pltpu.VMEM((OCT * KP, leaf_dev), bf16), pltpu.VMEM((part, atoms), f32)],
    )(near, far, down, base, inside)

    axes = ("cells", "chan")
    if devices == KP:
        parts = lax.all_to_all(grads, axes, 0, 0)
        spread_out = call(
            reduce_kernel, shape((devices, KP, 128), bf16), [], in_specs=[near_by, pl.BlockSpec(memory_space=pl.ANY)]
        )(parts, potential)
        whole = lax.all_to_all(spread_out, axes, 0, 0)
    else:
        laid = grads.reshape(KP, 2, slots // 4, 4, KP)
        laid = jnp.transpose(laid, (0, 4, 1, 3, 2)).reshape(devices, -1, 128)
        parts = lax.all_to_all(laid, axes, 0, 0)
        mine = jnp.sum(parts.astype(f32), axis=0).astype(bf16)
        whole = lax.all_gather(mine, axes).reshape(KP, KP, 128)
    grad_shape = shape((kcount, kcount, slots), f32)
    grad_leaf, grad_coarse = call(unpack_kernel, (grad_shape, grad_shape), [])(whole)

    refined = call(
        mixing_kernel,
        shape((part, atoms), bf16),
        [pltpu.VMEM((mix.shape[0], atoms), f32)],
    )(lax.all_gather(potential, "chan", axis=0, tiled=True), mix_near, charges_near)
    return refined, grad_leaf, grad_coarse


def solution(mesh):
    placed = (
        P("chan", "cells"),
        P(None, "cells"),
        P("cells"),
        P(None, "cells"),
        P(None, "cells"),
        P(),
        P(),
        P(),
        P(),
        P(),
        P("chan", "cells"),
    )
    return jax.shard_map(
        local, mesh=mesh, in_specs=placed, out_specs=(P("chan", "cells"), P(), P()), check_vma=False
    )
```

time: 93.9 us -> 63 us (0.67)
  local copies, waits for them, and re-layouts: 15.8 us -> 0.01 us
  Pallas kernels: 40.1 us -> 27.3 us
  blocking collectives: 16.4 us -> 7.4 us
  waiting for transfers between devices: 6.45 us -> 11.5 us
  starting transfers between devices: 12.5 us -> 15.8 us
    all_to_all x1 -> x0, blocking collectives: 16.4 us -> none  [local(): parts = lax.all_to_all(grads, axes, 0, 0)]
    unnamed x32 -> x2, local copies, waits for them, and re-layouts: 14.1 us -> 0.01 us
    pallas_call x4 -> x5, Pallas kernels: 37.5 us -> 23.6 us  [the longest x1 15.8 us: local(): call(grads_kernel, (shape((KP, wide), f32), shape((KP, wide // OCT), f32)...]
    all_to_all x0 -> x1, waiting for transfers between devices: none -> 8.19 us  [local(): parts = lax.all_to_all(grads, axes, 0, 0)]
    all_gather x0 -> x1, blocking collectives: none -> 7.4 us  [local(): lax.all_gather(potential, 'chan', axis=0, tiled=True)]
    ppermute x6 -> x5, waiting for transfers between devices: 6.44 us -> 0.96 us  [the longest x3 0.96 us: from_chan(): lax.ppermute(block, 'chan', [(i, i ^ d) for i in range(count)])]
    all_to_all x0 -> x1, starting transfers between devices: none -> 4.62 us  [local(): parts = lax.all_to_all(grads, axes, 0, 0)]
    all_to_all x1, waiting for transfers between devices: 0.01 us -> 2.3 us  [local(): whole = lax.all_to_all(spread_out, axes, 0, 0)]
  transfers between devices with their start and end apart: 7 -> 7, of which waited for: 3 -> 3; matrix products, arithmetic and copies ran while one was open for 8% -> 0% of each run, Pallas kernels for 19% -> 12%
where the time goes in v2:
time: 63 us; the launch traced here: 62.7 us
  Pallas kernels  27.3 us (43%)
  starting transfers between devices  15.8 us (25%)
  waiting for transfers between devices  11.5 us (18%)
  blocking collectives  7.4 us (12%)
  between operations  0.73 us (1%)
    pallas_call x1, Pallas kernels, local(): call(grads_kernel, (shape((KP, wide), f32), shape((KP, wide // OCT), f32)...  15.8 us
    all_to_all x1, waiting for transfers between devices, local(): parts = lax.all_to_all(grads, axes, 0, 0)  8.19 us
    all_gather x1, blocking collectives, local(): lax.all_gather(potential, 'chan', axis=0, tiled=True)  7.4 us
    ppermute x1, starting transfers between devices, local(): second = lax.ppermute(second, 'cells', outer + [(b, a) for a, b in outer])  5.79 us
    all_to_all x1, starting transfers between devices, local(): parts = lax.all_to_all(grads, axes, 0, 0)  4.62 us
    pallas_call x1, Pallas kernels, local(): call(prepare_kernel, (shape((128, 128), bf16), wide_ops, wide_ops, wide_o...  2.78 us
    all_to_all x1, starting transfers between devices, local(): whole = lax.all_to_all(spread_out, axes, 0, 0)  2.59 us
    pallas_call x1, Pallas kernels, local(): call(potential_kernel, shape((part, atoms), bf16), [pltpu.VMEM((OCT * KP,...  2.41 us
  transfers between devices with their start and end apart: 7, of which 3 were waited for; matrix products, arithmetic and copies ran while one was open for 0% of the time, Pallas kernels for 12%

profile of v2, /device:TPU:0, one launch (start us, length us, event | category | flops | bytes accessed | tf_op | source)
XLA Modules:
  0.0 62.7 jit_solution(17655700525222159882)
XLA Ops:
  0.6 0.0 copy-start
  0.6 1.9 %shard_map.130 = (bf16[1024,128]{1,0:T(8,128)(2,1)S(1)}, bf16[512,128]{1,0:T(8,128)(2,1)S(1)}, bf16[512,128]{1,0:T(8,128)(2,1)S(1)}, f32[32,1024]{1,0:T(8,128)S(...) custom-call(bf16[32,1024]{1,0:T(8,128)(2,1)} %charges_hbm.1, ...), custom_call_target="tpu_custom_call" | custom-call | flops 100000000 | bytes 1000000 | tf_op jit(solution)/shard_map/pallas_call | solution.py:399
  2.5 0.7 %collective-permute-start = (bf16[512,128]{1,0:T(8,128)(2,1)S(1)}, bf16[512,128]{1,0:T(8,128)(2,1)S(1)}, u32[]{:S(2)}, u32[]{:S(2)}) collective-permute-start(bf16[512,128]{1,0:T(8,128)(2,1)S(1)} %get-tuple-element.33), channel_id=1, source_target_pairs={{4,8},{12,16},{20,24},{8,4},{16,12},{24,20},{5,9},{13,17},{21,25},... | collective-permute-start | bytes 393224 | tf_op jit(solution)/shard_map/ppermute | solution.py:415
  3.2 5.8 %collective-permute-start.1 = (bf16[512,128]{1,0:T(8,128)(2,1)S(1)}, bf16[512,128]{1,0:T(8,128)(2,1)S(1)}, u32[]{:S(2)}, u32[]{:S(2)}) collective-permute-start(bf16[512,128]{1,0:T(8,128)(2,1)S(1)} %get-tuple-element.34), channel_id=1, source_target_pairs={{0,4},{8,12},{16,20},{24,28},{4,0},{12,8},{20,16},{28,24},{1,5},{9... | collective-permute-start | bytes 393224 | tf_op jit(solution)/shard_map/ppermute | solution.py:416
  9.0 0.0 copy-done
  9.0 0.0 collective-permute-start.2
  9.0 1.6 %collective-permute-start.4 = (bf16[32,1024]{1,0:T(8,128)(2,1)S(1)}, bf16[32,1024]{1,0:T(8,128)(2,1)S(1)}, u32[]{:S(2)}, u32[]{:S(2)}) collective-permute-start(bf16[32,1024]{1,0:T(8,128)(2,1)S(1)} %copy-done), channel_id=1, source_target_pairs={{0,3},{1,2},{2,1},{3,0},{4,7},{5,6},{6,5},{7,4},{8,11},{9,10},{10,... | collective-permute-start | bytes 196616 | tf_op jit(solution)/shard_map/ppermute | solution.py:366
  10.6 0.5 collective-permute-start.3
  11.1 2.8 %shard_map.131 = (bf16[128,128]{1,0:T(8,128)(2,1)S(1)}, bf16[32,256]{1,0:T(8,128)(2,1)S(1)}, bf16[32,256]{1,0:T(8,128)(2,1)S(1)}, bf16[32,256]{1,0:T(8,128)(2,1)...) custom-call(bf16[25,8,25]{2,1,0:T(8,128)(2,1)S(1)} %get-tuple-elemen, ...), custom_call_target="tpu_custom_call" | custom-call | flops 100000000 | bytes 1000000 | tf_op jit(solution)/shard_map/pallas_call | solution.py:420
  13.9 0.0 collective-permute-done.2.core
  13.9 0.0 collective-permute-done.4.other
  14.0 1.0 %collective-permute-done.3.cross = bf16[32,1024]{1,0:T(8,128)(2,1)S(1)} collective-permute-done((bf16[32,1024]{1,0:T(8,128)(2,1)S(1)}, bf16[32,1024]{1,0:T(8,128)(2,1)S(1)}, u32[]{:S(2)}, u32[]{:S(2)}) %collective-permute-start.3) | collective-permute-done | bytes 65568 | tf_op jit(solution)/shard_map/ppermute | solution.py:366
  14.9 1.7 %shard_map.132 = (bf16[32,4096]{1,0:T(8,128)(2,1)S(1)}, bf16[32,512]{1,0:T(8,128)(2,1)S(1)}) custom-call(bf16[32,1024]{1,0:T(8,128)(2,1)S(1)} %get-tuple-element.42.own, bf16[32,1024]{1,0:T(8,128)(2,1)S(1)} %collective-permute-done.2.core, bf16[32,1024]{1,0:T(8,128)(2,1)S(1)} %collective-permute-done.3.cross, ...), custom_call_target="tpu_custom_call" | custom-call | flops 100000000 | bytes 1000000 | tf_op jit(solution)/shard_map/pallas_call | solution.py:440
  16.7 0.0 collective-permute-done.first
  16.7 0.0 collective-permute-done.1.second
  16.7 15.8 %shard_map.133 = (f32[32,4096]{1,0:T(8,128)S(1)}, f32[32,512]{1,0:T(8,128)S(1)}, bf16[32,32,128]{2,1,0:T(8,128)(2,1)}) custom-call(bf16[1024,128]{1,0:T(8,128)(2,1)S(1)} %get-tuple-element.32.m, bf16[512,128]{1,0:T(8,128)(2,1)S(1)} %collective-permute-done.first, bf16[512,128]{1,0:T(8,128)(2,1)S(1)} %collective-permute-done.1.second, ...), custom_call_target="tpu_custom_call" | custom-call | flops 100000000 | bytes 1000000 | tf_op jit(solution)/shard_map/pallas_call | solution.py:450
  32.5 4.6 %all-to-all-start = ((bf16[32,32,128]{2,1,0:T(8,128)(2,1)}), bf16[32,32,128]{2,1,0:T(8,128)(2,1)S(1)}, u32[]{:S(2)}, u32[]{:S(2)}) async-start(bf16[32,32,128]{2,1,0:T(8,128)(2,1)} %get-tuple-element.58), calls=%async_computation | async-start | bytes 524288 | tf_op jit(solution)/shard_map/all_to_all | solution.py:474
  37.1 2.4 %shard_map.134.after = bf16[32,1024]{1,0:T(8,128)(2,1)S(1)} custom-call(f32[32,4096]{1,0:T(8,128)S(1)} %get-tuple-element.54.near, f32[32,512]{1,0:T(8,128)S(1)} %get-tuple-element.55.far, bf16[32,256]{1,0:T(8,128)(2,1)S(1)} %get-tuple-element.56.down, f32[32,1024]{1,0:T(8,128)S(1)} %get-tuple-element.44.base, bf16[128,1024]{1,0:T(8,128)(2,1)S(1)} %get-tuple-element.45.inside), custom_call_target="tpu_custom_call" | custom-call | flops 100000000 | bytes 1000000 | tf_op jit(solution)/shard_map/pallas_call | solution.py:466
  39.5 8.2 %all-to-all-done.parts = bf16[32,32,128]{2,1,0:T(8,128)(2,1)S(1)} async-done(((bf16[32,32,128]{2,1,0:T(8,128)(2,1)}), bf16[32,32,128]{2,1,0:T(8,128)(2,1)S(1)}, u32[]{:S(2)}, u32[]{:S(2)}) %all-to-all-start) | async-done | bytes 262176 | tf_op jit(solution)/shard_map/all_to_all | solution.py:474
  47.7 0.9 %shard_map.136 = bf16[32,32,128]{2,1,0:T(8,128)(2,1)} custom-call(bf16[32,32,128]{2,1,0:T(8,128)(2,1)S(1)} %all-to-all-done.parts, bf16[32,1024]{1,0:T(8,128)(2,1)S(1)} %shard_map.134.after), custom_call_target="tpu_custom_call" | custom-call | flops 100000000 | bytes 1000000 | tf_op jit(solution)/shard_map/pallas_call | solution.py:475
  48.6 2.6 %all-to-all-start.1 = ((bf16[32,32,128]{2,1,0:T(8,128)(2,1)}), bf16[32,32,128]{2,1,0:T(8,128)(2,1)S(1)}, u32[]{:S(2)}, u32[]{:S(2)}) async-start(bf16[32,32,128]{2,1,0:T(8,128)(2,1)} %shard_map.136), calls=%async_computation.1 | async-start | bytes 524288 | tf_op jit(solution)/shard_map/all_to_all | solution.py:478
  51.2 7.4 %all_gather.3.whole = bf16[128,1024]{1,0:T(8,128)(2,1)S(1)} all-gather(bf16[32,1024]{1,0:T(8,128)(2,1)S(1)} %shard_map.134.after), channel_id=1, replica_groups=mesh['cells'=8,'chan'=4] {'chan'}, dimensions={0}, use_global_device_ids=true | all-gather | bytes 327680 | tf_op jit(solution)/shard_map/all_gather | solution.py:492
  58.6 0.9 %shard_map.135 = bf16[32,1024]{1,0:T(8,128)(2,1)} custom-call(bf16[128,1024]{1,0:T(8,128)(2,1)S(1)} %all_gather.3.whole, bf16[128,128]{1,0:T(8,128)(2,1)S(1)} %get-tuple-element.43.mix, bf16[32,1024]{1,0:T(8,128)(2,1)S(1)} %get-tuple-element.57.charges), custom_call_target="tpu_custom_call" | custom-call | flops 100000000 | bytes 1000000 | tf_op jit(solution)/shard_map/pallas_call | solution.py:488
  59.5 2.3 %all-to-all-done.1.whole = bf16[32,32,128]{2,1,0:T(8,128)(2,1)S(1)} async-done(((bf16[32,32,128]{2,1,0:T(8,128)(2,1)}), bf16[32,32,128]{2,1,0:T(8,128)(2,1)S(1)}, u32[]{:S(2)}, u32[]{:S(2)}) %all-to-all-start.1) | async-done | bytes 262176 | tf_op jit(solution)/shard_map/all_to_all | solution.py:478
  61.8 0.9 %shard_map.137 = (f32[25,25,64]{2,1,0:T(8,128)}, f32[25,25,64]{2,1,0:T(8,128)}) custom-call(bf16[32,32,128]{2,1,0:T(8,128)(2,1)S(1)} %all-to-all-done.1.whole), custom_call_target="tpu_custom_call" | custom-call | flops 100000000 | bytes 1000000 | tf_op jit(solution)/shard_map/pallas_call | solution.py:486
Async XLA Ops:
  0.6 8.4 %copy-start = (bf16[32,1024]{1,0:T(8,128)(2,1)S(1)}, bf16[32,1024]{1,0:T(8,128)(2,1)}, u32[]{:S(2)}) copy-start(bf16[32,1024]{1,0:T(8,128)(2,1)} %rest_0_.1) | copy-start | bytes 196612
  2.5 14.1 %collective-permute-start = (bf16[512,128]{1,0:T(8,128)(2,1)S(1)}, bf16[512,128]{1,0:T(8,128)(2,1)S(1)}, u32[]{:S(2)}, u32[]{:S(2)}) collective-permute-start(bf16[512,128]{1,0:T(8,128)(2,1)S(1)} %get-tuple-element.33), channel_id=1, source_target_pairs={{4,8},{12,16},{20,24},{8,4},{16,12},{24,20},{5,9},{13,17},{21,25},... | collective-permute-start | bytes 393224 | tf_op jit(solution)/shard_map/ppermute | solution.py:415
  3.2 13.5 %collective-permute-start.1 = (bf16[512,128]{1,0:T(8,128)(2,1)S(1)}, bf16[512,128]{1,0:T(8,128)(2,1)S(1)}, u32[]{:S(2)}, u32[]{:S(2)}) collective-permute-start(bf16[512,128]{1,0:T(8,128)(2,1)S(1)} %get-tuple-element.34), channel_id=1, source_target_pairs={{0,4},{8,12},{16,20},{24,28},{4,0},{12,8},{20,16},{28,24},{1,5},{9... | collective-permute-start | bytes 393224 | tf_op jit(solution)/shard_map/ppermute | solution.py:416
  9.0 4.9 %collective-permute-start.2 = (bf16[32,1024]{1,0:T(8,128)(2,1)S(1)}, bf16[32,1024]{1,0:T(8,128)(2,1)S(1)}, u32[]{:S(2)}, u32[]{:S(2)}) collective-permute-start(bf16[32,1024]{1,0:T(8,128)(2,1)S(1)} %copy-done), channel_id=1, source_target_pairs={{0,1},{1,0},{2,3},{3,2},{4,5},{5,4},{6,7},{7,6},{8,9},{9,8},{10,11... | collective-permute-start | bytes 196616 | tf_op jit(solution)/shard_map/ppermute | solution.py:366
  9.0 4.9 %collective-permute-start.4 = (bf16[32,1024]{1,0:T(8,128)(2,1)S(1)}, bf16[32,1024]{1,0:T(8,128)(2,1)S(1)}, u32[]{:S(2)}, u32[]{:S(2)}) collective-permute-start(bf16[32,1024]{1,0:T(8,128)(2,1)S(1)} %copy-done), channel_id=1, source_target_pairs={{0,3},{1,2},{2,1},{3,0},{4,7},{5,6},{6,5},{7,4},{8,11},{9,10},{10,... | collective-permute-start | bytes 196616 | tf_op jit(solution)/shard_map/ppermute | solution.py:366
  10.6 4.3 %collective-permute-start.3 = (bf16[32,1024]{1,0:T(8,128)(2,1)S(1)}, bf16[32,1024]{1,0:T(8,128)(2,1)S(1)}, u32[]{:S(2)}, u32[]{:S(2)}) collective-permute-start(bf16[32,1024]{1,0:T(8,128)(2,1)S(1)} %copy-done), channel_id=1, source_target_pairs={{0,2},{1,3},{2,0},{3,1},{4,6},{5,7},{6,4},{7,5},{8,10},{9,11},{10,... | collective-permute-start | bytes 196616 | tf_op jit(solution)/shard_map/ppermute | solution.py:366
  32.5 15.2 %all-to-all-start = ((bf16[32,32,128]{2,1,0:T(8,128)(2,1)}), bf16[32,32,128]{2,1,0:T(8,128)(2,1)S(1)}, u32[]{:S(2)}, u32[]{:S(2)}) async-start(bf16[32,32,128]{2,1,0:T(8,128)(2,1)} %get-tuple-element.58), calls=%async_computation | async-start | bytes 524288 | tf_op jit(solution)/shard_map/all_to_all | solution.py:474
  48.6 13.2 %all-to-all-start.1 = ((bf16[32,32,128]{2,1,0:T(8,128)(2,1)}), bf16[32,32,128]{2,1,0:T(8,128)(2,1)S(1)}, u32[]{:S(2)}, u32[]{:S(2)}) async-start(bf16[32,32,128]{2,1,0:T(8,128)(2,1)} %shard_map.136), calls=%async_computation.1 | async-start | bytes 524288 | tf_op jit(solution)/shard_map/all_to_all | solution.py:478

commit v3 on v2

--- a/solution.py
+++ b/solution.py
@@ -1,3 +1,5 @@
+import functools
+
 import jax
 import jax.numpy as jnp
 from jax import lax
@@ -7,7 +9,9 @@
 
 KP = 32
 GROUP = 8
-CHUNK = 128
+KM = 24
+CHUNK = 8
+FOUR = 4
 OCT = 8
 MORE = 8
 VMEM_BYTES = 24 * 1024 * 1024
@@ -30,8 +34,21 @@
 
 def spread(base, values, scaled):
     wide = values.astype(f32)
-    for c in range(values.shape[0]):
-        scaled[c * KP : (c + 1) * KP, :] = (base[...] * wide[c : c + 1, :]).astype(bf16)
+    count = values.shape[0]
+    for c in range(0, count, 2):
+        pair = [base[0:KM, :] * wide[c + i : c + i + 1, :] for i in range(2)]
+        scaled[c * KM : (c + 2) * KM, :] = jnp.concatenate(pair, axis=0).astype(bf16)
+    scaled[count * KM :, :] = (base[KM : KM + 1, :] * wide).astype(bf16)
+
+
+def lay_wide(rows, out):
+    count = rows.shape[0] // (KM + 1)
+    lanes = rows.shape[1]
+    top = lax.broadcasted_iota(jnp.int32, (KP - KM, lanes), 0) == 0
+    for c in range(count):
+        last = jnp.where(top, rows[count * KM + c : count * KM + c + 1, :], 0.0)
+        block = jnp.concatenate([rows[c * KM : (c + 1) * KM, :], last], axis=0)
+        out[:, c * lanes : (c + 1) * lanes] = block.astype(bf16)
 
 
 def fetch(pairs, sems):
@@ -62,7 +79,14 @@
     for part in range(wide_ref.shape[1] // lanes):
         spaced = by_octant(wide_ref[:, part * lanes : (part + 1) * lanes])
         sums[part * KP : (part + 1) * KP, :] = nn(ops, spaced).astype(bf16)
-    return nn(sums[...], pooling(lanes, 128)).astype(bf16)
+    return nn(sums[...], pooling(lanes, 128))
+
+
+def tightened(rows):
+    count = rows.shape[0] // KP
+    whole = [rows[c * KP : c * KP + KM] for c in range(count)]
+    last = [rows[c * KP + KM : c * KP + KM + 1] for c in range(count)]
+    return jnp.concatenate(whole + last, axis=0).astype(bf16)
 
 
 def moments_kernel(charges_hbm, basis_hbm, leaf_hbm, *rest):
@@ -97,6 +121,10 @@
         copy.wait()
 
 
+def slot_of(group, at):
+    return at * GROUP + group
+
+
 def slot_ops(ops, padded, turned, out):
     kcount, jcount, slots = ops.shape
     turned[...] = jnp.zeros_like(turned)
@@ -104,11 +132,11 @@
     for k in range(kcount):
         padded[k, 0:jcount, 0:slots] = ops[k].astype(f32)
         turned[k, :, :] = padded[k].T[0:slots]
-    blocks = slots // 4
-    for b in range(blocks):
-        out[:, b * 128 : (b + 1) * 128] = jnp.concatenate(
-            [turned[:, place * blocks + b, :] for place in range(4)], axis=1
-        ).astype(bf16)
+    for group in range(out.shape[0]):
+        held = [turned[:, slot_of(group, at), :] for at in range(GROUP)]
+        pieces = [a[:, 0:KM] for a in held] + [a[:, KM : KM + 1] for a in held]
+        pieces.append(jnp.zeros((KP, GROUP * KP - GROUP * (KM + 1)), f32))
+        out[group] = jnp.concatenate(pieces, axis=1).astype(bf16)
 
 
 def prepare_kernel(
@@ -138,8 +166,7 @@
     kcount = up.shape[0]
     coarse_dev, slots = cl.shape
     cell = lax.axis_index("cells")
-    for c in range(m.shape[0] // KP):
-        wide[:, c * leaf_dev : (c + 1) * leaf_dev] = m[c * KP : (c + 1) * KP, :]
+    lay_wide(m[...].astype(f32), wide)
     stack[...] = jnp.zeros_like(stack)
     for k in range(kcount):
         stack[0, :, k, 0:kcount] = up[k].astype(f32)
@@ -151,7 +178,7 @@
     up_out[...] = side_by_side([stack[0, o, :, 0:KP] for o in range(OCT)])
     down_out[...] = side_by_side([stack[1, o, :, 0:KP] for o in range(OCT)])
     back_out[...] = side_by_side([stack[1, o].T[0:KP, :] for o in range(OCT)])
-    cc_out[...] = upward(up_out[...], wide, sums)
+    cc_out[...] = tightened(upward(up_out[...], wide, sums))
 
     slot_ops(lops, padded, turned, lops_out)
     slot_ops(cops, padded, turned, cops_out)
@@ -175,7 +202,6 @@
 
 
 def back_kernel(own, core, cross, other, mix, base, inside, back_ops, be_out, bf_out, scaled, gathered, sums):
-    leaf_dev = inside.shape[0]
     part = own.shape[0]
     me = lax.axis_index("chan")
     gathered[pl.ds(me * part, part), :] = own[...]
@@ -184,16 +210,10 @@
     gathered[pl.ds((me ^ 3) * part, part), :] = other[...]
     potential = nn(mix[pl.ds(me * part, part), :], gathered[...]).astype(bf16)
     spread(base, potential, scaled)
-    be = nt(scaled[...], inside[...]).astype(bf16)
-    for c in range(part):
-        be_out[:, c * leaf_dev : (c + 1) * leaf_dev] = be[c * KP : (c + 1) * KP, :]
-    far = upward(back_ops[...], be_out, sums)
+    lay_wide(nt(scaled[...], inside[...]), be_out)
+    far = upward(back_ops[...], be_out, sums).astype(bf16)
     for at in range(far.shape[0] // KP):
         bf_out[:, at * 128 : (at + 1) * 128] = far[at * KP : (at + 1) * KP, :]
-
-
-def slot_of(group, at):
-    return (at % 4) * 16 + 2 * group + at // 4
 
 
 def grads_kernel(
@@ -218,17 +238,22 @@
     odd,
     even_c,
     odd_c,
+    even_last,
+    odd_last,
+    even_c_last,
+    odd_c_last,
     sums,
     blocks,
-    turned,
+    flat,
+    *,
+    kcount,
 ):
     leaf_dev = m.shape[1]
     half = leaf_dev // 2
     window = 2 * leaf_dev
-    channels = m.shape[0] // KP
-    slots = idx.shape[0]
-    steps = slots // GROUP
-    rows = GROUP * KP
+    channels = m.shape[0] // kcount
+    steps = idx.shape[0] // GROUP
+    tight = even.shape[0]
     is_odd = lax.rem(lax.axis_index("cells"), 2) == 1
 
     src[:, 0:leaf_dev] = m[...]
@@ -236,67 +261,86 @@
     a, b = first[...].astype(f32), second[...].astype(f32)
     low, high = jnp.where(is_odd, b, a), jnp.where(is_odd, a, b)
     low_lane = lax.broadcasted_iota(jnp.int32, (mid, leaf_dev), 1) < half
-    src[0:mid, leaf_dev:] = jnp.where(low_lane, low, pltpu.roll(high, half, 1)).astype(bf16)
-    src[mid:, leaf_dev:] = jnp.where(low_lane, pltpu.roll(low, half, 1), high).astype(bf16)
-    for c in range(channels):
-        wide[:, c * leaf_dev : (c + 1) * leaf_dev] = src[c * KP : (c + 1) * KP, leaf_dev:]
+    upper = jnp.where(low_lane, low, pltpu.roll(high, half, 1))
+    lower = jnp.where(low_lane, pltpu.roll(low, half, 1), high)
+    src[0:mid, leaf_dev:] = upper.astype(bf16)
+    src[mid:, leaf_dev:] = lower.astype(bf16)
+    lay_wide(src[:, leaf_dev:].astype(f32), wide)
     srcc[:, 0:128] = cc[...]
-    srcc[:, 128:] = upward(up[...], wide, sums)
+    srcc[:, 128:] = tightened(upward(up[...], wide, sums))
     place_of = lax.broadcasted_iota(jnp.int32, (window, 128), 0)
 
     def chosen(ref, group, at):
         row = ref[pl.ds(slot_of(group, at), 1), :]
         return jnp.where(place_of == row, 1.0, 0.0).astype(bf16)
 
-    def picks(source, ref, group, out, chunk):
+    def picks(source, ref, group, held, last, chunk):
+        count = source.shape[0] // kcount
         for pair in range(GROUP // 2):
             at = 2 * pair
             both = jnp.concatenate([chosen(ref, group, at), chosen(ref, group, at + 1)], axis=1)
-            for begin in range(0, source.shape[0], chunk):
-                picked = nn(source[begin : begin + chunk, :], both).astype(bf16)
-                for i in range(2):
-                    for c in range(chunk // KP):
-                        lane = (begin // KP + c) * 128
-                        out[(at + i) * KP : (at + i + 1) * KP, lane : lane + 128] = picked[
-                            c * KP : (c + 1) * KP, i * 128 : (i + 1) * 128
-                        ]
+            for begin in range(0, count, chunk):
+                picked = nn(source[begin * KM : (begin + chunk) * KM, :], both)
+                for c in range(chunk):
+                    rows = picked[c * KM : (c + 1) * KM]
+                    lane = (begin + c) * 128
+                    held[at * KM : (at + 2) * KM, lane : lane + 128] = jnp.concatenate(
+                        [rows[:, 0:128], rows[:, 128:]], axis=0
+                    ).astype(bf16)
+            picked = nn(source[count * KM :, :], both)
+            for i in range(2):
+                for c in range(count):
+                    last[at + i : at + i + 1, c * 128 : (c + 1) * 128] = picked[
+                        c : c + 1, i * 128 : (i + 1) * 128
+                    ]
+        held[GROUP * KM :, :] = last[...].astype(bf16)
+
+    def pick_group(group, held, last, held_c, last_c):
+        picks(src, idx, group, held, last, CHUNK)
+        picks(srcc, idxc, group, held_c, last_c, srcc.shape[0] // kcount)
 
     def products(group, held, held_c):
-        leaf_part = nt(be[...], held[...])
-        coarse_part = nt(bf[...], held_c[...])
-        for i in range(2):
-            blocks[2 * group + i] = leaf_part[:, i * 128 : (i + 1) * 128]
-            blocks[2 * group + slots // 4 + i] = coarse_part[:, i * 128 : (i + 1) * 128]
-        ops = pl.ds(pl.multiple_of(group * rows, rows), rows)
-        near[...] += nn(lops[:, ops], held[...])
-        far[...] += nn(cops[:, ops], held_c[...])
-
-    def pick_group(group, held, held_c):
-        picks(src, idx, group, held, CHUNK)
-        picks(srcc, idxc, group, held_c, 128)
-
-    near[...] = jnp.zeros_like(near)
-    far[...] = jnp.zeros_like(far)
-    pick_group(0, even, even_c)
+        blocks[group, :, 0:tight] = nt(be[...], held[...])
+        blocks[steps + group, :, 0:tight] = nt(bf[...], held_c[...])
+        near[...] += nn(lops[group][:, 0:tight], held[...])
+        far[...] += nn(cops[group][:, 0:tight], held_c[...])
+
+    for ref in (near, far, even_last, odd_last, even_c_last, odd_c_last):
+        ref[...] = jnp.zeros_like(ref)
+    evens, odds = (even, even_last, even_c, even_c_last), (odd, odd_last, odd_c, odd_c_last)
+    pick_group(0, *evens)
 
     def two_groups(i, carry):
         group = 2 * i + 1
-        pick_group(group, odd, odd_c)
+        pick_group(group, *odds)
         products(group - 1, even, even_c)
-        pick_group(group + 1, even, even_c)
+        pick_group(group + 1, *evens)
         products(group, odd, odd_c)
         return carry
 
     lax.fori_loop(0, steps // 2 - 1, two_groups, 0)
-    pick_group(steps - 1, odd, odd_c)
+    pick_group(steps - 1, *odds)
     products(steps - 2, even, even_c)
     products(steps - 1, odd, odd_c)
-    for b in range(slots // 2):
-        turned[:, b, :] = blocks[b]
-    g_out[...] = turned[...].astype(bf16)
-
-
-def potential_kernel(near, far, down, base, inside, out, field, total):
+    flat[...] = jnp.zeros_like(flat)
+    main = GROUP * KM
+    for turn in range(-(-kcount // FOUR)):
+        several = jnp.concatenate([blocks[:, turn * FOUR + k, :] for k in range(FOUR)], axis=0)
+        across = several.T
+        for tile in range(GROUP // 2):
+            at = 2 * tile
+            body = jnp.concatenate([across[a * KM : (a + 1) * KM] for a in (at, at + 1)], axis=1)
+            rest = jnp.concatenate([across[main + a : main + a + 1] for a in (at, at + 1)], axis=1)
+            rows = pl.ds(turn * FOUR * kcount + tile, kcount, stride=FOUR)
+            flat[rows, :] = jnp.concatenate([body, rest], axis=0)
+    if len(g_out.shape) == 2:
+        g_out[...] = flat[...].astype(bf16)
+    else:
+        for d in range(g_out.shape[0]):
+            g_out[d] = flat[d * g_out.shape[1] : (d + 1) * g_out.shape[1], :].astype(bf16)
+
+
+def potential_kernel(near, far, down, base, inside, out, order, field, total):
     leaf_dev = near.shape[1] // out.shape[0]
     lanes = OCT * 128
     copies = jnp.where(
@@ -317,28 +361,42 @@
             per_atom = nn(field[c * KP : (c + 1) * KP, :], inside[...])
             total[row : row + 1, :] = jnp.sum(base[...] * per_atom, axis=0, keepdims=True)
     out[...] = total[...].astype(bf16)
-
-
-def reduce_kernel(parts, after, out):
-    total = parts[0].astype(f32)
+    order[...] = turned_order()
+
+
+def turned_order():
+    size = FOUR * 128
+    row = lax.broadcasted_iota(jnp.int32, (size, size), 0)
+    k, level, group, at = row // 16 % FOUR, row // GROUP % 2, row % GROUP, row // 64
+    wanted = k * 128 + level * 64 + slot_of(group, at)
+    return jnp.where(lax.broadcasted_iota(jnp.int32, (size, size), 1) == wanted, 1.0, 0.0).astype(bf16)
+
+
+def reduce_kernel(parts, after, order, out, total, laid):
+    summed = parts[0].astype(f32)
     for d in range(1, parts.shape[0]):
-        total = total + parts[d].astype(f32)
-    turned = total.T
-    pieces = []
-    for level in range(2):
-        for place in range(4):
-            pieces.append(turned[place * KP : (place + 1) * KP, level * 16 : (level + 1) * 16])
-    laid = jnp.concatenate(pieces, axis=1).astype(bf16)
+        summed = summed + parts[d].astype(f32)
+    total[...] = summed
+    count = summed.shape[0] // FOUR
+    tiles = [total[pl.ds(tile, count, stride=FOUR), :] for tile in range(FOUR)]
+    turned = nn(jnp.concatenate(tiles, axis=1).astype(bf16), order[...])
+    for k in range(FOUR):
+        laid[pl.ds(k, count, stride=FOUR), :] = turned[:, k * 128 : (k + 1) * 128]
     for d in range(out.shape[0]):
-        out[d] = laid
-
-
-def unpack_kernel(whole, leaf_out, coarse_out):
+        out[d] = laid[...].astype(bf16)
+
+
+def unpack_kernel(whole, leaf_out, coarse_out, flat):
     kcount, jcount, slots = leaf_out.shape
+    if len(whole.shape) == 2:
+        flat[...] = whole[...].astype(f32)
+    else:
+        for d in range(whole.shape[0]):
+            flat[d * whole.shape[1] : (d + 1) * whole.shape[1], :] = whole[d].astype(f32)
     for k in range(kcount):
-        row = whole[k].astype(f32)
-        leaf_out[k] = row[0:jcount, 0:slots]
-        coarse_out[k] = pltpu.roll(row, slots, 1)[0:jcount, 0:slots]
+        row = flat[pl.ds(k // FOUR * FOUR * jcount + k % FOUR, jcount, stride=FOUR), :]
+        leaf_out[k] = row[:, 0:slots]
+        coarse_out[k] = pltpu.roll(row, slots, 1)[:, 0:slots]
 
 
 def mixing_kernel(whole, mix, charges, out, mixed):
@@ -372,7 +430,8 @@
     part, atoms = charges.shape
     kcount = basis.shape[0]
     slots, leaf_dev = leaf_lists.shape
-    rows = part * KP
+    rows = part * kcount
+    coarse_rows = rows // OCT
     steps = slots // GROUP
     cells = lax.axis_size("cells")
     devices = cells * lax.axis_size("chan")
@@ -383,7 +442,6 @@
     like = lambda a: pltpu.VMEM(a.shape, a.dtype)
     stay = lambda *arrays: [pltpu.with_memory_space_constraint(a, pltpu.HBM) for a in arrays]
     wide = part * leaf_dev
-    count = slots * KP
 
     cot = from_chan(cotangent)
     held = (
@@ -417,15 +475,16 @@
     own, mix_near, *prepared = held
 
     wide_ops = shape((KP, OCT * KP), bf16)
+    group_ops = shape((steps, KP, GROUP * KP), bf16)
     cc, up, down, back_ops, lops, cops, idx, idxc = call(
         prepare_kernel,
         (
-            shape((128, 128), bf16),
+            shape((coarse_rows, 128), bf16),
             wide_ops,
             wide_ops,
             wide_ops,
-            shape((KP, count), bf16),
-            shape((KP, count), bf16),
+            group_ops,
+            group_ops,
             shape((slots, 128), jnp.int32),
             shape((slots, 128), jnp.int32),
         ),
@@ -447,43 +506,57 @@
         ],
     )(own, *cot, mix_near, base, inside, back_ops)
 
+    flat_rows = -(-(-(-kcount // FOUR) * FOUR * kcount) // 256) * 256
+    fits = flat_rows % (8 * devices) == 0
+    laid = (devices, flat_rows // devices, 128) if fits else (flat_rows, 128)
     near, far, grads = call(
-        grads_kernel,
-        (shape((KP, wide), f32), shape((KP, wide // OCT), f32), shape((KP, slots // 2, 128), bf16)),
+        functools.partial(grads_kernel, kcount=kcount),
+        (shape((KP, wide), f32), shape((KP, wide // OCT), f32), shape(laid, bf16)),
         [
             pltpu.VMEM((rows, 2 * leaf_dev), bf16),
-            pltpu.VMEM((128, 256), bf16),
+            pltpu.VMEM((coarse_rows, 256), bf16),
             pltpu.VMEM((KP, wide), bf16),
-            pltpu.VMEM((GROUP * KP, wide), bf16),
-            pltpu.VMEM((GROUP * KP, wide), bf16),
-            pltpu.VMEM((GROUP * KP, wide // OCT), bf16),
-            pltpu.VMEM((GROUP * KP, wide // OCT), bf16),
+            pltpu.VMEM((GROUP * KM + 16, wide), bf16),
+            pltpu.VMEM((GROUP * KM + 16, wide), bf16),
+            pltpu.VMEM((GROUP * KM + 16, wide // OCT), bf16),
+            pltpu.VMEM((GROUP * KM + 16, wide // OCT), bf16),
+            pltpu.VMEM((16, wide), f32),
+            pltpu.VMEM((16, wide), f32),
+            pltpu.VMEM((16, wide // OCT), f32),
+            pltpu.VMEM((16, wide // OCT), f32),
             pltpu.VMEM((128, OCT * 128), bf16),
-            pltpu.VMEM((slots // 2, KP, 128), f32),
-            pltpu.VMEM((KP, slots // 2, 128), f32),
+            pltpu.VMEM((2 * steps, KP, GROUP * KP), f32),
+            pltpu.VMEM((flat_rows, 128), f32),
         ],
     )(m, first, second, cc, be, bf, up, idx, idxc, lops, cops)
-    potential = call(
+    potential, order = call(
         potential_kernel,
-        shape((part, atoms), bf16),
+        (shape((part, atoms), bf16), shape((FOUR * 128, FOUR * 128), bf16)),
         [pltpu.VMEM((OCT * KP, leaf_dev), bf16), pltpu.VMEM((part, atoms), f32)],
     )(near, far, down, base, inside)
 
     axes = ("cells", "chan")
-    if devices == KP:
+    if fits:
         parts = lax.all_to_all(grads, axes, 0, 0)
         spread_out = call(
-            reduce_kernel, shape((devices, KP, 128), bf16), [], in_specs=[near_by, pl.BlockSpec(memory_space=pl.ANY)]
-        )(parts, potential)
+            reduce_kernel,
+            shape(laid, bf16),
+            [pltpu.VMEM(laid[1:], f32), pltpu.VMEM(laid[1:], f32)],
+            in_specs=[near_by, pl.BlockSpec(memory_space=pl.ANY), near_by],
+        )(parts, potential, order)
         whole = lax.all_to_all(spread_out, axes, 0, 0)
     else:
-        laid = grads.reshape(KP, 2, slots // 4, 4, KP)
-        laid = jnp.transpose(laid, (0, 4, 1, 3, 2)).reshape(devices, -1, 128)
-        parts = lax.all_to_all(laid, axes, 0, 0)
+        split = -(-flat_rows // devices) * devices
+        pieces = jnp.pad(grads, ((0, split - flat_rows), (0, 0))).reshape(devices, -1, 128)
+        parts = lax.all_to_all(pieces, axes, 0, 0)
         mine = jnp.sum(parts.astype(f32), axis=0).astype(bf16)
-        whole = lax.all_gather(mine, axes).reshape(KP, KP, 128)
+        whole = lax.all_gather(mine, axes).reshape(split, 128)[:flat_rows]
+        whole = whole.reshape(flat_rows // FOUR, FOUR, 2, FOUR, 2, GROUP)
+        whole = jnp.transpose(whole, (0, 3, 4, 1, 2, 5)).reshape(flat_rows, 128)
     grad_shape = shape((kcount, kcount, slots), f32)
-    grad_leaf, grad_coarse = call(unpack_kernel, (grad_shape, grad_shape), [])(whole)
+    grad_leaf, grad_coarse = call(
+        unpack_kernel, (grad_shape, grad_shape), [pltpu.VMEM((flat_rows, 128), f32)]
+    )(whole)
 
     refined = call(
         mixing_kernel,

time: 63 us -> 58.8 us (0.933)
  waiting for transfers between devices: 11.5 us -> 7.78 us
  Pallas kernels: 27.3 us -> 26.5 us
    all_to_all x1, waiting for transfers between devices: 8.19 us -> 6.08 us  [local(): parts = lax.all_to_all(grads, axes, 0, 0)]
    all_to_all x1, waiting for transfers between devices: 2.3 us -> 0.79 us  [local(): whole = lax.all_to_all(spread_out, axes, 0, 0)]
    pallas_call x5, Pallas kernels: 22.8 us -> 21.9 us  [the longest x1 14.6 us: local(): call(functools.partial(grads_kernel, kcount=kcount), (shape((KP, wide), f...]
  transfers between devices with their start and end apart: 7 -> 7, of which waited for: 3 -> 3; matrix products, arithmetic and copies ran while one was open for 0% -> 0% of each run, Pallas kernels for 12% -> 14%
where the time goes in v3:
time: 58.8 us; the launch traced here: 58.3 us
  Pallas kernels  26.5 us (45%)
  starting transfers between devices  16.1 us (27%)
  waiting for transfers between devices  7.78 us (13%)
  blocking collectives  7.21 us (12%)
  between operations  0.73 us (1%)
    pallas_call x1, Pallas kernels, local(): call(functools.partial(grads_kernel, kcount=kcount), (shape((KP, wide), f...  14.6 us
    all_gather x1, blocking collectives, local(): lax.all_gather(potential, 'chan', axis=0, tiled=True)  7.21 us
    all_to_all x1, waiting for transfers between devices, local(): parts = lax.all_to_all(grads, axes, 0, 0)  6.08 us
    ppermute x1, starting transfers between devices, local(): second = lax.ppermute(second, 'cells', outer + [(b, a) for a, b in outer])  5.79 us
    all_to_all x1, starting transfers between devices, local(): parts = lax.all_to_all(grads, axes, 0, 0)  4.8 us
    pallas_call x1, Pallas kernels, local(): call(prepare_kernel, (shape((coarse_rows, 128), bf16), wide_ops, wide_ops...  2.84 us
    all_to_all x1, starting transfers between devices, local(): whole = lax.all_to_all(spread_out, axes, 0, 0)  2.71 us
    pallas_call x1, Pallas kernels, local(): call(potential_kernel, (shape((part, atoms), bf16), shape((FOUR * 128, FO...  2.62 us
  transfers between devices with their start and end apart: 7, of which 3 were waited for; matrix products, arithmetic and copies ran while one was open for 0% of the time, Pallas kernels for 14%

profile of v3, /device:TPU:0, one launch (start us, length us, event | category | flops | bytes accessed | tf_op | source)
XLA Modules:
  0.0 58.3 jit_solution(5284037022266887414)
XLA Ops:
  0.6 0.0 copy-start
  0.6 1.8 %shard_map.130 = (bf16[800,128]{1,0:T(8,128)(2,1)S(1)}, bf16[400,128]{1,0:T(8,128)(2,1)S(1)}, bf16[400,128]{1,0:T(8,128)(2,1)S(1)}, f32[32,1024]{1,0:T(8,128)S(1...) custom-call(bf16[32,1024]{1,0:T(8,128)(2,1)} %charges_hbm.1, ...), custom_call_target="tpu_custom_call" | custom-call | flops 100000000 | bytes 1000000 | tf_op jit(solution)/shard_map/pallas_call | solution.py:457
  2.4 0.7 %collective-permute-start = (bf16[400,128]{1,0:T(8,128)(2,1)S(1)}, bf16[400,128]{1,0:T(8,128)(2,1)S(1)}, u32[]{:S(2)}, u32[]{:S(2)}) collective-permute-start(bf16[400,128]{1,0:T(8,128)(2,1)S(1)} %get-tuple-element.35), channel_id=1, source_target_pairs={{4,8},{12,16},{20,24},{8,4},{16,12},{24,20},{5,9},{13,17},{21,25},... | collective-permute-start | bytes 307208 | tf_op jit(solution)/shard_map/ppermute | solution.py:473
  3.1 5.8 %collective-permute-start.1 = (bf16[400,128]{1,0:T(8,128)(2,1)S(1)}, bf16[400,128]{1,0:T(8,128)(2,1)S(1)}, u32[]{:S(2)}, u32[]{:S(2)}) collective-permute-start(bf16[400,128]{1,0:T(8,128)(2,1)S(1)} %get-tuple-element.36), channel_id=1, source_target_pairs={{0,4},{8,12},{16,20},{24,28},{4,0},{12,8},{20,16},{28,24},{1,5},{9... | collective-permute-start | bytes 307208 | tf_op jit(solution)/shard_map/ppermute | solution.py:474
  8.9 0.0 copy-done
  8.9 0.0 collective-permute-start.2
  8.9 1.6 %collective-permute-start.4 = (bf16[32,1024]{1,0:T(8,128)(2,1)S(1)}, bf16[32,1024]{1,0:T(8,128)(2,1)S(1)}, u32[]{:S(2)}, u32[]{:S(2)}) collective-permute-start(bf16[32,1024]{1,0:T(8,128)(2,1)S(1)} %copy-done), channel_id=1, source_target_pairs={{0,3},{1,2},{2,1},{3,0},{4,7},{5,6},{6,5},{7,4},{8,11},{9,10},{10,... | collective-permute-start | bytes 196616 | tf_op jit(solution)/shard_map/ppermute | solution.py:424
  10.5 0.5 collective-permute-start.3
  11.0 2.8 %shard_map.131 = (bf16[100,128]{1,0:T(8,128)(2,1)S(1)}, bf16[32,256]{1,0:T(8,128)(2,1)S(1)}, bf16[32,256]{1,0:T(8,128)(2,1)S(1)}, bf16[32,256]{1,0:T(8,128)(2,1)...) custom-call(bf16[25,8,25]{2,1,0:T(8,128)(2,1)S(1)} %get-tuple-elemen, ...), custom_call_target="tpu_custom_call" | custom-call | flops 100000000 | bytes 1000000 | tf_op jit(solution)/shard_map/pallas_call | solution.py:479
  13.9 0.0 collective-permute-done.2.core
  13.9 0.0 collective-permute-done.4.other
  13.9 0.9 %collective-permute-done.3.cross = bf16[32,1024]{1,0:T(8,128)(2,1)S(1)} collective-permute-done((bf16[32,1024]{1,0:T(8,128)(2,1)S(1)}, bf16[32,1024]{1,0:T(8,128)(2,1)S(1)}, u32[]{:S(2)}, u32[]{:S(2)}) %collective-permute-start.3) | collective-permute-done | bytes 65568 | tf_op jit(solution)/shard_map/ppermute | solution.py:424
  14.8 1.9 %shard_map.132 = (bf16[32,4096]{1,0:T(8,128)(2,1)S(1)}, bf16[32,512]{1,0:T(8,128)(2,1)S(1)}) custom-call(bf16[32,1024]{1,0:T(8,128)(2,1)S(1)} %get-tuple-element.44.own, bf16[32,1024]{1,0:T(8,128)(2,1)S(1)} %collective-permute-done.2.core, bf16[32,1024]{1,0:T(8,128)(2,1)S(1)} %collective-permute-done.3.cross, ...), custom_call_target="tpu_custom_call" | custom-call | flops 100000000 | bytes 1000000 | tf_op jit(solution)/shard_map/pallas_call | solution.py:499
  16.7 0.0 collective-permute-done.first
  16.7 0.0 collective-permute-done.1.second
  16.7 14.6 %shard_map.133 = (f32[32,4096]{1,0:T(8,128)S(1)}, f32[32,512]{1,0:T(8,128)S(1)}, bf16[32,24,128]{2,1,0:T(8,128)(2,1)}) custom-call(bf16[800,128]{1,0:T(8,128)(2,1)S(1)} %get-tuple-element.34.m, bf16[400,128]{1,0:T(8,128)(2,1)S(1)} %collective-permute-done.first, bf16[400,128]{1,0:T(8,128)(2,1)S(1)} %collective-permute-done.1.second, ...), custom_call_target="tpu_custom_call" | custom-call | flops 100000000 | bytes 1000000 | tf_op jit(solution)/shard_map/pallas_call | solution.py:512
  31.3 4.8 %all-to-all-start = ((bf16[32,24,128]{2,1,0:T(8,128)(2,1)}), bf16[32,24,128]{2,1,0:T(8,128)(2,1)S(1)}, u32[]{:S(2)}, u32[]{:S(2)}) async-start(bf16[32,24,128]{2,1,0:T(8,128)(2,1)} %get-tuple-element.61), calls=%async_computation | async-start | bytes 393216 | tf_op jit(solution)/shard_map/all_to_all | solution.py:540
  36.1 2.6 %shard_map.134 = (bf16[32,1024]{1,0:T(8,128)(2,1)S(1)}, bf16[512,512]{1,0:T(8,128)(2,1)S(1)}) custom-call(f32[32,4096]{1,0:T(8,128)S(1)} %get-tuple-element.56.near, f32[32,512]{1,0:T(8,128)S(1)} %get-tuple-element.57.far, bf16[32,256]{1,0:T(8,128)(2,1)S(1)} %get-tuple-element.58.down, f32[32,1024]{1,0:T(8,128)S(1)} %get-tuple-element.46.base, ...), custom_call_target="tpu_custom_call" | custom-call | flops 100000000 | bytes 1000000 | tf_op jit(solution)/shard_map/pallas_call | solution.py:532
  38.8 6.1 %all-to-all-done.parts = bf16[32,24,128]{2,1,0:T(8,128)(2,1)S(1)} async-done(((bf16[32,24,128]{2,1,0:T(8,128)(2,1)}), bf16[32,24,128]{2,1,0:T(8,128)(2,1)S(1)}, u32[]{:S(2)}, u32[]{:S(2)}) %all-to-all-start) | async-done | bytes 196640 | tf_op jit(solution)/shard_map/all_to_all | solution.py:540
  44.9 0.9 %shard_map.136 = bf16[32,24,128]{2,1,0:T(8,128)(2,1)} custom-call(bf16[32,24,128]{2,1,0:T(8,128)(2,1)S(1)} %all-to-all-done.parts, bf16[32,1024]{1,0:T(8,128)(2,1)S(1)} %get-tuple-element.59.after, bf16[512,512]{1,0:T(8,128)(2,1)S(1)} %get-tuple-element.62.order), custom_call_target="tpu_custom_call" | custom-call | flops 100000000 | bytes 1000000 | tf_op jit(solution)/shard_map/pallas_call | solution.py:541
  45.8 2.7 %all-to-all-start.1 = ((bf16[32,24,128]{2,1,0:T(8,128)(2,1)}), bf16[32,24,128]{2,1,0:T(8,128)(2,1)S(1)}, u32[]{:S(2)}, u32[]{:S(2)}) async-start(bf16[32,24,128]{2,1,0:T(8,128)(2,1)} %shard_map.136), calls=%async_computation.1 | async-start | bytes 393216 | tf_op jit(solution)/shard_map/all_to_all | solution.py:547
  48.5 7.2 %all_gather.3.whole = bf16[128,1024]{1,0:T(8,128)(2,1)S(1)} all-gather(bf16[32,1024]{1,0:T(8,128)(2,1)S(1)} %get-tuple-element.59.after), channel_id=1, replica_groups=mesh['cells'=8,'chan'=4] {'chan'}, dimensions={0}, use_global_device_ids=true | all-gather | bytes 327680 | tf_op jit(solution)/shard_map/all_gather | solution.py:565
  55.7 0.9 %shard_map.135 = bf16[32,1024]{1,0:T(8,128)(2,1)} custom-call(bf16[128,1024]{1,0:T(8,128)(2,1)S(1)} %all_gather.3.whole, bf16[128,128]{1,0:T(8,128)(2,1)S(1)} %get-tuple-element.45.mix, bf16[32,1024]{1,0:T(8,128)(2,1)S(1)} %get-tuple-element.60.charges), custom_call_target="tpu_custom_call" | custom-call | flops 100000000 | bytes 1000000 | tf_op jit(solution)/shard_map/pallas_call | solution.py:561
  56.6 0.8 %all-to-all-done.1.whole = bf16[32,24,128]{2,1,0:T(8,128)(2,1)S(1)} async-done(((bf16[32,24,128]{2,1,0:T(8,128)(2,1)}), bf16[32,24,128]{2,1,0:T(8,128)(2,1)S(1)}, u32[]{:S(2)}, u32[]{:S(2)}) %all-to-all-start.1) | async-done | bytes 196640 | tf_op jit(solution)/shard_map/all_to_all | solution.py:547
  57.4 0.9 %shard_map.137 = (f32[25,25,64]{2,1,0:T(8,128)}, f32[25,25,64]{2,1,0:T(8,128)}) custom-call(bf16[32,24,128]{2,1,0:T(8,128)(2,1)S(1)} %all-to-all-done.1.whole), custom_call_target="tpu_custom_call" | custom-call | flops 100000000 | bytes 1000000 | tf_op jit(solution)/shard_map/pallas_call | solution.py:557
Async XLA Ops:
  0.6 8.3 %copy-start = (bf16[32,1024]{1,0:T(8,128)(2,1)S(1)}, bf16[32,1024]{1,0:T(8,128)(2,1)}, u32[]{:S(2)}) copy-start(bf16[32,1024]{1,0:T(8,128)(2,1)} %rest_0_.1) | copy-start | bytes 196612
  2.4 14.3 %collective-permute-start = (bf16[400,128]{1,0:T(8,128)(2,1)S(1)}, bf16[400,128]{1,0:T(8,128)(2,1)S(1)}, u32[]{:S(2)}, u32[]{:S(2)}) collective-permute-start(bf16[400,128]{1,0:T(8,128)(2,1)S(1)} %get-tuple-element.35), channel_id=1, source_target_pairs={{4,8},{12,16},{20,24},{8,4},{16,12},{24,20},{5,9},{13,17},{21,25},... | collective-permute-start | bytes 307208 | tf_op jit(solution)/shard_map/ppermute | solution.py:473
  3.1 13.6 %collective-permute-start.1 = (bf16[400,128]{1,0:T(8,128)(2,1)S(1)}, bf16[400,128]{1,0:T(8,128)(2,1)S(1)}, u32[]{:S(2)}, u32[]{:S(2)}) collective-permute-start(bf16[400,128]{1,0:T(8,128)(2,1)S(1)} %get-tuple-element.36), channel_id=1, source_target_pairs={{0,4},{8,12},{16,20},{24,28},{4,0},{12,8},{20,16},{28,24},{1,5},{9... | collective-permute-start | bytes 307208 | tf_op jit(solution)/shard_map/ppermute | solution.py:474
  8.9 5.0 %collective-permute-start.2 = (bf16[32,1024]{1,0:T(8,128)(2,1)S(1)}, bf16[32,1024]{1,0:T(8,128)(2,1)S(1)}, u32[]{:S(2)}, u32[]{:S(2)}) collective-permute-start(bf16[32,1024]{1,0:T(8,128)(2,1)S(1)} %copy-done), channel_id=1, source_target_pairs={{0,1},{1,0},{2,3},{3,2},{4,5},{5,4},{6,7},{7,6},{8,9},{9,8},{10,11... | collective-permute-start | bytes 196616 | tf_op jit(solution)/shard_map/ppermute | solution.py:424
  8.9 5.0 %collective-permute-start.4 = (bf16[32,1024]{1,0:T(8,128)(2,1)S(1)}, bf16[32,1024]{1,0:T(8,128)(2,1)S(1)}, u32[]{:S(2)}, u32[]{:S(2)}) collective-permute-start(bf16[32,1024]{1,0:T(8,128)(2,1)S(1)} %copy-done), channel_id=1, source_target_pairs={{0,3},{1,2},{2,1},{3,0},{4,7},{5,6},{6,5},{7,4},{8,11},{9,10},{10,... | collective-permute-start | bytes 196616 | tf_op jit(solution)/shard_map/ppermute | solution.py:424
  10.5 4.3 %collective-permute-start.3 = (bf16[32,1024]{1,0:T(8,128)(2,1)S(1)}, bf16[32,1024]{1,0:T(8,128)(2,1)S(1)}, u32[]{:S(2)}, u32[]{:S(2)}) collective-permute-start(bf16[32,1024]{1,0:T(8,128)(2,1)S(1)} %copy-done), channel_id=1, source_target_pairs={{0,2},{1,3},{2,0},{3,1},{4,6},{5,7},{6,4},{7,5},{8,10},{9,11},{10,... | collective-permute-start | bytes 196616 | tf_op jit(solution)/shard_map/ppermute | solution.py:424
  31.3 13.5 %all-to-all-start = ((bf16[32,24,128]{2,1,0:T(8,128)(2,1)}), bf16[32,24,128]{2,1,0:T(8,128)(2,1)S(1)}, u32[]{:S(2)}, u32[]{:S(2)}) async-start(bf16[32,24,128]{2,1,0:T(8,128)(2,1)} %get-tuple-element.61), calls=%async_computation | async-start | bytes 393216 | tf_op jit(solution)/shard_map/all_to_all | solution.py:540
  45.8 11.6 %all-to-all-start.1 = ((bf16[32,24,128]{2,1,0:T(8,128)(2,1)}), bf16[32,24,128]{2,1,0:T(8,128)(2,1)S(1)}, u32[]{:S(2)}, u32[]{:S(2)}) async-start(bf16[32,24,128]{2,1,0:T(8,128)(2,1)} %shard_map.136), calls=%async_computation.1 | async-start | bytes 393216 | tf_op jit(solution)/shard_map/all_to_all | solution.py:547

commit v4 on v3

--- a/solution.py
+++ b/solution.py
@@ -74,12 +74,12 @@
     )
 
 
-def upward(ops, wide_ref, sums):
+def upward(ops, wide_ref, sums, pool):
     lanes = OCT * 128
     for part in range(wide_ref.shape[1] // lanes):
         spaced = by_octant(wide_ref[:, part * lanes : (part + 1) * lanes])
         sums[part * KP : (part + 1) * KP, :] = nn(ops, spaced).astype(bf16)
-    return nn(sums[...], pooling(lanes, 128))
+    return nn(sums[...], pool[...])
 
 
 def tightened(rows):
@@ -91,9 +91,9 @@
 
 def moments_kernel(charges_hbm, basis_hbm, leaf_hbm, *rest):
     more = rest[:MORE]
-    m_out, first_out, second_out, base_out, inside_out, charges = rest[MORE : MORE + 6]
-    held = rest[MORE + 6 : 2 * MORE + 6]
-    basis, leaf, scaled, sems = rest[2 * MORE + 6 :]
+    m_out, first_out, second_out, base_out, inside_out, pool_out, charges = rest[MORE : MORE + 7]
+    held = rest[MORE + 7 : 2 * MORE + 7]
+    basis, leaf, scaled, sems = rest[2 * MORE + 7 :]
     leaf_dev = m_out.shape[1]
     half = leaf_dev // 2
     cell = lax.axis_index("cells")
@@ -102,6 +102,7 @@
     )
     kcount = basis.shape[0]
     base_out[...] = jnp.zeros_like(base_out)
+    pool_out[...] = pooling(*pool_out.shape)
     for copy in copies[:3]:
         copy.wait()
     base_out[0:kcount, :] = basis[...]
@@ -147,6 +148,7 @@
     ll,
     cl,
     m,
+    pool,
     cc_out,
     up_out,
     down_out,
@@ -178,7 +180,7 @@
     up_out[...] = side_by_side([stack[0, o, :, 0:KP] for o in range(OCT)])
     down_out[...] = side_by_side([stack[1, o, :, 0:KP] for o in range(OCT)])
     back_out[...] = side_by_side([stack[1, o].T[0:KP, :] for o in range(OCT)])
-    cc_out[...] = tightened(upward(up_out[...], wide, sums))
+    cc_out[...] = tightened(upward(up_out[...], wide, sums, pool))
 
     slot_ops(lops, padded, turned, lops_out)
     slot_ops(cops, padded, turned, cops_out)
@@ -201,7 +203,7 @@
     idxc[...] = jnp.where(spot < 0, -1, spot + start)
 
 
-def back_kernel(own, core, cross, other, mix, base, inside, back_ops, be_out, bf_out, scaled, gathered, sums):
+def back_kernel(own, core, cross, other, mix, base, inside, pool, back_ops, be_out, bf_out, scaled, gathered, sums):
     part = own.shape[0]
     me = lax.axis_index("chan")
     gathered[pl.ds(me * part, part), :] = own[...]
@@ -211,7 +213,7 @@
     potential = nn(mix[pl.ds(me * part, part), :], gathered[...]).astype(bf16)
     spread(base, potential, scaled)
     lay_wide(nt(scaled[...], inside[...]), be_out)
-    far = upward(back_ops[...], be_out, sums).astype(bf16)
+    far = upward(back_ops[...], be_out, sums, pool).astype(bf16)
     for at in range(far.shape[0] // KP):
         bf_out[:, at * 128 : (at + 1) * 128] = far[at * KP : (at + 1) * KP, :]
 
@@ -228,6 +230,7 @@
     idxc,
     lops,
     cops,
+    pool,
     near,
     far,
     g_out,
@@ -267,7 +270,7 @@
     src[mid:, leaf_dev:] = lower.astype(bf16)
     lay_wide(src[:, leaf_dev:].astype(f32), wide)
     srcc[:, 0:128] = cc[...]
-    srcc[:, 128:] = tightened(upward(up[...], wide, sums))
+    srcc[:, 128:] = tightened(upward(up[...], wide, sums, pool))
     place_of = lax.broadcasted_iota(jnp.int32, (window, 128), 0)
 
     def chosen(ref, group, at):
@@ -280,19 +283,19 @@
             at = 2 * pair
             both = jnp.concatenate([chosen(ref, group, at), chosen(ref, group, at + 1)], axis=1)
             for begin in range(0, count, chunk):
-                picked = nn(source[begin * KM : (begin + chunk) * KM, :], both)
+                end = begin + chunk
+                end_row = end * KM if end < count else source.shape[0]
+                picked = nn(source[begin * KM : end_row, :], both)
                 for c in range(chunk):
                     rows = picked[c * KM : (c + 1) * KM]
                     lane = (begin + c) * 128
                     held[at * KM : (at + 2) * KM, lane : lane + 128] = jnp.concatenate(
                         [rows[:, 0:128], rows[:, 128:]], axis=0
                     ).astype(bf16)
-            picked = nn(source[count * KM :, :], both)
+            rows = picked[chunk * KM :]
             for i in range(2):
                 for c in range(count):
-                    last[at + i : at + i + 1, c * 128 : (c + 1) * 128] = picked[
-                        c : c + 1, i * 128 : (i + 1) * 128
-                    ]
+                    last[at + i : at + i + 1, c * 128 : (c + 1) * 128] = rows[c : c + 1, i * 128 : (i + 1) * 128]
         held[GROUP * KM :, :] = last[...].astype(bf16)
 
     def pick_group(group, held, last, held_c, last_c):
@@ -421,7 +424,12 @@
 
 def from_chan(block):
     count = lax.axis_size("chan")
-    return [lax.ppermute(block, "chan", [(i, i ^ d) for i in range(count)]) for d in range(1, count)]
+
+    def swap(part, d):
+        return lax.ppermute(part, "chan", [(i, i ^ d) for i in range(count)])
+
+    cross = swap(block, 2)
+    return [swap(block, 1), cross, swap(cross, 1)]
 
 
 def local(
@@ -454,7 +462,7 @@
         leaf_lists,
         coarse_lists.T,
     )
-    m, first, second, base, inside, charges_near, *held = call(
+    m, first, second, base, inside, pool, charges_near, *held = call(
         moments_kernel,
         (
             shape((rows, leaf_dev), bf16),
@@ -462,6 +470,7 @@
             shape((rows // 2, leaf_dev), bf16),
             shape((KP, atoms), f32),
             shape((leaf_dev, atoms), bf16),
+            shape((OCT * 128, 128), bf16),
             shape(charges.shape, bf16),
             *[shape(a.shape, a.dtype) for a in held],
         ),
@@ -495,7 +504,8 @@
             pltpu.VMEM((KP, slots, KP), f32),
             pltpu.VMEM((128, OCT * 128), bf16),
         ],
-    )(*prepared, m)
+        flops=2 * 10**9,
+    )(*prepared, m, pool)
     be, bf = call(
         back_kernel,
         (shape((KP, wide), bf16), shape((KP, wide // OCT), bf16)),
@@ -504,7 +514,7 @@
             pltpu.VMEM((mix.shape[0], atoms), bf16),
             pltpu.VMEM((128, OCT * 128), bf16),
         ],
-    )(own, *cot, mix_near, base, inside, back_ops)
+    )(own, *cot, mix_near, base, inside, pool, back_ops)
 
     flat_rows = -(-(-(-kcount // FOUR) * FOUR * kcount) // 256) * 256
     fits = flat_rows % (8 * devices) == 0
@@ -528,7 +538,7 @@
             pltpu.VMEM((2 * steps, KP, GROUP * KP), f32),
             pltpu.VMEM((flat_rows, 128), f32),
         ],
-    )(m, first, second, cc, be, bf, up, idx, idxc, lops, cops)
+    )(m, first, second, cc, be, bf, up, idx, idxc, lops, cops, pool)
     potential, order = call(
         potential_kernel,
         (shape((part, atoms), bf16), shape((FOUR * 128, FOUR * 128), bf16)),

time: 58.8 us -> 55.7 us (0.947)
  Pallas kernels: 26.5 us -> 25 us
  waiting for transfers between devices: 7.78 us -> 6.88 us
  starting transfers between devices: 16.1 us -> 15.5 us
    ppermute x1, starting transfers between devices: 5.79 us -> 4.34 us  [local(): second = lax.ppermute(second, 'cells', outer + [(b, a) for a, b in outer])]
    pallas_call x1, Pallas kernels: 14.6 us -> 13.3 us  [local(): call(functools.partial(grads_kernel, kcount=kcount), (shape((KP, wide), f...]
    ppermute x3, waiting for transfers between devices: 0.91 us -> 0.01 us  [swap(): return lax.ppermute(part, 'chan', [(i, i ^ d) for i in range(count)])]
    ppermute x3, starting transfers between devices: 2.14 us -> 3.04 us  [swap(): return lax.ppermute(part, 'chan', [(i, i ^ d) for i in range(count)])]
  transfers between devices with their start and end apart: 7 -> 7, of which waited for: 3 -> 2; matrix products, arithmetic and copies ran while one was open for 0% -> 0% of each run, Pallas kernels for 14% -> 18%
where the time goes in v4:
time: 55.7 us; the launch traced here: 55.3 us
  Pallas kernels  25 us (45%)
  starting transfers between devices  15.5 us (28%)
  blocking collectives  7.21 us (13%)
  waiting for transfers between devices  6.88 us (12%)
  between operations  0.72 us (1%)
    pallas_call x1, Pallas kernels, local(): call(functools.partial(grads_kernel, kcount=kcount), (shape((KP, wide), f...  13.3 us
    all_gather x1, blocking collectives, local(): lax.all_gather(potential, 'chan', axis=0, tiled=True)  7.21 us
    all_to_all x1, waiting for transfers between devices, local(): parts = lax.all_to_all(grads, axes, 0, 0)  6.08 us
    all_to_all x1, starting transfers between devices, local(): parts = lax.all_to_all(grads, axes, 0, 0)  4.72 us
    ppermute x1, starting transfers between devices, local(): second = lax.ppermute(second, 'cells', outer + [(b, a) for a, b in outer])  4.34 us
    ppermute x3, starting transfers between devices, swap(): return lax.ppermute(part, 'chan', [(i, i ^ d) for i in range(count)])  3.04 us
    pallas_call x1, Pallas kernels, local(): call(prepare_kernel, (shape((coarse_rows, 128), bf16), wide_ops, wide_ops...  2.73 us
    all_to_all x1, starting transfers between devices, local(): whole = lax.all_to_all(spread_out, axes, 0, 0)  2.71 us
  transfers between devices with their start and end apart: 7, of which 2 were waited for; matrix products, arithmetic and copies ran while one was open for 0% of the time, Pallas kernels for 18%

profile of v4, /device:TPU:0, one launch (start us, length us, event | category | flops | bytes accessed | tf_op | source)
XLA Modules:
  0.0 55.3 jit_solution(13969262219162873385)
XLA Ops:
  0.6 3.0 %collective-permute-start.3 = (bf16[32,1024]{1,0:T(8,128)(2,1)}, bf16[32,1024]{1,0:T(8,128)(2,1)S(1)}, u32[]{:S(2)}, u32[]{:S(2)}) collective-permute-start(bf16[32,1024]{1,0:T(8,128)(2,1)} %rest_0_.1), channel_id=1, source_target_pairs={{0,2},{1,3},{2,0},{3,1},{4,6},{5,7},{6,4},{7,5},{8,10},{9,11},{10,... | collective-permute-start | bytes 196616 | tf_op jit(solution)/shard_map/ppermute | solution.py:429
  3.7 0.0 collective-permute-start.2
  3.7 1.7 %shard_map.130 = (bf16[800,128]{1,0:T(8,128)(2,1)S(1)}, bf16[400,128]{1,0:T(8,128)(2,1)S(1)}, bf16[400,128]{1,0:T(8,128)(2,1)S(1)}, f32[32,1024]{1,0:T(8,128)S(1...) custom-call(bf16[32,1024]{1,0:T(8,128)(2,1)} %charges_hbm.1, ...), custom_call_target="tpu_custom_call" | custom-call | flops 100000000 | bytes 1000000 | tf_op jit(solution)/shard_map/pallas_call | solution.py:465
  5.4 0.7 %collective-permute-start = (bf16[400,128]{1,0:T(8,128)(2,1)S(1)}, bf16[400,128]{1,0:T(8,128)(2,1)S(1)}, u32[]{:S(2)}, u32[]{:S(2)}) collective-permute-start(bf16[400,128]{1,0:T(8,128)(2,1)S(1)} %get-tuple-element.36), channel_id=1, source_target_pairs={{4,8},{12,16},{20,24},{8,4},{16,12},{24,20},{5,9},{13,17},{21,25},... | collective-permute-start | bytes 307208 | tf_op jit(solution)/shard_map/ppermute | solution.py:482
  6.1 4.3 %collective-permute-start.1 = (bf16[400,128]{1,0:T(8,128)(2,1)S(1)}, bf16[400,128]{1,0:T(8,128)(2,1)S(1)}, u32[]{:S(2)}, u32[]{:S(2)}) collective-permute-start(bf16[400,128]{1,0:T(8,128)(2,1)S(1)} %get-tuple-element.37), channel_id=1, source_target_pairs={{0,4},{8,12},{16,20},{24,28},{4,0},{12,8},{20,16},{28,24},{1,5},{9... | collective-permute-start | bytes 307208 | tf_op jit(solution)/shard_map/ppermute | solution.py:483
  10.4 0.0 collective-permute-done.3.cross
  10.4 0.0 collective-permute-start.4
  10.5 2.7 %shard_map.131 = (bf16[100,128]{1,0:T(8,128)(2,1)S(1)}, bf16[32,256]{1,0:T(8,128)(2,1)S(1)}, bf16[32,256]{1,0:T(8,128)(2,1)S(1)}, bf16[32,256]{1,0:T(8,128)(2,1)...) custom-call(bf16[25,8,25]{2,1,0:T(8,128)(2,1)S(1)} %get-tuple-elemen, ...), custom_call_target="tpu_custom_call" | custom-call | flops 2000000000 | bytes 1000000 | tf_op jit(solution)/shard_map/pallas_call | solution.py:488
  13.2 0.0 collective-permute-done.2.core
  13.2 0.0 collective-permute-done.4.other
  13.2 1.9 %shard_map.132 = (bf16[32,4096]{1,0:T(8,128)(2,1)S(1)}, bf16[32,512]{1,0:T(8,128)(2,1)S(1)}) custom-call(bf16[32,1024]{1,0:T(8,128)(2,1)S(1)} %get-tuple-element.46.own, bf16[32,1024]{1,0:T(8,128)(2,1)S(1)} %collective-permute-done.2.core, bf16[32,1024]{1,0:T(8,128)(2,1)S(1)} %collective-permute-done.3.cross, ...), custom_call_target="tpu_custom_call" | custom-call | flops 100000000 | bytes 1000000 | tf_op jit(solution)/shard_map/pallas_call | solution.py:509
  15.1 0.0 collective-permute-done.first
  15.1 0.0 collective-permute-done.1.second
  15.1 13.3 %shard_map.133 = (f32[32,4096]{1,0:T(8,128)S(1)}, f32[32,512]{1,0:T(8,128)S(1)}, bf16[32,24,128]{2,1,0:T(8,128)(2,1)}) custom-call(bf16[800,128]{1,0:T(8,128)(2,1)S(1)} %get-tuple-element.35.m, bf16[400,128]{1,0:T(8,128)(2,1)S(1)} %collective-permute-done.first, bf16[400,128]{1,0:T(8,128)(2,1)S(1)} %collective-permute-done.1.second, ...), custom_call_target="tpu_custom_call" | custom-call | flops 100000000 | bytes 1000000 | tf_op jit(solution)/shard_map/pallas_call | solution.py:522
  28.4 4.7 %all-to-all-start = ((bf16[32,24,128]{2,1,0:T(8,128)(2,1)}), bf16[32,24,128]{2,1,0:T(8,128)(2,1)S(1)}, u32[]{:S(2)}, u32[]{:S(2)}) async-start(bf16[32,24,128]{2,1,0:T(8,128)(2,1)} %get-tuple-element.63), calls=%async_computation | async-start | bytes 393216 | tf_op jit(solution)/shard_map/all_to_all | solution.py:550
  33.1 2.6 %shard_map.134 = (bf16[32,1024]{1,0:T(8,128)(2,1)S(1)}, bf16[512,512]{1,0:T(8,128)(2,1)S(1)}) custom-call(f32[32,4096]{1,0:T(8,128)S(1)} %get-tuple-element.58.near, f32[32,512]{1,0:T(8,128)S(1)} %get-tuple-element.59.far, bf16[32,256]{1,0:T(8,128)(2,1)S(1)} %get-tuple-element.60.down, f32[32,1024]{1,0:T(8,128)S(1)} %get-tuple-element.48.base, ...), custom_call_target="tpu_custom_call" | custom-call | flops 100000000 | bytes 1000000 | tf_op jit(solution)/shard_map/pallas_call | solution.py:542
  35.7 6.1 %all-to-all-done.parts = bf16[32,24,128]{2,1,0:T(8,128)(2,1)S(1)} async-done(((bf16[32,24,128]{2,1,0:T(8,128)(2,1)}), bf16[32,24,128]{2,1,0:T(8,128)(2,1)S(1)}, u32[]{:S(2)}, u32[]{:S(2)}) %all-to-all-start) | async-done | bytes 196640 | tf_op jit(solution)/shard_map/all_to_all | solution.py:550
  41.8 0.9 %shard_map.136 = bf16[32,24,128]{2,1,0:T(8,128)(2,1)} custom-call(bf16[32,24,128]{2,1,0:T(8,128)(2,1)S(1)} %all-to-all-done.parts, bf16[32,1024]{1,0:T(8,128)(2,1)S(1)} %get-tuple-element.61.after, bf16[512,512]{1,0:T(8,128)(2,1)S(1)} %get-tuple-element.64.order), custom_call_target="tpu_custom_call" | custom-call | flops 100000000 | bytes 1000000 | tf_op jit(solution)/shard_map/pallas_call | solution.py:551
  42.7 2.7 %all-to-all-start.1 = ((bf16[32,24,128]{2,1,0:T(8,128)(2,1)}), bf16[32,24,128]{2,1,0:T(8,128)(2,1)S(1)}, u32[]{:S(2)}, u32[]{:S(2)}) async-start(bf16[32,24,128]{2,1,0:T(8,128)(2,1)} %shard_map.136), calls=%async_computation.1 | async-start | bytes 393216 | tf_op jit(solution)/shard_map/all_to_all | solution.py:557
  45.4 7.2 %all_gather.3.whole = bf16[128,1024]{1,0:T(8,128)(2,1)S(1)} all-gather(bf16[32,1024]{1,0:T(8,128)(2,1)S(1)} %get-tuple-element.61.after), channel_id=1, replica_groups=mesh['cells'=8,'chan'=4] {'chan'}, dimensions={0}, use_global_device_ids=true | all-gather | bytes 327680 | tf_op jit(solution)/shard_map/all_gather | solution.py:575
  52.6 0.9 %shard_map.135 = bf16[32,1024]{1,0:T(8,128)(2,1)} custom-call(bf16[128,1024]{1,0:T(8,128)(2,1)S(1)} %all_gather.3.whole, bf16[128,128]{1,0:T(8,128)(2,1)S(1)} %get-tuple-element.47.mix, bf16[32,1024]{1,0:T(8,128)(2,1)S(1)} %get-tuple-element.62.charges), custom_call_target="tpu_custom_call" | custom-call | flops 100000000 | bytes 1000000 | tf_op jit(solution)/shard_map/pallas_call | solution.py:571
  53.5 0.8 %all-to-all-done.1.whole = bf16[32,24,128]{2,1,0:T(8,128)(2,1)S(1)} async-done(((bf16[32,24,128]{2,1,0:T(8,128)(2,1)}), bf16[32,24,128]{2,1,0:T(8,128)(2,1)S(1)}, u32[]{:S(2)}, u32[]{:S(2)}) %all-to-all-start.1) | async-done | bytes 196640 | tf_op jit(solution)/shard_map/all_to_all | solution.py:557
  54.3 0.9 %shard_map.137 = (f32[25,25,64]{2,1,0:T(8,128)}, f32[25,25,64]{2,1,0:T(8,128)}) custom-call(bf16[32,24,128]{2,1,0:T(8,128)(2,1)S(1)} %all-to-all-done.1.whole), custom_call_target="tpu_custom_call" | custom-call | flops 100000000 | bytes 1000000 | tf_op jit(solution)/shard_map/pallas_call | solution.py:567
Async XLA Ops:
  0.6 9.8 %collective-permute-start.3 = (bf16[32,1024]{1,0:T(8,128)(2,1)}, bf16[32,1024]{1,0:T(8,128)(2,1)S(1)}, u32[]{:S(2)}, u32[]{:S(2)}) collective-permute-start(bf16[32,1024]{1,0:T(8,128)(2,1)} %rest_0_.1), channel_id=1, source_target_pairs={{0,2},{1,3},{2,0},{3,1},{4,6},{5,7},{6,4},{7,5},{8,10},{9,11},{10,... | collective-permute-start | bytes 196616 | tf_op jit(solution)/shard_map/ppermute | solution.py:429
  3.7 9.5 %collective-permute-start.2 = (bf16[32,1024]{1,0:T(8,128)(2,1)}, bf16[32,1024]{1,0:T(8,128)(2,1)S(1)}, u32[]{:S(2)}, u32[]{:S(2)}) collective-permute-start(bf16[32,1024]{1,0:T(8,128)(2,1)} %rest_0_.1), channel_id=1, source_target_pairs={{0,1},{1,0},{2,3},{3,2},{4,5},{5,4},{6,7},{7,6},{8,9},{9,8},{10,11... | collective-permute-start | bytes 196616 | tf_op jit(solution)/shard_map/ppermute | solution.py:429
  5.4 9.7 %collective-permute-start = (bf16[400,128]{1,0:T(8,128)(2,1)S(1)}, bf16[400,128]{1,0:T(8,128)(2,1)S(1)}, u32[]{:S(2)}, u32[]{:S(2)}) collective-permute-start(bf16[400,128]{1,0:T(8,128)(2,1)S(1)} %get-tuple-element.36), channel_id=1, source_target_pairs={{4,8},{12,16},{20,24},{8,4},{16,12},{24,20},{5,9},{13,17},{21,25},... | collective-permute-start | bytes 307208 | tf_op jit(solution)/shard_map/ppermute | solution.py:482
  6.1 9.0 %collective-permute-start.1 = (bf16[400,128]{1,0:T(8,128)(2,1)S(1)}, bf16[400,128]{1,0:T(8,128)(2,1)S(1)}, u32[]{:S(2)}, u32[]{:S(2)}) collective-permute-start(bf16[400,128]{1,0:T(8,128)(2,1)S(1)} %get-tuple-element.37), channel_id=1, source_target_pairs={{0,4},{8,12},{16,20},{24,28},{4,0},{12,8},{20,16},{28,24},{1,5},{9... | collective-permute-start | bytes 307208 | tf_op jit(solution)/shard_map/ppermute | solution.py:483
  10.4 2.7 %collective-permute-start.4 = (bf16[32,1024]{1,0:T(8,128)(2,1)S(1)}, bf16[32,1024]{1,0:T(8,128)(2,1)S(1)}, u32[]{:S(2)}, u32[]{:S(2)}) collective-permute-start(bf16[32,1024]{1,0:T(8,128)(2,1)S(1)} %collective-permute-done.3.cross), channel_id=1, source_target_pairs={{0,1},{1,0},{2,3},{3,2},{4,5},{5,4},{6,7},{7,6},{8,9},{9,8},{10,11... | collective-permute-start | bytes 196616 | tf_op jit(solution)/shard_map/ppermute | solution.py:429
  28.4 13.4 %all-to-all-start = ((bf16[32,24,128]{2,1,0:T(8,128)(2,1)}), bf16[32,24,128]{2,1,0:T(8,128)(2,1)S(1)}, u32[]{:S(2)}, u32[]{:S(2)}) async-start(bf16[32,24,128]{2,1,0:T(8,128)(2,1)} %get-tuple-element.63), calls=%async_computation | async-start | bytes 393216 | tf_op jit(solution)/shard_map/all_to_all | solution.py:550
  42.7 11.6 %all-to-all-start.1 = ((bf16[32,24,128]{2,1,0:T(8,128)(2,1)}), bf16[32,24,128]{2,1,0:T(8,128)(2,1)S(1)}, u32[]{:S(2)}, u32[]{:S(2)}) async-start(bf16[32,24,128]{2,1,0:T(8,128)(2,1)} %shard_map.136), calls=%async_computation.1 | async-start | bytes 393216 | tf_op jit(solution)/shard_map/all_to_all | solution.py:557

commit v5 on v4

--- a/solution.py
+++ b/solution.py
@@ -10,7 +10,7 @@
 KP = 32
 GROUP = 8
 KM = 24
-CHUNK = 8
+CHUNK = 16
 FOUR = 4
 OCT = 8
 MORE = 8
@@ -268,14 +268,11 @@
     lower = jnp.where(low_lane, pltpu.roll(low, half, 1), high)
     src[0:mid, leaf_dev:] = upper.astype(bf16)
     src[mid:, leaf_dev:] = lower.astype(bf16)
-    lay_wide(src[:, leaf_dev:].astype(f32), wide)
-    srcc[:, 0:128] = cc[...]
-    srcc[:, 128:] = tightened(upward(up[...], wide, sums, pool))
-    place_of = lax.broadcasted_iota(jnp.int32, (window, 128), 0)
+    place_of = lax.broadcasted_iota(jnp.int32, (window, 128), 0).astype(f32).astype(bf16)
 
     def chosen(ref, group, at):
-        row = ref[pl.ds(slot_of(group, at), 1), :]
-        return jnp.where(place_of == row, 1.0, 0.0).astype(bf16)
+        row = ref[pl.ds(slot_of(group, at), 1), :].astype(f32).astype(bf16)
+        return jnp.where(place_of == row, jnp.ones((), bf16), jnp.zeros((), bf16))
 
     def picks(source, ref, group, held, last, chunk):
         count = source.shape[0] // kcount
@@ -298,33 +295,47 @@
                     last[at + i : at + i + 1, c * 128 : (c + 1) * 128] = rows[c : c + 1, i * 128 : (i + 1) * 128]
         held[GROUP * KM :, :] = last[...].astype(bf16)
 
+    def pick_leaves(group, held, last):
+        picks(src, idx, group, held, last, CHUNK)
+
+    def pick_parents(group, held_c, last_c):
+        picks(srcc, idxc, group, held_c, last_c, srcc.shape[0] // kcount)
+
     def pick_group(group, held, last, held_c, last_c):
-        picks(src, idx, group, held, last, CHUNK)
-        picks(srcc, idxc, group, held_c, last_c, srcc.shape[0] // kcount)
-
-    def products(group, held, held_c):
+        pick_leaves(group, held, last)
+        pick_parents(group, held_c, last_c)
+
+    def gradients(group, held, held_c):
         blocks[group, :, 0:tight] = nt(be[...], held[...])
         blocks[steps + group, :, 0:tight] = nt(bf[...], held_c[...])
+
+    def fields(group, held, held_c):
         near[...] += nn(lops[group][:, 0:tight], held[...])
         far[...] += nn(cops[group][:, 0:tight], held_c[...])
 
     for ref in (near, far, even_last, odd_last, even_c_last, odd_c_last):
         ref[...] = jnp.zeros_like(ref)
     evens, odds = (even, even_last, even_c, even_c_last), (odd, odd_last, odd_c, odd_c_last)
-    pick_group(0, *evens)
+    pick_leaves(0, even, even_last)
+    lay_wide(jnp.concatenate([upper, lower], axis=0), wide)
+    srcc[:, 0:128] = cc[...]
+    srcc[:, 128:] = tightened(upward(up[...], wide, sums, pool))
+    pick_parents(0, even_c, even_c_last)
 
     def two_groups(i, carry):
         group = 2 * i + 1
+        gradients(group - 1, even, even_c)
         pick_group(group, *odds)
-        products(group - 1, even, even_c)
+        fields(group - 1, even, even_c)
+        gradients(group, odd, odd_c)
         pick_group(group + 1, *evens)
-        products(group, odd, odd_c)
+        fields(group, odd, odd_c)
         return carry
 
     lax.fori_loop(0, steps // 2 - 1, two_groups, 0)
     pick_group(steps - 1, *odds)
-    products(steps - 2, even, even_c)
-    products(steps - 1, odd, odd_c)
+    gradients(steps - 2, even, even_c)
+    gradients(steps - 1, odd, odd_c)
     flat[...] = jnp.zeros_like(flat)
     main = GROUP * KM
     for turn in range(-(-kcount // FOUR)):
@@ -336,6 +347,8 @@
             rest = jnp.concatenate([across[main + a : main + a + 1] for a in (at, at + 1)], axis=1)
             rows = pl.ds(turn * FOUR * kcount + tile, kcount, stride=FOUR)
             flat[rows, :] = jnp.concatenate([body, rest], axis=0)
+    fields(steps - 2, even, even_c)
+    fields(steps - 1, odd, odd_c)
     if len(g_out.shape) == 2:
         g_out[...] = flat[...].astype(bf16)
     else:
@@ -451,7 +464,6 @@
     stay = lambda *arrays: [pltpu.with_memory_space_constraint(a, pltpu.HBM) for a in arrays]
     wide = part * leaf_dev
 
-    cot = from_chan(cotangent)
     held = (
         cotangent,
         mix,
@@ -482,6 +494,7 @@
     first = lax.ppermute(first, "cells", inner + [(b, a) for a, b in inner])
     second = lax.ppermute(second, "cells", outer + [(b, a) for a, b in outer])
     own, mix_near, *prepared = held
+    cot = from_chan(own)
 
     wide_ops = shape((KP, OCT * KP), bf16)
     group_ops = shape((steps, KP, GROUP * KP), bf16)
@@ -504,7 +517,7 @@
             pltpu.VMEM((KP, slots, KP), f32),
             pltpu.VMEM((128, OCT * 128), bf16),
         ],
-        flops=2 * 10**9,
+        flops=10**8,
     )(*prepared, m, pool)
     be, bf = call(
         back_kernel,

time: 55.7 us -> 54.7 us (0.982)
  Pallas kernels: 25 us -> 24.3 us
    all_to_all x1, starting transfers between devices: 4.72 us -> 3.95 us  [local(): parts = lax.all_to_all(grads, axes, 0, 0)]
    pallas_call x1, Pallas kernels: 13.3 us -> 12.5 us  [local(): call(functools.partial(grads_kernel, kcount=kcount), (shape((KP, wide), f...]
  transfers between devices with their start and end apart: 7 -> 7, of which waited for: 2 -> 2; matrix products, arithmetic and copies ran while one was open for 0% -> 0% of each run, Pallas kernels for 18% -> 15%
where the time goes in v5:
time: 54.7 us; the launch traced here: 54.3 us
  Pallas kernels  24.3 us (44%)
  starting transfers between devices  15.2 us (28%)
  blocking collectives  7.21 us (13%)
  waiting for transfers between devices  6.88 us (13%)
  between operations  0.72 us (1%)
    pallas_call x1, Pallas kernels, local(): call(functools.partial(grads_kernel, kcount=kcount), (shape((KP, wide), f...  12.5 us
    all_gather x1, blocking collectives, local(): lax.all_gather(potential, 'chan', axis=0, tiled=True)  7.21 us
    all_to_all x1, waiting for transfers between devices, local(): parts = lax.all_to_all(grads, axes, 0, 0)  6.08 us
    ppermute x1, starting transfers between devices, local(): second = lax.ppermute(second, 'cells', outer + [(b, a) for a, b in outer])  4.34 us
    all_to_all x1, starting transfers between devices, local(): parts = lax.all_to_all(grads, axes, 0, 0)  3.95 us
    ppermute x3, starting transfers between devices, swap(): return lax.ppermute(part, 'chan', [(i, i ^ d) for i in range(count)])  3.54 us
    pallas_call x1, Pallas kernels, local(): call(prepare_kernel, (shape((coarse_rows, 128), bf16), wide_ops, wide_ops...  2.74 us
    all_to_all x1, starting transfers between devices, local(): whole = lax.all_to_all(spread_out, axes, 0, 0)  2.71 us
  transfers between devices with their start and end apart: 7, of which 2 were waited for; matrix products, arithmetic and copies ran while one was open for 0% of the time, Pallas kernels for 15%

profile of v5, /device:TPU:0, one launch (start us, length us, event | category | flops | bytes accessed | tf_op | source)
XLA Modules:
  0.0 54.3 jit_solution(5320957267499636244)
XLA Ops:
  0.6 1.8 %shard_map.130 = (bf16[800,128]{1,0:T(8,128)(2,1)S(1)}, bf16[400,128]{1,0:T(8,128)(2,1)S(1)}, bf16[400,128]{1,0:T(8,128)(2,1)S(1)}, f32[32,1024]{1,0:T(8,128)S(1...) custom-call(bf16[32,1024]{1,0:T(8,128)(2,1)} %charges_hbm.1, ...), custom_call_target="tpu_custom_call" | custom-call | flops 100000000 | bytes 1000000 | tf_op jit(solution)/shard_map/pallas_call | solution.py:477
  2.4 3.0 %collective-permute-start.3 = (bf16[32,1024]{1,0:T(8,128)(2,1)S(1)}, bf16[32,1024]{1,0:T(8,128)(2,1)S(1)}, u32[]{:S(2)}, u32[]{:S(2)}) collective-permute-start(bf16[32,1024]{1,0:T(8,128)(2,1)S(1)} %get-tuple-element.46.own), channel_id=1, source_target_pairs={{0,2},{1,3},{2,0},{3,1},{4,6},{5,7},{6,4},{7,5},{8,10},{9,11},{10,... | collective-permute-start | bytes 196616 | tf_op jit(solution)/shard_map/ppermute | solution.py:442
  5.4 0.7 %collective-permute-start = (bf16[400,128]{1,0:T(8,128)(2,1)S(1)}, bf16[400,128]{1,0:T(8,128)(2,1)S(1)}, u32[]{:S(2)}, u32[]{:S(2)}) collective-permute-start(bf16[400,128]{1,0:T(8,128)(2,1)S(1)} %get-tuple-element.36), channel_id=1, source_target_pairs={{4,8},{12,16},{20,24},{8,4},{16,12},{24,20},{5,9},{13,17},{21,25},... | collective-permute-start | bytes 307208 | tf_op jit(solution)/shard_map/ppermute | solution.py:494
  6.1 4.3 %collective-permute-start.1 = (bf16[400,128]{1,0:T(8,128)(2,1)S(1)}, bf16[400,128]{1,0:T(8,128)(2,1)S(1)}, u32[]{:S(2)}, u32[]{:S(2)}) collective-permute-start(bf16[400,128]{1,0:T(8,128)(2,1)S(1)} %get-tuple-element.37), channel_id=1, source_target_pairs={{0,4},{8,12},{16,20},{24,28},{4,0},{12,8},{20,16},{28,24},{1,5},{9... | collective-permute-start | bytes 307208 | tf_op jit(solution)/shard_map/ppermute | solution.py:495
  10.4 0.0 collective-permute-start.2
  10.4 0.0 collective-permute-done.3.cross
  10.4 0.5 collective-permute-start.4
  10.9 2.7 %shard_map.131 = (bf16[100,128]{1,0:T(8,128)(2,1)S(1)}, bf16[32,256]{1,0:T(8,128)(2,1)S(1)}, bf16[32,256]{1,0:T(8,128)(2,1)S(1)}, bf16[32,256]{1,0:T(8,128)(2,1)...) custom-call(bf16[25,8,25]{2,1,0:T(8,128)(2,1)S(1)} %get-tuple-elemen, ...), custom_call_target="tpu_custom_call" | custom-call | flops 100000000 | bytes 1000000 | tf_op jit(solution)/shard_map/pallas_call | solution.py:501
  13.7 0.0 collective-permute-done.2.core
  13.7 0.0 collective-permute-done.4.other
  13.7 1.9 %shard_map.132 = (bf16[32,4096]{1,0:T(8,128)(2,1)S(1)}, bf16[32,512]{1,0:T(8,128)(2,1)S(1)}) custom-call(bf16[32,1024]{1,0:T(8,128)(2,1)S(1)} %get-tuple-element.46.own, bf16[32,1024]{1,0:T(8,128)(2,1)S(1)} %collective-permute-done.2.core, bf16[32,1024]{1,0:T(8,128)(2,1)S(1)} %collective-permute-done.3.cross, ...), custom_call_target="tpu_custom_call" | custom-call | flops 100000000 | bytes 1000000 | tf_op jit(solution)/shard_map/pallas_call | solution.py:522
  15.6 0.0 collective-permute-done.first
  15.6 0.0 collective-permute-done.1.second
  15.6 12.5 %shard_map.133 = (f32[32,4096]{1,0:T(8,128)S(1)}, f32[32,512]{1,0:T(8,128)S(1)}, bf16[32,24,128]{2,1,0:T(8,128)(2,1)}) custom-call(bf16[800,128]{1,0:T(8,128)(2,1)S(1)} %get-tuple-element.35.m, bf16[400,128]{1,0:T(8,128)(2,1)S(1)} %collective-permute-done.first, bf16[400,128]{1,0:T(8,128)(2,1)S(1)} %collective-permute-done.1.second, ...), custom_call_target="tpu_custom_call" | custom-call | flops 100000000 | bytes 1000000 | tf_op jit(solution)/shard_map/pallas_call | solution.py:535
  28.1 3.9 %all-to-all-start = ((bf16[32,24,128]{2,1,0:T(8,128)(2,1)}), bf16[32,24,128]{2,1,0:T(8,128)(2,1)S(1)}, u32[]{:S(2)}, u32[]{:S(2)}) async-start(bf16[32,24,128]{2,1,0:T(8,128)(2,1)} %get-tuple-element.63), calls=%async_computation | async-start | bytes 393216 | tf_op jit(solution)/shard_map/all_to_all | solution.py:563
  32.1 2.6 %shard_map.134 = (bf16[32,1024]{1,0:T(8,128)(2,1)S(1)}, bf16[512,512]{1,0:T(8,128)(2,1)S(1)}) custom-call(f32[32,4096]{1,0:T(8,128)S(1)} %get-tuple-element.58.near, f32[32,512]{1,0:T(8,128)S(1)} %get-tuple-element.59.far, bf16[32,256]{1,0:T(8,128)(2,1)S(1)} %get-tuple-element.60.down, f32[32,1024]{1,0:T(8,128)S(1)} %get-tuple-element.48.base, ...), custom_call_target="tpu_custom_call" | custom-call | flops 100000000 | bytes 1000000 | tf_op jit(solution)/shard_map/pallas_call | solution.py:555
  34.7 6.1 %all-to-all-done.parts = bf16[32,24,128]{2,1,0:T(8,128)(2,1)S(1)} async-done(((bf16[32,24,128]{2,1,0:T(8,128)(2,1)}), bf16[32,24,128]{2,1,0:T(8,128)(2,1)S(1)}, u32[]{:S(2)}, u32[]{:S(2)}) %all-to-all-start) | async-done | bytes 196640 | tf_op jit(solution)/shard_map/all_to_all | solution.py:563
  40.8 0.9 %shard_map.136 = bf16[32,24,128]{2,1,0:T(8,128)(2,1)} custom-call(bf16[32,24,128]{2,1,0:T(8,128)(2,1)S(1)} %all-to-all-done.parts, bf16[32,1024]{1,0:T(8,128)(2,1)S(1)} %get-tuple-element.61.after, bf16[512,512]{1,0:T(8,128)(2,1)S(1)} %get-tuple-element.64.order), custom_call_target="tpu_custom_call" | custom-call | flops 100000000 | bytes 1000000 | tf_op jit(solution)/shard_map/pallas_call | solution.py:564
  41.7 2.7 %all-to-all-start.1 = ((bf16[32,24,128]{2,1,0:T(8,128)(2,1)}), bf16[32,24,128]{2,1,0:T(8,128)(2,1)S(1)}, u32[]{:S(2)}, u32[]{:S(2)}) async-start(bf16[32,24,128]{2,1,0:T(8,128)(2,1)} %shard_map.136), calls=%async_computation.1 | async-start | bytes 393216 | tf_op jit(solution)/shard_map/all_to_all | solution.py:570
  44.4 7.2 %all_gather.3.whole = bf16[128,1024]{1,0:T(8,128)(2,1)S(1)} all-gather(bf16[32,1024]{1,0:T(8,128)(2,1)S(1)} %get-tuple-element.61.after), channel_id=1, replica_groups=mesh['cells'=8,'chan'=4] {'chan'}, dimensions={0}, use_global_device_ids=true | all-gather | bytes 327680 | tf_op jit(solution)/shard_map/all_gather | solution.py:588
  51.6 0.9 %shard_map.135 = bf16[32,1024]{1,0:T(8,128)(2,1)} custom-call(bf16[128,1024]{1,0:T(8,128)(2,1)S(1)} %all_gather.3.whole, bf16[128,128]{1,0:T(8,128)(2,1)S(1)} %get-tuple-element.47.mix, bf16[32,1024]{1,0:T(8,128)(2,1)S(1)} %get-tuple-element.62.charges), custom_call_target="tpu_custom_call" | custom-call | flops 100000000 | bytes 1000000 | tf_op jit(solution)/shard_map/pallas_call | solution.py:584
  52.5 0.8 %all-to-all-done.1.whole = bf16[32,24,128]{2,1,0:T(8,128)(2,1)S(1)} async-done(((bf16[32,24,128]{2,1,0:T(8,128)(2,1)}), bf16[32,24,128]{2,1,0:T(8,128)(2,1)S(1)}, u32[]{:S(2)}, u32[]{:S(2)}) %all-to-all-start.1) | async-done | bytes 196640 | tf_op jit(solution)/shard_map/all_to_all | solution.py:570
  53.3 0.9 %shard_map.137 = (f32[25,25,64]{2,1,0:T(8,128)}, f32[25,25,64]{2,1,0:T(8,128)}) custom-call(bf16[32,24,128]{2,1,0:T(8,128)(2,1)S(1)} %all-to-all-done.1.whole), custom_call_target="tpu_custom_call" | custom-call | flops 100000000 | bytes 1000000 | tf_op jit(solution)/shard_map/pallas_call | solution.py:580
Async XLA Ops:
  2.4 8.0 %collective-permute-start.3 = (bf16[32,1024]{1,0:T(8,128)(2,1)S(1)}, bf16[32,1024]{1,0:T(8,128)(2,1)S(1)}, u32[]{:S(2)}, u32[]{:S(2)}) collective-permute-start(bf16[32,1024]{1,0:T(8,128)(2,1)S(1)} %get-tuple-element.46.own), channel_id=1, source_target_pairs={{0,2},{1,3},{2,0},{3,1},{4,6},{5,7},{6,4},{7,5},{8,10},{9,11},{10,... | collective-permute-start | bytes 196616 | tf_op jit(solution)/shard_map/ppermute | solution.py:442
  5.4 10.2 %collective-permute-start = (bf16[400,128]{1,0:T(8,128)(2,1)S(1)}, bf16[400,128]{1,0:T(8,128)(2,1)S(1)}, u32[]{:S(2)}, u32[]{:S(2)}) collective-permute-start(bf16[400,128]{1,0:T(8,128)(2,1)S(1)} %get-tuple-element.36), channel_id=1, source_target_pairs={{4,8},{12,16},{20,24},{8,4},{16,12},{24,20},{5,9},{13,17},{21,25},... | collective-permute-start | bytes 307208 | tf_op jit(solution)/shard_map/ppermute | solution.py:494
  6.1 9.5 %collective-permute-start.1 = (bf16[400,128]{1,0:T(8,128)(2,1)S(1)}, bf16[400,128]{1,0:T(8,128)(2,1)S(1)}, u32[]{:S(2)}, u32[]{:S(2)}) collective-permute-start(bf16[400,128]{1,0:T(8,128)(2,1)S(1)} %get-tuple-element.37), channel_id=1, source_target_pairs={{0,4},{8,12},{16,20},{24,28},{4,0},{12,8},{20,16},{28,24},{1,5},{9... | collective-permute-start | bytes 307208 | tf_op jit(solution)/shard_map/ppermute | solution.py:495
  10.4 3.3 %collective-permute-start.2 = (bf16[32,1024]{1,0:T(8,128)(2,1)S(1)}, bf16[32,1024]{1,0:T(8,128)(2,1)S(1)}, u32[]{:S(2)}, u32[]{:S(2)}) collective-permute-start(bf16[32,1024]{1,0:T(8,128)(2,1)S(1)} %get-tuple-element.46.own), channel_id=1, source_target_pairs={{0,1},{1,0},{2,3},{3,2},{4,5},{5,4},{6,7},{7,6},{8,9},{9,8},{10,11... | collective-permute-start | bytes 196616 | tf_op jit(solution)/shard_map/ppermute | solution.py:442
  10.4 3.3 %collective-permute-start.4 = (bf16[32,1024]{1,0:T(8,128)(2,1)S(1)}, bf16[32,1024]{1,0:T(8,128)(2,1)S(1)}, u32[]{:S(2)}, u32[]{:S(2)}) collective-permute-start(bf16[32,1024]{1,0:T(8,128)(2,1)S(1)} %collective-permute-done.3.cross), channel_id=1, source_target_pairs={{0,1},{1,0},{2,3},{3,2},{4,5},{5,4},{6,7},{7,6},{8,9},{9,8},{10,11... | collective-permute-start | bytes 196616 | tf_op jit(solution)/shard_map/ppermute | solution.py:442
  28.1 12.7 %all-to-all-start = ((bf16[32,24,128]{2,1,0:T(8,128)(2,1)}), bf16[32,24,128]{2,1,0:T(8,128)(2,1)S(1)}, u32[]{:S(2)}, u32[]{:S(2)}) async-start(bf16[32,24,128]{2,1,0:T(8,128)(2,1)} %get-tuple-element.63), calls=%async_computation | async-start | bytes 393216 | tf_op jit(solution)/shard_map/all_to_all | solution.py:563
  41.7 11.6 %all-to-all-start.1 = ((bf16[32,24,128]{2,1,0:T(8,128)(2,1)}), bf16[32,24,128]{2,1,0:T(8,128)(2,1)S(1)}, u32[]{:S(2)}, u32[]{:S(2)}) async-start(bf16[32,24,128]{2,1,0:T(8,128)(2,1)} %shard_map.136), calls=%async_computation.1 | async-start | bytes 393216 | tf_op jit(solution)/shard_map/all_to_all | solution.py:570

commit v6 on v5

--- a/solution.py
+++ b/solution.py
@@ -186,7 +186,8 @@
     slot_ops(cops, padded, turned, cops_out)
     rel = ll[...] - cell * leaf_dev
     place = jnp.where(rel < 0, rel + leaf_dev + half, jnp.where(rel < leaf_dev, rel, rel + half))
-    idx[...] = jnp.where(ll[...] < 0, -1, place)
+    idx[0:slots, :] = jnp.where(ll[...] < 0, -1, place)
+    idx[slots:, :] = jnp.full_like(idx[slots:, :], -1)
     crel = cl[...] - cell * coarse_dev
     side = coarse_dev // 2
     cplace = jnp.where(crel < 0, crel + 128 + side, jnp.where(crel < coarse_dev, crel, crel + 128 - side))
@@ -200,7 +201,8 @@
     spot = lax.dot_general(cplace, copied, (((0,), (0,)), ((), ())), preferred_element_type=f32)
     spot = spot.astype(jnp.int32)
     start = lax.broadcasted_iota(jnp.int32, (slots, 128), 1) // coarse_dev * coarse_dev
-    idxc[...] = jnp.where(spot < 0, -1, spot + start)
+    idxc[0:slots, :] = jnp.where(spot < 0, -1, spot + start)
+    idxc[slots:, :] = jnp.full_like(idxc[slots:, :], -1)
 
 
 def back_kernel(own, core, cross, other, mix, base, inside, pool, back_ops, be_out, bf_out, scaled, gathered, sums):
@@ -255,7 +257,7 @@
     half = leaf_dev // 2
     window = 2 * leaf_dev
     channels = m.shape[0] // kcount
-    steps = idx.shape[0] // GROUP
+    steps = lops.shape[0]
     tight = even.shape[0]
     is_odd = lax.rem(lax.axis_index("cells"), 2) == 1
 
@@ -392,14 +394,14 @@
     summed = parts[0].astype(f32)
     for d in range(1, parts.shape[0]):
         summed = summed + parts[d].astype(f32)
-    total[...] = summed
+    total[0 : summed.shape[0], :] = summed
     count = summed.shape[0] // FOUR
     tiles = [total[pl.ds(tile, count, stride=FOUR), :] for tile in range(FOUR)]
     turned = nn(jnp.concatenate(tiles, axis=1).astype(bf16), order[...])
     for k in range(FOUR):
         laid[pl.ds(k, count, stride=FOUR), :] = turned[:, k * 128 : (k + 1) * 128]
     for d in range(out.shape[0]):
-        out[d] = laid[...].astype(bf16)
+        out[d] = laid[0 : summed.shape[0], :].astype(bf16)
 
 
 def unpack_kernel(whole, leaf_out, coarse_out, flat):
@@ -507,8 +509,8 @@
             wide_ops,
             group_ops,
             group_ops,
-            shape((slots, 128), jnp.int32),
-            shape((slots, 128), jnp.int32),
+            shape((slots + 8, 128), jnp.int32),
+            shape((slots + 8, 128), jnp.int32),
         ),
         [
             pltpu.VMEM((KP, wide), bf16),
@@ -564,7 +566,7 @@
         spread_out = call(
             reduce_kernel,
             shape(laid, bf16),
-            [pltpu.VMEM(laid[1:], f32), pltpu.VMEM(laid[1:], f32)],
+            [pltpu.VMEM((laid[1] + 16, 128), f32), pltpu.VMEM((laid[1] + 16, 128), f32)],
             in_specs=[near_by, pl.BlockSpec(memory_space=pl.ANY), near_by],
         )(parts, potential, order)
         whole = lax.all_to_all(spread_out, axes, 0, 0)

time: 54.7 us -> 54.7 us (level)
  no operation moved by 1% of the time
where the time goes in v6:
time: 54.7 us; the launch traced here: 54.3 us
  Pallas kernels  24.3 us (44%)
  starting transfers between devices  15.2 us (28%)
  blocking collectives  7.21 us (13%)
  waiting for transfers between devices  6.87 us (13%)
  between operations  0.72 us (1%)
    pallas_call x1, Pallas kernels, local(): call(functools.partial(grads_kernel, kcount=kcount), (shape((KP, wide), f...  12.5 us
    all_gather x1, blocking collectives, local(): lax.all_gather(potential, 'chan', axis=0, tiled=True)  7.21 us
    all_to_all x1, waiting for transfers between devices, local(): parts = lax.all_to_all(grads, axes, 0, 0)  6.08 us
    ppermute x1, starting transfers between devices, local(): second = lax.ppermute(second, 'cells', outer + [(b, a) for a, b in outer])  4.34 us
    all_to_all x1, starting transfers between devices, local(): parts = lax.all_to_all(grads, axes, 0, 0)  3.96 us
    ppermute x3, starting transfers between devices, swap(): return lax.ppermute(part, 'chan', [(i, i ^ d) for i in range(count)])  3.54 us
    pallas_call x1, Pallas kernels, local(): call(prepare_kernel, (shape((coarse_rows, 128), bf16), wide_ops, wide_ops...  2.74 us
    all_to_all x1, starting transfers between devices, local(): whole = lax.all_to_all(spread_out, axes, 0, 0)  2.71 us
  transfers between devices with their start and end apart: 7, of which 2 were waited for; matrix products, arithmetic and copies ran while one was open for 0% of the time, Pallas kernels for 15%

profile of v6, /device:TPU:0, one launch (start us, length us, event | category | flops | bytes accessed | tf_op | source)
XLA Modules:
  0.0 54.3 jit_solution(11272289813555015076)
XLA Ops:
  0.6 1.8 %shard_map.130 = (bf16[800,128]{1,0:T(8,128)(2,1)S(1)}, bf16[400,128]{1,0:T(8,128)(2,1)S(1)}, bf16[400,128]{1,0:T(8,128)(2,1)S(1)}, f32[32,1024]{1,0:T(8,128)S(1...) custom-call(bf16[32,1024]{1,0:T(8,128)(2,1)} %charges_hbm.1, ...), custom_call_target="tpu_custom_call" | custom-call | flops 100000000 | bytes 1000000 | tf_op jit(solution)/shard_map/pallas_call | solution.py:479
  2.4 3.0 %collective-permute-start.3 = (bf16[32,1024]{1,0:T(8,128)(2,1)S(1)}, bf16[32,1024]{1,0:T(8,128)(2,1)S(1)}, u32[]{:S(2)}, u32[]{:S(2)}) collective-permute-start(bf16[32,1024]{1,0:T(8,128)(2,1)S(1)} %get-tuple-element.46.own), channel_id=1, source_target_pairs={{0,2},{1,3},{2,0},{3,1},{4,6},{5,7},{6,4},{7,5},{8,10},{9,11},{10,... | collective-permute-start | bytes 196616 | tf_op jit(solution)/shard_map/ppermute | solution.py:444
  5.4 0.7 %collective-permute-start = (bf16[400,128]{1,0:T(8,128)(2,1)S(1)}, bf16[400,128]{1,0:T(8,128)(2,1)S(1)}, u32[]{:S(2)}, u32[]{:S(2)}) collective-permute-start(bf16[400,128]{1,0:T(8,128)(2,1)S(1)} %get-tuple-element.36), channel_id=1, source_target_pairs={{4,8},{12,16},{20,24},{8,4},{16,12},{24,20},{5,9},{13,17},{21,25},... | collective-permute-start | bytes 307208 | tf_op jit(solution)/shard_map/ppermute | solution.py:496
  6.1 4.3 %collective-permute-start.1 = (bf16[400,128]{1,0:T(8,128)(2,1)S(1)}, bf16[400,128]{1,0:T(8,128)(2,1)S(1)}, u32[]{:S(2)}, u32[]{:S(2)}) collective-permute-start(bf16[400,128]{1,0:T(8,128)(2,1)S(1)} %get-tuple-element.37), channel_id=1, source_target_pairs={{0,4},{8,12},{16,20},{24,28},{4,0},{12,8},{20,16},{28,24},{1,5},{9... | collective-permute-start | bytes 307208 | tf_op jit(solution)/shard_map/ppermute | solution.py:497
  10.4 0.0 collective-permute-start.2
  10.4 0.0 collective-permute-done.3.cross
  10.4 0.5 collective-permute-start.4
  10.9 2.7 %shard_map.131 = (bf16[100,128]{1,0:T(8,128)(2,1)S(1)}, bf16[32,256]{1,0:T(8,128)(2,1)S(1)}, bf16[32,256]{1,0:T(8,128)(2,1)S(1)}, bf16[32,256]{1,0:T(8,128)(2,1)...) custom-call(bf16[25,8,25]{2,1,0:T(8,128)(2,1)S(1)} %get-tuple-elemen, ...), custom_call_target="tpu_custom_call" | custom-call | flops 100000000 | bytes 1000000 | tf_op jit(solution)/shard_map/pallas_call | solution.py:503
  13.7 0.0 collective-permute-done.2.core
  13.7 0.0 collective-permute-done.4.other
  13.7 1.9 %shard_map.132 = (bf16[32,4096]{1,0:T(8,128)(2,1)S(1)}, bf16[32,512]{1,0:T(8,128)(2,1)S(1)}) custom-call(bf16[32,1024]{1,0:T(8,128)(2,1)S(1)} %get-tuple-element.46.own, bf16[32,1024]{1,0:T(8,128)(2,1)S(1)} %collective-permute-done.2.core, bf16[32,1024]{1,0:T(8,128)(2,1)S(1)} %collective-permute-done.3.cross, ...), custom_call_target="tpu_custom_call" | custom-call | flops 100000000 | bytes 1000000 | tf_op jit(solution)/shard_map/pallas_call | solution.py:524
  15.6 0.0 collective-permute-done.first
  15.6 0.0 collective-permute-done.1.second
  15.6 12.5 %shard_map.133 = (f32[32,4096]{1,0:T(8,128)S(1)}, f32[32,512]{1,0:T(8,128)S(1)}, bf16[32,24,128]{2,1,0:T(8,128)(2,1)}) custom-call(bf16[800,128]{1,0:T(8,128)(2,1)S(1)} %get-tuple-element.35.m, bf16[400,128]{1,0:T(8,128)(2,1)S(1)} %collective-permute-done.first, bf16[400,128]{1,0:T(8,128)(2,1)S(1)} %collective-permute-done.1.second, ...), custom_call_target="tpu_custom_call" | custom-call | flops 100000000 | bytes 1000000 | tf_op jit(solution)/shard_map/pallas_call | solution.py:537
  28.1 4.0 %all-to-all-start = ((bf16[32,24,128]{2,1,0:T(8,128)(2,1)}), bf16[32,24,128]{2,1,0:T(8,128)(2,1)S(1)}, u32[]{:S(2)}, u32[]{:S(2)}) async-start(bf16[32,24,128]{2,1,0:T(8,128)(2,1)} %get-tuple-element.63), calls=%async_computation | async-start | bytes 393216 | tf_op jit(solution)/shard_map/all_to_all | solution.py:565
  32.1 2.6 %shard_map.134 = (bf16[32,1024]{1,0:T(8,128)(2,1)S(1)}, bf16[512,512]{1,0:T(8,128)(2,1)S(1)}) custom-call(f32[32,4096]{1,0:T(8,128)S(1)} %get-tuple-element.58.near, f32[32,512]{1,0:T(8,128)S(1)} %get-tuple-element.59.far, bf16[32,256]{1,0:T(8,128)(2,1)S(1)} %get-tuple-element.60.down, f32[32,1024]{1,0:T(8,128)S(1)} %get-tuple-element.48.base, ...), custom_call_target="tpu_custom_call" | custom-call | flops 100000000 | bytes 1000000 | tf_op jit(solution)/shard_map/pallas_call | solution.py:557
  34.7 6.1 %all-to-all-done.parts = bf16[32,24,128]{2,1,0:T(8,128)(2,1)S(1)} async-done(((bf16[32,24,128]{2,1,0:T(8,128)(2,1)}), bf16[32,24,128]{2,1,0:T(8,128)(2,1)S(1)}, u32[]{:S(2)}, u32[]{:S(2)}) %all-to-all-start) | async-done | bytes 196640 | tf_op jit(solution)/shard_map/all_to_all | solution.py:565
  40.8 0.9 %shard_map.136 = bf16[32,24,128]{2,1,0:T(8,128)(2,1)} custom-call(bf16[32,24,128]{2,1,0:T(8,128)(2,1)S(1)} %all-to-all-done.parts, bf16[32,1024]{1,0:T(8,128)(2,1)S(1)} %get-tuple-element.61.after, bf16[512,512]{1,0:T(8,128)(2,1)S(1)} %get-tuple-element.64.order), custom_call_target="tpu_custom_call" | custom-call | flops 100000000 | bytes 1000000 | tf_op jit(solution)/shard_map/pallas_call | solution.py:566
  41.7 2.7 %all-to-all-start.1 = ((bf16[32,24,128]{2,1,0:T(8,128)(2,1)}), bf16[32,24,128]{2,1,0:T(8,128)(2,1)S(1)}, u32[]{:S(2)}, u32[]{:S(2)}) async-start(bf16[32,24,128]{2,1,0:T(8,128)(2,1)} %shard_map.136), calls=%async_computation.1 | async-start | bytes 393216 | tf_op jit(solution)/shard_map/all_to_all | solution.py:572
  44.4 7.2 %all_gather.3.whole = bf16[128,1024]{1,0:T(8,128)(2,1)S(1)} all-gather(bf16[32,1024]{1,0:T(8,128)(2,1)S(1)} %get-tuple-element.61.after), channel_id=1, replica_groups=mesh['cells'=8,'chan'=4] {'chan'}, dimensions={0}, use_global_device_ids=true | all-gather | bytes 327680 | tf_op jit(solution)/shard_map/all_gather | solution.py:590
  51.7 0.9 %shard_map.135 = bf16[32,1024]{1,0:T(8,128)(2,1)} custom-call(bf16[128,1024]{1,0:T(8,128)(2,1)S(1)} %all_gather.3.whole, bf16[128,128]{1,0:T(8,128)(2,1)S(1)} %get-tuple-element.47.mix, bf16[32,1024]{1,0:T(8,128)(2,1)S(1)} %get-tuple-element.62.charges), custom_call_target="tpu_custom_call" | custom-call | flops 100000000 | bytes 1000000 | tf_op jit(solution)/shard_map/pallas_call | solution.py:586
  52.6 0.8 %all-to-all-done.1.whole = bf16[32,24,128]{2,1,0:T(8,128)(2,1)S(1)} async-done(((bf16[32,24,128]{2,1,0:T(8,128)(2,1)}), bf16[32,24,128]{2,1,0:T(8,128)(2,1)S(1)}, u32[]{:S(2)}, u32[]{:S(2)}) %all-to-all-start.1) | async-done | bytes 196640 | tf_op jit(solution)/shard_map/all_to_all | solution.py:572
  53.3 0.9 %shard_map.137 = (f32[25,25,64]{2,1,0:T(8,128)}, f32[25,25,64]{2,1,0:T(8,128)}) custom-call(bf16[32,24,128]{2,1,0:T(8,128)(2,1)S(1)} %all-to-all-done.1.whole), custom_call_target="tpu_custom_call" | custom-call | flops 100000000 | bytes 1000000 | tf_op jit(solution)/shard_map/pallas_call | solution.py:582
Async XLA Ops:
  2.4 8.0 %collective-permute-start.3 = (bf16[32,1024]{1,0:T(8,128)(2,1)S(1)}, bf16[32,1024]{1,0:T(8,128)(2,1)S(1)}, u32[]{:S(2)}, u32[]{:S(2)}) collective-permute-start(bf16[32,1024]{1,0:T(8,128)(2,1)S(1)} %get-tuple-element.46.own), channel_id=1, source_target_pairs={{0,2},{1,3},{2,0},{3,1},{4,6},{5,7},{6,4},{7,5},{8,10},{9,11},{10,... | collective-permute-start | bytes 196616 | tf_op jit(solution)/shard_map/ppermute | solution.py:444
  5.4 10.2 %collective-permute-start = (bf16[400,128]{1,0:T(8,128)(2,1)S(1)}, bf16[400,128]{1,0:T(8,128)(2,1)S(1)}, u32[]{:S(2)}, u32[]{:S(2)}) collective-permute-start(bf16[400,128]{1,0:T(8,128)(2,1)S(1)} %get-tuple-element.36), channel_id=1, source_target_pairs={{4,8},{12,16},{20,24},{8,4},{16,12},{24,20},{5,9},{13,17},{21,25},... | collective-permute-start | bytes 307208 | tf_op jit(solution)/shard_map/ppermute | solution.py:496
  6.1 9.5 %collective-permute-start.1 = (bf16[400,128]{1,0:T(8,128)(2,1)S(1)}, bf16[400,128]{1,0:T(8,128)(2,1)S(1)}, u32[]{:S(2)}, u32[]{:S(2)}) collective-permute-start(bf16[400,128]{1,0:T(8,128)(2,1)S(1)} %get-tuple-element.37), channel_id=1, source_target_pairs={{0,4},{8,12},{16,20},{24,28},{4,0},{12,8},{20,16},{28,24},{1,5},{9... | collective-permute-start | bytes 307208 | tf_op jit(solution)/shard_map/ppermute | solution.py:497
  10.4 3.3 %collective-permute-start.2 = (bf16[32,1024]{1,0:T(8,128)(2,1)S(1)}, bf16[32,1024]{1,0:T(8,128)(2,1)S(1)}, u32[]{:S(2)}, u32[]{:S(2)}) collective-permute-start(bf16[32,1024]{1,0:T(8,128)(2,1)S(1)} %get-tuple-element.46.own), channel_id=1, source_target_pairs={{0,1},{1,0},{2,3},{3,2},{4,5},{5,4},{6,7},{7,6},{8,9},{9,8},{10,11... | collective-permute-start | bytes 196616 | tf_op jit(solution)/shard_map/ppermute | solution.py:444
  10.4 3.3 %collective-permute-start.4 = (bf16[32,1024]{1,0:T(8,128)(2,1)S(1)}, bf16[32,1024]{1,0:T(8,128)(2,1)S(1)}, u32[]{:S(2)}, u32[]{:S(2)}) collective-permute-start(bf16[32,1024]{1,0:T(8,128)(2,1)S(1)} %collective-permute-done.3.cross), channel_id=1, source_target_pairs={{0,1},{1,0},{2,3},{3,2},{4,5},{5,4},{6,7},{7,6},{8,9},{9,8},{10,11... | collective-permute-start | bytes 196616 | tf_op jit(solution)/shard_map/ppermute | solution.py:444
  28.1 12.7 %all-to-all-start = ((bf16[32,24,128]{2,1,0:T(8,128)(2,1)}), bf16[32,24,128]{2,1,0:T(8,128)(2,1)S(1)}, u32[]{:S(2)}, u32[]{:S(2)}) async-start(bf16[32,24,128]{2,1,0:T(8,128)(2,1)} %get-tuple-element.63), calls=%async_computation | async-start | bytes 393216 | tf_op jit(solution)/shard_map/all_to_all | solution.py:565
  41.7 11.6 %all-to-all-start.1 = ((bf16[32,24,128]{2,1,0:T(8,128)(2,1)}), bf16[32,24,128]{2,1,0:T(8,128)(2,1)S(1)}, u32[]{:S(2)}, u32[]{:S(2)}) async-start(bf16[32,24,128]{2,1,0:T(8,128)(2,1)} %shard_map.136), calls=%async_computation.1 | async-start | bytes 393216 | tf_op jit(solution)/shard_map/all_to_all | solution.py:572

commit v7 on v6

--- a/solution.py
+++ b/solution.py
@@ -278,9 +278,9 @@
 
     def picks(source, ref, group, held, last, chunk):
         count = source.shape[0] // kcount
-        for pair in range(GROUP // 2):
-            at = 2 * pair
-            both = jnp.concatenate([chosen(ref, group, at), chosen(ref, group, at + 1)], axis=1)
+        wide_by = 4 if count * KM < 128 else 2
+        for first in range(0, GROUP, wide_by):
+            both = jnp.concatenate([chosen(ref, group, first + i) for i in range(wide_by)], axis=1)
             for begin in range(0, count, chunk):
                 end = begin + chunk
                 end_row = end * KM if end < count else source.shape[0]
@@ -288,13 +288,15 @@
                 for c in range(chunk):
                     rows = picked[c * KM : (c + 1) * KM]
                     lane = (begin + c) * 128
-                    held[at * KM : (at + 2) * KM, lane : lane + 128] = jnp.concatenate(
-                        [rows[:, 0:128], rows[:, 128:]], axis=0
-                    ).astype(bf16)
+                    for i in range(0, wide_by, 2):
+                        at = first + i
+                        held[at * KM : (at + 2) * KM, lane : lane + 128] = jnp.concatenate(
+                            [rows[:, i * 128 : (i + 1) * 128], rows[:, (i + 1) * 128 : (i + 2) * 128]], axis=0
+                        ).astype(bf16)
             rows = picked[chunk * KM :]
-            for i in range(2):
+            for i in range(wide_by):
                 for c in range(count):
-                    last[at + i : at + i + 1, c * 128 : (c + 1) * 128] = rows[c : c + 1, i * 128 : (i + 1) * 128]
+                    last[first + i : first + i + 1, c * 128 : (c + 1) * 128] = rows[c : c + 1, i * 128 : (i + 1) * 128]
         held[GROUP * KM :, :] = last[...].astype(bf16)
 
     def pick_leaves(group, held, last):
@@ -404,17 +406,27 @@
         out[d] = laid[0 : summed.shape[0], :].astype(bf16)
 
 
-def unpack_kernel(whole, leaf_out, coarse_out, flat):
-    kcount, jcount, slots = leaf_out.shape
+def unpack_kernel(whole, leaf_out, coarse_out, leaf, coarse, flat, sems):
+    kcount, jcount, slots = leaf.shape
     if len(whole.shape) == 2:
         flat[...] = whole[...].astype(f32)
     else:
         for d in range(whole.shape[0]):
             flat[d * whole.shape[1] : (d + 1) * whole.shape[1], :] = whole[d].astype(f32)
+
+    def row_of(k):
+        return flat[pl.ds(k // FOUR * FOUR * jcount + k % FOUR, jcount, stride=FOUR), :]
+
     for k in range(kcount):
-        row = flat[pl.ds(k // FOUR * FOUR * jcount + k % FOUR, jcount, stride=FOUR), :]
-        leaf_out[k] = row[:, 0:slots]
-        coarse_out[k] = pltpu.roll(row, slots, 1)[:, 0:slots]
+        leaf[k] = row_of(k)[:, 0:slots]
+    first = pltpu.make_async_copy(leaf, leaf_out, sems.at[0])
+    first.start()
+    for k in range(kcount):
+        coarse[k] = pltpu.roll(row_of(k), slots, 1)[:, 0:slots]
+    second = pltpu.make_async_copy(coarse, coarse_out, sems.at[1])
+    second.start()
+    first.wait()
+    second.wait()
 
 
 def mixing_kernel(whole, mix, charges, out, mixed):
@@ -580,7 +592,15 @@
         whole = jnp.transpose(whole, (0, 3, 4, 1, 2, 5)).reshape(flat_rows, 128)
     grad_shape = shape((kcount, kcount, slots), f32)
     grad_leaf, grad_coarse = call(
-        unpack_kernel, (grad_shape, grad_shape), [pltpu.VMEM((flat_rows, 128), f32)]
+        unpack_kernel,
+        (grad_shape, grad_shape),
+        [
+            pltpu.VMEM(grad_shape.shape, f32),
+            pltpu.VMEM(grad_shape.shape, f32),
+            pltpu.VMEM((flat_rows, 128), f32),
+            pltpu.SemaphoreType.DMA((2,)),
+        ],
+        out_specs=[far_off, far_off],
     )(whole)
 
     refined = call(

time: 54.7 us -> 54.8 us (level)
  no operation moved by 1% of the time
where the time goes in v7:
time: 54.8 us; the launch traced here: 54.4 us
  Pallas kernels  24.2 us (44%)
  starting transfers between devices  15.2 us (28%)
  blocking collectives  7.21 us (13%)
  waiting for transfers between devices  6.87 us (13%)
  between operations  0.88 us (2%)
    pallas_call x1, Pallas kernels, local(): call(functools.partial(grads_kernel, kcount=kcount), (shape((KP, wide), f...  12.5 us
    all_gather x1, blocking collectives, local(): lax.all_gather(potential, 'chan', axis=0, tiled=True)  7.21 us
    all_to_all x1, waiting for transfers between devices, local(): parts = lax.all_to_all(grads, axes, 0, 0)  6.08 us
    ppermute x1, starting transfers between devices, local(): second = lax.ppermute(second, 'cells', outer + [(b, a) for a, b in outer])  4.34 us
    all_to_all x1, starting transfers between devices, local(): parts = lax.all_to_all(grads, axes, 0, 0)  3.96 us
    ppermute x3, starting transfers between devices, swap(): return lax.ppermute(part, 'chan', [(i, i ^ d) for i in range(count)])  3.54 us
    pallas_call x1, Pallas kernels, local(): call(prepare_kernel, (shape((coarse_rows, 128), bf16), wide_ops, wide_ops...  2.74 us
    all_to_all x1, starting transfers between devices, local(): whole = lax.all_to_all(spread_out, axes, 0, 0)  2.71 us
  transfers between devices with their start and end apart: 7, of which 2 were waited for; matrix products, arithmetic and copies ran while one was open for 0% of the time, Pallas kernels for 15%

profile of v7, /device:TPU:0, one launch (start us, length us, event | category | flops | bytes accessed | tf_op | source)
XLA Modules:
  0.0 54.4 jit_solution(1906352158115295314)
XLA Ops:
  0.6 1.8 %shard_map.130 = (bf16[800,128]{1,0:T(8,128)(2,1)S(1)}, bf16[400,128]{1,0:T(8,128)(2,1)S(1)}, bf16[400,128]{1,0:T(8,128)(2,1)S(1)}, f32[32,1024]{1,0:T(8,128)S(1...) custom-call(bf16[32,1024]{1,0:T(8,128)(2,1)} %charges_hbm.1, ...), custom_call_target="tpu_custom_call" | custom-call | flops 100000000 | bytes 1000000 | tf_op jit(solution)/shard_map/pallas_call | solution.py:491
  2.4 3.0 %collective-permute-start.3 = (bf16[32,1024]{1,0:T(8,128)(2,1)S(1)}, bf16[32,1024]{1,0:T(8,128)(2,1)S(1)}, u32[]{:S(2)}, u32[]{:S(2)}) collective-permute-start(bf16[32,1024]{1,0:T(8,128)(2,1)S(1)} %get-tuple-element.46.own), channel_id=1, source_target_pairs={{0,2},{1,3},{2,0},{3,1},{4,6},{5,7},{6,4},{7,5},{8,10},{9,11},{10,... | collective-permute-start | bytes 196616 | tf_op jit(solution)/shard_map/ppermute | solution.py:456
  5.4 0.7 %collective-permute-start = (bf16[400,128]{1,0:T(8,128)(2,1)S(1)}, bf16[400,128]{1,0:T(8,128)(2,1)S(1)}, u32[]{:S(2)}, u32[]{:S(2)}) collective-permute-start(bf16[400,128]{1,0:T(8,128)(2,1)S(1)} %get-tuple-element.36), channel_id=1, source_target_pairs={{4,8},{12,16},{20,24},{8,4},{16,12},{24,20},{5,9},{13,17},{21,25},... | collective-permute-start | bytes 307208 | tf_op jit(solution)/shard_map/ppermute | solution.py:508
  6.1 4.3 %collective-permute-start.1 = (bf16[400,128]{1,0:T(8,128)(2,1)S(1)}, bf16[400,128]{1,0:T(8,128)(2,1)S(1)}, u32[]{:S(2)}, u32[]{:S(2)}) collective-permute-start(bf16[400,128]{1,0:T(8,128)(2,1)S(1)} %get-tuple-element.37), channel_id=1, source_target_pairs={{0,4},{8,12},{16,20},{24,28},{4,0},{12,8},{20,16},{28,24},{1,5},{9... | collective-permute-start | bytes 307208 | tf_op jit(solution)/shard_map/ppermute | solution.py:509
  10.4 0.0 collective-permute-start.2
  10.4 0.0 collective-permute-done.3.cross
  10.4 0.5 collective-permute-start.4
  10.9 2.7 %shard_map.131 = (bf16[100,128]{1,0:T(8,128)(2,1)S(1)}, bf16[32,256]{1,0:T(8,128)(2,1)S(1)}, bf16[32,256]{1,0:T(8,128)(2,1)S(1)}, bf16[32,256]{1,0:T(8,128)(2,1)...) custom-call(bf16[25,8,25]{2,1,0:T(8,128)(2,1)S(1)} %get-tuple-elemen, ...), custom_call_target="tpu_custom_call" | custom-call | flops 100000000 | bytes 1000000 | tf_op jit(solution)/shard_map/pallas_call | solution.py:515
  13.7 0.0 collective-permute-done.2.core
  13.7 0.0 collective-permute-done.4.other
  13.7 1.9 %shard_map.132 = (bf16[32,4096]{1,0:T(8,128)(2,1)S(1)}, bf16[32,512]{1,0:T(8,128)(2,1)S(1)}) custom-call(bf16[32,1024]{1,0:T(8,128)(2,1)S(1)} %get-tuple-element.46.own, bf16[32,1024]{1,0:T(8,128)(2,1)S(1)} %collective-permute-done.2.core, bf16[32,1024]{1,0:T(8,128)(2,1)S(1)} %collective-permute-done.3.cross, ...), custom_call_target="tpu_custom_call" | custom-call | flops 100000000 | bytes 1000000 | tf_op jit(solution)/shard_map/pallas_call | solution.py:536
  15.6 0.0 collective-permute-done.first
  15.6 0.0 collective-permute-done.1.second
  15.6 12.5 %shard_map.133 = (f32[32,4096]{1,0:T(8,128)S(1)}, f32[32,512]{1,0:T(8,128)S(1)}, bf16[32,24,128]{2,1,0:T(8,128)(2,1)}) custom-call(bf16[800,128]{1,0:T(8,128)(2,1)S(1)} %get-tuple-element.35.m, bf16[400,128]{1,0:T(8,128)(2,1)S(1)} %collective-permute-done.first, bf16[400,128]{1,0:T(8,128)(2,1)S(1)} %collective-permute-done.1.second, ...), custom_call_target="tpu_custom_call" | custom-call | flops 100000000 | bytes 1000000 | tf_op jit(solution)/shard_map/pallas_call | solution.py:549
  28.1 4.0 %all-to-all-start = ((bf16[32,24,128]{2,1,0:T(8,128)(2,1)}), bf16[32,24,128]{2,1,0:T(8,128)(2,1)S(1)}, u32[]{:S(2)}, u32[]{:S(2)}) async-start(bf16[32,24,128]{2,1,0:T(8,128)(2,1)} %get-tuple-element.63), calls=%async_computation | async-start | bytes 393216 | tf_op jit(solution)/shard_map/all_to_all | solution.py:577
  32.1 2.6 %shard_map.134 = (bf16[32,1024]{1,0:T(8,128)(2,1)S(1)}, bf16[512,512]{1,0:T(8,128)(2,1)S(1)}) custom-call(f32[32,4096]{1,0:T(8,128)S(1)} %get-tuple-element.58.near, f32[32,512]{1,0:T(8,128)S(1)} %get-tuple-element.59.far, bf16[32,256]{1,0:T(8,128)(2,1)S(1)} %get-tuple-element.60.down, f32[32,1024]{1,0:T(8,128)S(1)} %get-tuple-element.48.base, ...), custom_call_target="tpu_custom_call" | custom-call | flops 100000000 | bytes 1000000 | tf_op jit(solution)/shard_map/pallas_call | solution.py:569
  34.7 6.1 %all-to-all-done.parts = bf16[32,24,128]{2,1,0:T(8,128)(2,1)S(1)} async-done(((bf16[32,24,128]{2,1,0:T(8,128)(2,1)}), bf16[32,24,128]{2,1,0:T(8,128)(2,1)S(1)}, u32[]{:S(2)}, u32[]{:S(2)}) %all-to-all-start) | async-done | bytes 196640 | tf_op jit(solution)/shard_map/all_to_all | solution.py:577
  40.8 0.9 %shard_map.136 = bf16[32,24,128]{2,1,0:T(8,128)(2,1)} custom-call(bf16[32,24,128]{2,1,0:T(8,128)(2,1)S(1)} %all-to-all-done.parts, bf16[32,1024]{1,0:T(8,128)(2,1)S(1)} %get-tuple-element.61.after, bf16[512,512]{1,0:T(8,128)(2,1)S(1)} %get-tuple-element.64.order), custom_call_target="tpu_custom_call" | custom-call | flops 100000000 | bytes 1000000 | tf_op jit(solution)/shard_map/pallas_call | solution.py:578
  41.7 2.7 %all-to-all-start.1 = ((bf16[32,24,128]{2,1,0:T(8,128)(2,1)}), bf16[32,24,128]{2,1,0:T(8,128)(2,1)S(1)}, u32[]{:S(2)}, u32[]{:S(2)}) async-start(bf16[32,24,128]{2,1,0:T(8,128)(2,1)} %shard_map.136), calls=%async_computation.1 | async-start | bytes 393216 | tf_op jit(solution)/shard_map/all_to_all | solution.py:584
  44.4 7.2 %all_gather.3.whole = bf16[128,1024]{1,0:T(8,128)(2,1)S(1)} all-gather(bf16[32,1024]{1,0:T(8,128)(2,1)S(1)} %get-tuple-element.61.after), channel_id=1, replica_groups=mesh['cells'=8,'chan'=4] {'chan'}, dimensions={0}, use_global_device_ids=true | all-gather | bytes 327680 | tf_op jit(solution)/shard_map/all_gather | solution.py:610
  51.7 0.9 %shard_map.135 = bf16[32,1024]{1,0:T(8,128)(2,1)} custom-call(bf16[128,1024]{1,0:T(8,128)(2,1)S(1)} %all_gather.3.whole, bf16[128,128]{1,0:T(8,128)(2,1)S(1)} %get-tuple-element.47.mix, bf16[32,1024]{1,0:T(8,128)(2,1)S(1)} %get-tuple-element.62.charges), custom_call_target="tpu_custom_call" | custom-call | flops 100000000 | bytes 1000000 | tf_op jit(solution)/shard_map/pallas_call | solution.py:606
  52.6 0.8 %all-to-all-done.1.whole = bf16[32,24,128]{2,1,0:T(8,128)(2,1)S(1)} async-done(((bf16[32,24,128]{2,1,0:T(8,128)(2,1)}), bf16[32,24,128]{2,1,0:T(8,128)(2,1)S(1)}, u32[]{:S(2)}, u32[]{:S(2)}) %all-to-all-start.1) | async-done | bytes 196640 | tf_op jit(solution)/shard_map/all_to_all | solution.py:584
  53.3 0.9 %shard_map.137 = (f32[25,25,64]{2,1,0:T(8,128)}, f32[25,25,64]{2,1,0:T(8,128)}) custom-call(bf16[32,24,128]{2,1,0:T(8,128)(2,1)S(1)} %all-to-all-done.1.whole), custom_call_target="tpu_custom_call" | custom-call | flops 100000000 | bytes 1000000 | tf_op jit(solution)/shard_map/pallas_call | solution.py:594
Async XLA Ops:
  2.4 8.0 %collective-permute-start.3 = (bf16[32,1024]{1,0:T(8,128)(2,1)S(1)}, bf16[32,1024]{1,0:T(8,128)(2,1)S(1)}, u32[]{:S(2)}, u32[]{:S(2)}) collective-permute-start(bf16[32,1024]{1,0:T(8,128)(2,1)S(1)} %get-tuple-element.46.own), channel_id=1, source_target_pairs={{0,2},{1,3},{2,0},{3,1},{4,6},{5,7},{6,4},{7,5},{8,10},{9,11},{10,... | collective-permute-start | bytes 196616 | tf_op jit(solution)/shard_map/ppermute | solution.py:456
  5.4 10.2 %collective-permute-start = (bf16[400,128]{1,0:T(8,128)(2,1)S(1)}, bf16[400,128]{1,0:T(8,128)(2,1)S(1)}, u32[]{:S(2)}, u32[]{:S(2)}) collective-permute-start(bf16[400,128]{1,0:T(8,128)(2,1)S(1)} %get-tuple-element.36), channel_id=1, source_target_pairs={{4,8},{12,16},{20,24},{8,4},{16,12},{24,20},{5,9},{13,17},{21,25},... | collective-permute-start | bytes 307208 | tf_op jit(solution)/shard_map/ppermute | solution.py:508
  6.1 9.5 %collective-permute-start.1 = (bf16[400,128]{1,0:T(8,128)(2,1)S(1)}, bf16[400,128]{1,0:T(8,128)(2,1)S(1)}, u32[]{:S(2)}, u32[]{:S(2)}) collective-permute-start(bf16[400,128]{1,0:T(8,128)(2,1)S(1)} %get-tuple-element.37), channel_id=1, source_target_pairs={{0,4},{8,12},{16,20},{24,28},{4,0},{12,8},{20,16},{28,24},{1,5},{9... | collective-permute-start | bytes 307208 | tf_op jit(solution)/shard_map/ppermute | solution.py:509
  10.4 3.3 %collective-permute-start.2 = (bf16[32,1024]{1,0:T(8,128)(2,1)S(1)}, bf16[32,1024]{1,0:T(8,128)(2,1)S(1)}, u32[]{:S(2)}, u32[]{:S(2)}) collective-permute-start(bf16[32,1024]{1,0:T(8,128)(2,1)S(1)} %get-tuple-element.46.own), channel_id=1, source_target_pairs={{0,1},{1,0},{2,3},{3,2},{4,5},{5,4},{6,7},{7,6},{8,9},{9,8},{10,11... | collective-permute-start | bytes 196616 | tf_op jit(solution)/shard_map/ppermute | solution.py:456
  10.4 3.3 %collective-permute-start.4 = (bf16[32,1024]{1,0:T(8,128)(2,1)S(1)}, bf16[32,1024]{1,0:T(8,128)(2,1)S(1)}, u32[]{:S(2)}, u32[]{:S(2)}) collective-permute-start(bf16[32,1024]{1,0:T(8,128)(2,1)S(1)} %collective-permute-done.3.cross), channel_id=1, source_target_pairs={{0,1},{1,0},{2,3},{3,2},{4,5},{5,4},{6,7},{7,6},{8,9},{9,8},{10,11... | collective-permute-start | bytes 196616 | tf_op jit(solution)/shard_map/ppermute | solution.py:456
  28.1 12.7 %all-to-all-start = ((bf16[32,24,128]{2,1,0:T(8,128)(2,1)}), bf16[32,24,128]{2,1,0:T(8,128)(2,1)S(1)}, u32[]{:S(2)}, u32[]{:S(2)}) async-start(bf16[32,24,128]{2,1,0:T(8,128)(2,1)} %get-tuple-element.63), calls=%async_computation | async-start | bytes 393216 | tf_op jit(solution)/shard_map/all_to_all | solution.py:577
  41.7 11.6 %all-to-all-start.1 = ((bf16[32,24,128]{2,1,0:T(8,128)(2,1)}), bf16[32,24,128]{2,1,0:T(8,128)(2,1)S(1)}, u32[]{:S(2)}, u32[]{:S(2)}) async-start(bf16[32,24,128]{2,1,0:T(8,128)(2,1)} %shard_map.136), calls=%async_computation.1 | async-start | bytes 393216 | tf_op jit(solution)/shard_map/all_to_all | solution.py:584
